TPU v7x, 32 devices: a whole 2x2x4 slice. The times are simulated.
32 devices in a mesh: batch: 4 (over y, x), blk: 8 (over z, core).
Axes of the slice: x: 2, y: 2, z: 4, core: 2. Of those that a mesh axis runs over, the one named last changes fastest.
Arguments:
- clean_latents: float32 [4, 4096, 16], P('batch', 'blk'), may hold values from -6 to 6
- noise_sample: float32 [4, 4096, 16], P('batch', 'blk'), may hold values from -6 to 6
- noise_levels: int32 [4, 16], replicated, may hold values from 0 to 31
- clean_flags: int32 [4, 16], replicated, may hold values 0 or 1
- span_frame: int32 [16], replicated, may hold values from 0 to 15, as said below
- patch_master: float32 [16, 1024], P(None, ('batch', 'blk')), may hold values from -1.5 to 1.5
- patch_first: float32 [16, 1024], P(None, ('batch', 'blk')), may hold values from -7.6293945e-06 to 7.6293945e-06
- patch_second: float32 [16, 1024], P(None, ('batch', 'blk')), may hold values from 2.111829e-14 to 8.447316e-14
- level_master: float32 [33, 1024], P(None, ('batch', 'blk')), may hold values from -5 to 5
- level_first: float32 [33, 1024], P(None, ('batch', 'blk')), may hold values from -7.6293945e-06 to 7.6293945e-06
- level_second: float32 [33, 1024], P(None, ('batch', 'blk')), may hold values from 2.111829e-14 to 8.447316e-14
- adaptive_master: float32 [1024, 6144], P(('batch', 'blk')), may hold values from -0.1875 to 0.1875
- adaptive_first: float32 [1024, 6144], P(('batch', 'blk')), may hold values from -7.6293945e-06 to 7.6293945e-06
- adaptive_second: float32 [1024, 6144], P(('batch', 'blk')), may hold values from 2.111829e-14 to 8.447316e-14
- triple_master: float32 [1024, 3072], P(('batch', 'blk')), may hold values from -0.1875 to 0.1875
- triple_first: float32 [1024, 3072], P(('batch', 'blk')), may hold values from -7.6293945e-06 to 7.6293945e-06
- triple_second: float32 [1024, 3072], P(('batch', 'blk')), may hold values from 2.111829e-14 to 8.447316e-14
- project_master: float32 [1024, 1024], P(('batch', 'blk')), may hold values from -1.5 to 1.5
- project_first: float32 [1024, 1024], P(('batch', 'blk')), may hold values from -7.6293945e-06 to 7.6293945e-06
- project_second: float32 [1024, 1024], P(('batch', 'blk')), may hold values from 2.111829e-14 to 8.447316e-14
- expand_master: float32 [1024, 4096], P(('batch', 'blk')), may hold values from -0.1875 to 0.1875
- expand_first: float32 [1024, 4096], P(('batch', 'blk')), may hold values from -7.6293945e-06 to 7.6293945e-06
- expand_second: float32 [1024, 4096], P(('batch', 'blk')), may hold values from 2.111829e-14 to 8.447316e-14
- reduce_master: float32 [4096, 1024], P(('batch', 'blk')), may hold values from -0.09375 to 0.09375
- reduce_first: float32 [4096, 1024], P(('batch', 'blk')), may hold values from -7.6293945e-06 to 7.6293945e-06
- reduce_second: float32 [4096, 1024], P(('batch', 'blk')), may hold values from 2.111829e-14 to 8.447316e-14
- readout_master: float32 [1024, 16], P(('batch', 'blk')), may hold values from -0.1875 to 0.1875
- readout_first: float32 [1024, 16], P(('batch', 'blk')), may hold values from -7.6293945e-06 to 7.6293945e-06
- readout_second: float32 [1024, 16], P(('batch', 'blk')), may hold values from 2.111829e-14 to 8.447316e-14
Outputs:
- loss_sum: float32 [], replicated
- frame_count: float32 [], replicated
- bucket_sums: float32 [32], replicated
- clip_norm: float32 [], replicated
- patch_first_next: float32 [16, 1024], P(None, ('batch', 'blk'))
- patch_second_next: float32 [16, 1024], P(None, ('batch', 'blk'))
- patch_master_next: float32 [16, 1024], P(None, ('batch', 'blk'))
- level_first_next: float32 [33, 1024], P(None, ('batch', 'blk'))
- level_second_next: float32 [33, 1024], P(None, ('batch', 'blk'))
- level_master_next: float32 [33, 1024], P(None, ('batch', 'blk'))
- adaptive_first_next: float32 [1024, 6144], P(('batch', 'blk'))
- adaptive_second_next: float32 [1024, 6144], P(('batch', 'blk'))
- adaptive_master_next: float32 [1024, 6144], P(('batch', 'blk'))
- triple_first_next: float32 [1024, 3072], P(('batch', 'blk'))
- triple_second_next: float32 [1024, 3072], P(('batch', 'blk'))
- triple_master_next: float32 [1024, 3072], P(('batch', 'blk'))
- project_first_next: float32 [1024, 1024], P(('batch', 'blk'))
- project_second_next: float32 [1024, 1024], P(('batch', 'blk'))
- project_master_next: float32 [1024, 1024], P(('batch', 'blk'))
- expand_first_next: float32 [1024, 4096], P(('batch', 'blk'))
- expand_second_next: float32 [1024, 4096], P(('batch', 'blk'))
- expand_master_next: float32 [1024, 4096], P(('batch', 'blk'))
- reduce_first_next: float32 [4096, 1024], P(('batch', 'blk'))
- reduce_second_next: float32 [4096, 1024], P(('batch', 'blk'))
- reduce_master_next: float32 [4096, 1024], P(('batch', 'blk'))
- readout_first_next: float32 [1024, 16], P(('batch', 'blk'))
- readout_second_next: float32 [1024, 16], P(('batch', 'blk'))
- readout_master_next: float32 [1024, 16], P(('batch', 'blk'))
Inputs may be any that keep to these rules, and one draw needn't show every extreme that they name: `span_frame`: each of the 16 time indices appears once; the stored frames form groups of 2 in a row, and group i holds, one in each half of it, the time indices i * 1 to (i + 1) * 1 - 1 and their mirror images 16 - 1 - t.
All inputs are finite; a program needn't handle non-finite values.
Results may differ from a plain program's by a relative error of at most 0.008.
The roundings to bfloat16 on the way count: a program that leaves them out, or rounds other values in their place, can miss the bound.
Values may be sent and summed in bfloat16 or wider, within the bound.
No kernel may reach another device: no remote copies, remote signals or barrier semaphores. Data moves between devices by JAX's collectives and lax.ppermute only.
A program may use at most 256 MiB of HBM per device.

v0:
```python
import math

import jax
import jax.numpy as jnp
from jax import lax
from jax.sharding import PartitionSpec as P

D = 1024
HEADS = 16
HEAD_DIM = 64
PATCH_FEAT = 16
FRAME_TOK = 256
SIDE = 16
NB = 32
STEP = 10


learn_rates = (0.5, 2.0, 0.05, 0.05, 0.5, 0.05, 0.05, 0.05)
beta_first = 0.9
beta_second = 0.999
decay_rate = 0.01
adam_floor = 1e-08
clip_bound = 0.02


def from_behind(x, axis, by):
    devices = lax.axis_size(axis)
    return lax.ppermute(x, axis, [(i, (i + by) % devices) for i in range(devices)])


def product(left, right):
    return jnp.dot(left, right, preferred_element_type=jnp.float32)


def across(left, right):
    return lax.dot_general(
        left, right, (((0,), (0,)), ((), ())), preferred_element_type=jnp.float32
    )


def against(left, right):
    return lax.dot_general(
        left, right, (((1,), (1,)), ((), ())), preferred_element_type=jnp.float32
    )


def plan(levels, clean_flags):
    alpha_bar = jnp.cos(0.5 * math.pi * (levels.astype(jnp.float32) + 1.0) / (NB + 1.0)) ** 2
    noised = (1 - clean_flags).astype(jnp.float32)
    table_index = jnp.where(clean_flags == 1, 0, levels + 1)
    return (alpha_bar, noised, table_index)


def noised_input(clean_tok, noise_tok, alpha_bar, noised):
    frame_shape = (alpha_bar.shape[0], -1, clean_tok.shape[-1])
    clean_frames = clean_tok.reshape(frame_shape)
    noise_frames = noise_tok.reshape(frame_shape)
    mixed_tok = (
        jnp.sqrt(alpha_bar)[:, None, None] * clean_frames
        + jnp.sqrt(1.0 - alpha_bar)[:, None, None] * noise_frames
    )
    return jnp.where(noised[:, None, None] > 0.5, mixed_tok, clean_frames).reshape(clean_tok.shape)


def rotary(frame_ids, token_count):
    in_frame = jnp.arange(token_count, dtype=jnp.int32) % FRAME_TOK
    row_pos = (in_frame // SIDE).astype(jnp.float32)
    col_pos = (in_frame % SIDE).astype(jnp.float32)
    frame_pos = jnp.repeat(frame_ids, FRAME_TOK, total_repeat_length=token_count).astype(
        jnp.float32
    )
    time_count = HEAD_DIM // 8
    space_count = 3 * HEAD_DIM // 16
    time_freq = 10000.0 ** (-jnp.arange(time_count, dtype=jnp.float32) / time_count)
    space_freq = 100.0 ** (-jnp.arange(space_count, dtype=jnp.float32) / space_count)
    angles = jnp.concatenate(
        [
            frame_pos[:, None] * time_freq,
            row_pos[:, None] * space_freq,
            col_pos[:, None] * space_freq,
        ],
        axis=1,
    )
    return (jnp.cos(angles), jnp.sin(angles))


def rotate(values, cosine_table, sine_table):
    half_dim = values.shape[-1] // 2
    first_half, second_half = (values[..., :half_dim], values[..., half_dim:])
    cosine_part, sine_part = (cosine_table[:, None, :], sine_table[:, None, :])
    return jnp.concatenate(
        [
            first_half * cosine_part - second_half * sine_part,
            second_half * cosine_part + first_half * sine_part,
        ],
        axis=-1,
    )


def layer_norm(hidden):
    centred = hidden - jnp.mean(hidden, axis=-1, keepdims=True)
    variance = jnp.mean(centred * centred, axis=-1, keepdims=True)
    return centred * lax.rsqrt(variance + 1e-06)


def modulate(hidden, shift, scale):
    normed = layer_norm(hidden).reshape(shift.shape[0], -1, hidden.shape[-1])
    return (normed * (1.0 + scale[:, None]) + shift[:, None]).reshape(hidden.shape)


def per_frame(gate, hidden):
    return (hidden.reshape(gate.shape[0], -1, hidden.shape[-1]) * gate[:, None]).reshape(
        hidden.shape
    )


def frame_sum(gate, hidden):
    return jnp.sum(hidden.reshape(gate.shape[0], -1, hidden.shape[-1]), axis=1)


def gelu_tanh(value):
    return jax.nn.gelu(value, approximate=True)


def adamw_update(master, first_moment, second_moment, gradient, factor, step_rate):
    clipped = gradient * factor
    first_new = beta_first * first_moment + (1.0 - beta_first) * clipped
    second_new = beta_second * second_moment + (1.0 - beta_second) * clipped * clipped
    first_hat = first_new / (1.0 - beta_first**STEP)
    second_hat = second_new / (1.0 - beta_second**STEP)
    master_new = master - step_rate * (
        first_hat / (jnp.sqrt(second_hat) + adam_floor) + decay_rate * master
    )
    return (first_new, second_new, master_new)


def forward_block(running, queries, key_part, value_part, query_frame, key_frame):
    row_max, row_total, weighted = running
    scores = jnp.einsum(
        "qhd,khd->hqk", queries, key_part, preferred_element_type=jnp.float32
    ) * HEAD_DIM ** (-0.5)
    allowed = query_frame[None, :, None] >= key_frame[None, None, :]
    scores = jnp.where(allowed, scores, -1e30)
    new_max = jnp.maximum(row_max, jnp.max(scores, axis=-1))
    rescale = jnp.exp(row_max - new_max)
    exponent = jnp.exp(scores - new_max[..., None])
    row_total = row_total * rescale + jnp.sum(exponent, axis=-1)
    weighted = weighted * rescale[..., None] + jnp.einsum(
        "hqk,khd->hqd",
        exponent.astype(jnp.bfloat16),
        value_part,
        preferred_element_type=jnp.float32,
    )
    return (new_max, row_total, weighted)


def visit(running, queries, key_part, value_part, query_frame, key_frame):
    return forward_block(running, queries, key_part, value_part, query_frame, key_frame)


def attend_forward(queries, key_block, values, query_frame, token_frame, chain_index):
    row_count = queries.shape[0]
    head_count = queries.shape[1]
    initial = (
        jnp.full((head_count, row_count), -1e30, jnp.float32),
        jnp.zeros((head_count, row_count), jnp.float32),
        jnp.zeros((head_count, row_count, queries.shape[2]), jnp.float32),
    )
    chain_count = lax.axis_size("blk")
    own_frame = lax.dynamic_slice_in_dim(token_frame, chain_index * row_count, row_count)
    running = visit(initial, queries, key_block, values, query_frame, own_frame)

    def hop_turn(hop_index, carried):
        running_now, keys_now, values_now = carried
        keys_now, values_now = from_behind((keys_now, values_now), "blk", 1)
        source_dev = (chain_index - hop_index) % chain_count
        key_frame = lax.dynamic_slice_in_dim(token_frame, source_dev * row_count, row_count)
        return (
            visit(running_now, queries, keys_now, values_now, query_frame, key_frame),
            keys_now,
            values_now,
        )

    running, _, _ = lax.fori_loop(1, chain_count, hop_turn, (running, key_block, values))
    row_max, row_total, weighted = running
    attended = jnp.transpose(weighted / row_total[..., None], (1, 0, 2))
    return (attended, row_max + jnp.log(row_total))


def backward_block(
    queries, key_part, value_part, grad_out, row_dot, log_total, query_frame, key_frame
):
    scale = HEAD_DIM ** (-0.5)
    scores = (
        jnp.einsum("qhd,khd->hqk", queries, key_part, preferred_element_type=jnp.float32) * scale
    )
    allowed = query_frame[None, :, None] >= key_frame[None, None, :]
    chances = jnp.where(allowed, jnp.exp(scores - log_total[..., None]), 0.0)
    grad_values = jnp.einsum(
        "hqk,qhd->khd", chances.astype(jnp.bfloat16), grad_out, preferred_element_type=jnp.float32
    )
    grad_chances = jnp.einsum(
        "qhd,khd->hqk", grad_out, value_part, preferred_element_type=jnp.float32
    )
    grad_scores = (chances * (grad_chances - row_dot[..., None])).astype(jnp.bfloat16)
    grad_queries = (
        jnp.einsum("hqk,khd->qhd", grad_scores, key_part, preferred_element_type=jnp.float32)
        * scale
    )
    grad_keys = (
        jnp.einsum("hqk,qhd->khd", grad_scores, queries, preferred_element_type=jnp.float32) * scale
    )
    return (grad_queries, grad_keys, grad_values)


def visit_back(queries, key_part, value_part, grad_out, row_dot, log_total, query_frame, key_frame):
    return backward_block(
        queries, key_part, value_part, grad_out, row_dot, log_total, query_frame, key_frame
    )


def pass_grads(grad_keys, grad_values):
    return (
        from_behind(grad_keys.astype(jnp.bfloat16), "blk", 1).astype(grad_keys.dtype),
        from_behind(grad_values.astype(jnp.bfloat16), "blk", 1).astype(grad_values.dtype),
    )


def attend_backward(
    queries, key_block, values, grad_out, attended, log_total, query_frame, token_frame, chain_index
):
    row_count = queries.shape[0]
    chain_count = lax.axis_size("blk")
    row_dot = jnp.transpose(jnp.sum(grad_out.astype(jnp.float32) * attended, axis=-1))
    own_frame = lax.dynamic_slice_in_dim(token_frame, chain_index * row_count, row_count)
    grad_queries, grad_keys, grad_values = visit_back(
        queries, key_block, values, grad_out, row_dot, log_total, query_frame, own_frame
    )

    def hop_turn(hop_index, carried):
        query_grad, keys_now, values_now, key_grad, value_grad = carried
        keys_now, values_now = from_behind((keys_now, values_now), "blk", 1)
        key_grad, value_grad = pass_grads(key_grad, value_grad)
        source_dev = (chain_index - hop_index) % chain_count
        key_frame = lax.dynamic_slice_in_dim(token_frame, source_dev * row_count, row_count)
        more_query, more_keys, more_values = visit_back(
            queries, keys_now, values_now, grad_out, row_dot, log_total, query_frame, key_frame
        )
        return (
            query_grad + more_query,
            keys_now,
            values_now,
            key_grad + more_keys,
            value_grad + more_values,
        )

    carried = lax.fori_loop(
        1, chain_count, hop_turn, (grad_queries, key_block, values, grad_keys, grad_values)
    )
    grad_keys, grad_values = pass_grads(carried[3], carried[4])
    return (carried[0], grad_keys, grad_values)


def per_device(
    clean_latents,
    noise_sample,
    noise_levels,
    clean_flags,
    span_frame,
    patch_master,
    patch_first,
    patch_second,
    level_master,
    level_first,
    level_second,
    adaptive_master,
    adaptive_first,
    adaptive_second,
    triple_master,
    triple_first,
    triple_second,
    project_master,
    project_first,
    project_second,
    expand_master,
    expand_first,
    expand_second,
    reduce_master,
    reduce_first,
    reduce_second,
    readout_master,
    readout_first,
    readout_second,
):
    low_type = jnp.bfloat16
    masters = (
        patch_master,
        level_master,
        adaptive_master,
        triple_master,
        project_master,
        expand_master,
        reduce_master,
        readout_master,
    )
    firsts = (
        patch_first,
        level_first,
        adaptive_first,
        triple_first,
        project_first,
        expand_first,
        reduce_first,
        readout_first,
    )
    seconds = (
        patch_second,
        level_second,
        adaptive_second,
        triple_second,
        project_second,
        expand_second,
        reduce_second,
        readout_second,
    )
    gathered = (
        lax.all_gather(patch_master.astype(low_type), ("batch", "blk"), axis=1, tiled=True),
        lax.all_gather(level_master.astype(low_type), ("batch", "blk"), axis=1, tiled=True),
        lax.all_gather(adaptive_master.astype(low_type), ("batch", "blk"), axis=0, tiled=True),
        lax.all_gather(triple_master.astype(low_type), ("batch", "blk"), axis=0, tiled=True),
        lax.all_gather(project_master.astype(low_type), ("batch", "blk"), axis=0, tiled=True),
        lax.all_gather(expand_master.astype(low_type), ("batch", "blk"), axis=0, tiled=True),
        lax.all_gather(reduce_master.astype(low_type), ("batch", "blk"), axis=0, tiled=True),
        lax.all_gather(readout_master.astype(low_type), ("batch", "blk"), axis=0, tiled=True),
    )
    (
        patch_weight,
        table_weight,
        adapt_weight,
        triple_weight,
        project_weight,
        expand_weight,
        reduce_weight,
        readout_weight,
    ) = gathered
    clip_index = lax.axis_index("batch")
    chain_index = lax.axis_index("blk")
    owner_index = clip_index * lax.axis_size("blk") + chain_index
    token_count = clean_latents.shape[1]
    frame_local = token_count // FRAME_TOK
    frame_start = chain_index * frame_local
    my_levels = lax.dynamic_slice_in_dim(
        lax.dynamic_index_in_dim(noise_levels, clip_index, 0, keepdims=False),
        frame_start,
        frame_local,
    )
    my_flags = lax.dynamic_slice_in_dim(
        lax.dynamic_index_in_dim(clean_flags, clip_index, 0, keepdims=False),
        frame_start,
        frame_local,
    )
    my_frames = lax.dynamic_slice_in_dim(span_frame, frame_start, frame_local)
    token_frame = jnp.repeat(span_frame, FRAME_TOK)
    query_frame = jnp.repeat(my_frames, FRAME_TOK)
    alpha_bar, noised, table_index = plan(my_levels, my_flags)
    clean_tok = clean_latents[0]
    noise_tok = noise_sample[0]
    inputs = noised_input(clean_tok, noise_tok, alpha_bar, noised).astype(low_type)
    one_hot = (table_index[:, None] == jnp.arange(NB + 1, dtype=jnp.int32)[None, :]).astype(
        jnp.float32
    )
    pre_cond = jnp.dot(one_hot, table_weight.astype(jnp.float32), precision=lax.Precision.HIGHEST)
    cond_value, silu_back = jax.vjp(jax.nn.silu, pre_cond)
    cond_low = cond_value.astype(low_type)
    adapt = product(cond_low, adapt_weight)
    shift_one, scale_one, gate_one, shift_two, scale_two, gate_two = jnp.split(adapt, 6, axis=1)
    hidden_zero = product(inputs, patch_weight)
    normed, first_back = jax.vjp(modulate, hidden_zero, shift_one, scale_one)
    normed_low = normed.astype(low_type)
    triple = product(normed_low, triple_weight).reshape(token_count, 3, HEADS, HEAD_DIM)
    cosine_table, sine_table = rotary(my_frames, token_count)
    queries = rotate(triple[:, 0], cosine_table, sine_table).astype(low_type)
    key_block = rotate(triple[:, 1], cosine_table, sine_table).astype(low_type)
    values = triple[:, 2].astype(low_type)
    attended, log_total = attend_forward(
        queries, key_block, values, query_frame, token_frame, chain_index
    )
    attended_low = attended.reshape(token_count, D).astype(low_type)
    branch = product(attended_low, project_weight)
    hidden_one = hidden_zero + per_frame(gate_one, branch)
    mixed_tok, second_back = jax.vjp(modulate, hidden_one, shift_two, scale_two)
    mixed_low = mixed_tok.astype(low_type)
    inner = product(mixed_low, expand_weight)
    active, gelu_back = jax.vjp(gelu_tanh, inner)
    active_low = active.astype(low_type)
    outer = product(active_low, reduce_weight)
    hidden_two = hidden_one + per_frame(gate_two, outer)
    final, final_back = jax.vjp(layer_norm, hidden_two)
    final_low = final.astype(low_type)
    predicted = product(final_low, readout_weight)
    residue = predicted - noise_tok
    frame_loss = jnp.mean(jnp.square(residue).reshape(frame_local, -1), axis=1) * noised
    frame_count = jnp.sum((1 - clean_flags).astype(jnp.float32))
    loss_scale = noised * (2.0 / (FRAME_TOK * PATCH_FEAT)) / jnp.maximum(frame_count, 1.0)
    grad_pred = (
        (residue.reshape(frame_local, -1, residue.shape[-1]) * loss_scale[:, None, None])
        .reshape(residue.shape)
        .astype(low_type)
    )
    grad_readout = across(final_low, grad_pred)
    (grad_hidden_two,) = final_back(against(grad_pred, readout_weight))
    grad_outer = per_frame(gate_two, grad_hidden_two).astype(low_type)
    grad_gate_two = frame_sum(gate_two, grad_hidden_two * outer)
    grad_reduce = across(active_low, grad_outer)
    (grad_inner,) = gelu_back(against(grad_outer, reduce_weight))
    grad_inner_low = grad_inner.astype(low_type)
    grad_expand = across(mixed_low, grad_inner_low)
    hidden_part, grad_shift_two, grad_scale_two = second_back(
        against(grad_inner_low, expand_weight)
    )
    grad_hidden_one = grad_hidden_two + hidden_part
    grad_branch = per_frame(gate_one, grad_hidden_one).astype(low_type)
    grad_gate_one = frame_sum(gate_one, grad_hidden_one * branch)
    grad_project = across(attended_low, grad_branch)
    grad_attended = (
        against(grad_branch, project_weight).astype(low_type).reshape(token_count, HEADS, HEAD_DIM)
    )
    grad_queries, grad_keys, grad_values = attend_backward(
        queries,
        key_block,
        values,
        grad_attended,
        attended,
        log_total,
        query_frame,
        token_frame,
        chain_index,
    )
    grad_triple_tok = (
        jnp.stack(
            [
                rotate(grad_queries, cosine_table, -sine_table),
                rotate(grad_keys, cosine_table, -sine_table),
                grad_values,
            ],
            axis=1,
        )
        .reshape(token_count, 3 * D)
        .astype(low_type)
    )
    grad_triple = across(normed_low, grad_triple_tok)
    hidden_part, grad_shift_one, grad_scale_one = first_back(
        against(grad_triple_tok, triple_weight)
    )
    grad_hidden_zero = (grad_hidden_one + hidden_part).astype(low_type)
    grad_patch = across(inputs, grad_hidden_zero)
    grad_adapt_tok = jnp.concatenate(
        [
            grad_shift_one,
            grad_scale_one,
            grad_gate_one,
            grad_shift_two,
            grad_scale_two,
            grad_gate_two,
        ],
        axis=1,
    ).astype(low_type)
    (grad_pre,) = silu_back(against(grad_adapt_tok, adapt_weight))
    cond_all, adapt_tok_all = (
        lax.all_gather(cond_low, ("batch", "blk"), axis=0, tiled=True),
        lax.all_gather(grad_adapt_tok, ("batch", "blk"), axis=0, tiled=True),
    )
    pre_all, hot_all = (
        lax.all_gather(grad_pre, ("batch", "blk"), axis=0, tiled=True),
        lax.all_gather(one_hot, ("batch", "blk"), axis=0, tiled=True),
    )
    adapt_rows = adaptive_master.shape[0]
    table_cols = level_master.shape[1]
    cond_own = lax.dynamic_slice_in_dim(cond_all, owner_index * adapt_rows, adapt_rows, 1)
    adapt_own = across(cond_own, adapt_tok_all)
    pre_own = lax.dynamic_slice_in_dim(pre_all, owner_index * table_cols, table_cols, 1)
    table_own = lax.dot_general(
        hot_all,
        pre_own,
        (((0,), (0,)), ((), ())),
        precision=lax.Precision.HIGHEST,
        preferred_element_type=jnp.float32,
    )
    rest = (
        lax.psum_scatter(grad_patch, ("batch", "blk"), scatter_dimension=1, tiled=True),
        lax.psum_scatter(grad_triple, ("batch", "blk"), scatter_dimension=0, tiled=True),
        lax.psum_scatter(grad_project, ("batch", "blk"), scatter_dimension=0, tiled=True),
        lax.psum_scatter(grad_expand, ("batch", "blk"), scatter_dimension=0, tiled=True),
        lax.psum_scatter(grad_reduce, ("batch", "blk"), scatter_dimension=0, tiled=True),
        lax.psum_scatter(grad_readout, ("batch", "blk"), scatter_dimension=0, tiled=True),
    )
    reduced = (rest[0], table_own, adapt_own, rest[1], rest[2], rest[3], rest[4], rest[5])
    squares = sum((jnp.sum(gradient * gradient) for gradient in reduced))
    level_hits = (my_levels[:, None] == jnp.arange(NB, dtype=jnp.int32)[None, :]).astype(
        jnp.float32
    )
    bucket_local = jnp.sum(level_hits * frame_loss[:, None], axis=0)
    global_sums = lax.psum((squares, jnp.sum(frame_loss), bucket_local), ("batch", "blk"))
    clip_norm = jnp.sqrt(global_sums[0])
    factor = jnp.minimum(1.0, clip_bound / clip_norm)
    new = [
        adamw_update(
            masters[item], firsts[item], seconds[item], reduced[item], factor, learn_rates[item]
        )
        for item in range(8)
    ]
    return (
        global_sums[1],
        frame_count,
        global_sums[2],
        clip_norm,
        new[0][0],
        new[0][1],
        new[0][2],
        new[1][0],
        new[1][1],
        new[1][2],
        new[2][0],
        new[2][1],
        new[2][2],
        new[3][0],
        new[3][1],
        new[3][2],
        new[4][0],
        new[4][1],
        new[4][2],
        new[5][0],
        new[5][1],
        new[5][2],
        new[6][0],
        new[6][1],
        new[6][2],
        new[7][0],
        new[7][1],
        new[7][2],
    )


def solution(mesh):
    in_specs = (
        P("batch", "blk", None),
        P("batch", "blk", None),
        P(),
        P(),
        P(),
        P(None, ("batch", "blk")),
        P(None, ("batch", "blk")),
        P(None, ("batch", "blk")),
        P(None, ("batch", "blk")),
        P(None, ("batch", "blk")),
        P(None, ("batch", "blk")),
        P(("batch", "blk"), None),
        P(("batch", "blk"), None),
        P(("batch", "blk"), None),
        P(("batch", "blk"), None),
        P(("batch", "blk"), None),
        P(("batch", "blk"), None),
        P(("batch", "blk"), None),
        P(("batch", "blk"), None),
        P(("batch", "blk"), None),
        P(("batch", "blk"), None),
        P(("batch", "blk"), None),
        P(("batch", "blk"), None),
        P(("batch", "blk"), None),
        P(("batch", "blk"), None),
        P(("batch", "blk"), None),
        P(("batch", "blk"), None),
        P(("batch", "blk"), None),
        P(("batch", "blk"), None),
    )
    out_specs = (
        P(),
        P(),
        P(),
        P(),
        P(None, ("batch", "blk")),
        P(None, ("batch", "blk")),
        P(None, ("batch", "blk")),
        P(None, ("batch", "blk")),
        P(None, ("batch", "blk")),
        P(None, ("batch", "blk")),
        P(("batch", "blk"), None),
        P(("batch", "blk"), None),
        P(("batch", "blk"), None),
        P(("batch", "blk"), None),
        P(("batch", "blk"), None),
        P(("batch", "blk"), None),
        P(("batch", "blk"), None),
        P(("batch", "blk"), None),
        P(("batch", "blk"), None),
        P(("batch", "blk"), None),
        P(("batch", "blk"), None),
        P(("batch", "blk"), None),
        P(("batch", "blk"), None),
        P(("batch", "blk"), None),
        P(("batch", "blk"), None),
        P(("batch", "blk"), None),
        P(("batch", "blk"), None),
        P(("batch", "blk"), None),
    )
    return jax.shard_map(
        per_device, mesh=mesh, in_specs=in_specs, out_specs=out_specs, check_vma=False
    )
```

profile of v0, /device:TPU:0, one launch (start us, length us, event | category | flops | bytes accessed | tf_op | source)
XLA Modules:
  0.0 2129.2 jit_solution(11827831868776063078)
XLA Ops:
  20.1 44.1 %all-gather.1 = bf16[32,32,16]{1,2,0:T(8,128)(2,1)S(1)} all-gather(bf16[1,32,16]{1,2,0:T(8,128)(2,1)S(1)} %convert_bitcast_fusion), channel_id=1, replica_groups=mesh['batch'=4,'blk'=8] {'batch','blk'}, dimensions={0}, use_global_device_ids=true | all-gather | bytes 33792 | tf_op jit(solution)/shard_map/all_gather | solution.py:334
  65.0 37.8 %all-gather = bf16[32,32,16]{1,2,0:T(8,128)(2,1)S(1)} all-gather(bf16[1,32,16]{1,2,0:T(8,128)(2,1)S(1)} %convert_bitcast_fusion.1), channel_id=1, replica_groups=mesh['batch'=4,'blk'=8] {'batch','blk'}, dimensions={0}, use_global_device_ids=true | all-gather | bytes 33792 | tf_op jit(solution)/shard_map/all_gather | solution.py:327
  103.0 39.8 %all_gather.37 = bf16[33,1024]{0,1:T(8,128)(2,1)S(1)} all-gather(bf16[33,32]{0,1:T(8,128)(2,1)S(1)} %convert_element_type.236), channel_id=1, replica_groups=mesh['batch'=4,'blk'=8] {'batch','blk'}, dimensions={1}, use_global_device_ids=true | all-gather | bytes 69696 | tf_op jit(solution)/shard_map/all_gather | solution.py:328
  156.7 26.9 %all-gather.12.cloned.1.call-done = bf16[1024,6144]{1,0:T(8,128)(2,1)} async-done(((bf16[32,6144]{1,0:T(8,128)(2,1)}), bf16[1024,6144]{1,0:T(8,128)(2,1)}) %all-gather.12.cloned.1.call-update) | async-done | bytes 12582928 | tf_op jit(solution)/shard_map/all_gather | solution.py:329
  234.9 352.0 %while.49 = (s32[]{:T(128)}, f32[16,512]{1,0:T(8,128)S(1)}, f32[16,512]{1,0:T(8,128)S(1)}, f32[16,512,64]{1,2,0:T(8,128)}, bf16[512,16,64]{0,2,1:T(8,128)(2,1)},...) while((s32[]{:T(128)}, f32[16,512]{1,0:T(8,128)S(1)}, ...), condition=%wide.region_7.8_spmd.clone, body=%wide.region_4.7_spmd.clone.sunk | while | flops 1121206272 | bytes 88619472 | solution.py:184
  237.0 14.4 collective-permute-done
  280.5 21.7 %collective-permute-done = bf16[512,16,64]{0,2,1:T(8,128)(2,1)S(1)} collective-permute-done((bf16[512,16,64]{0,2,1:T(8,128)(2,1)}, bf16[512,16,64]{0,2,1:T(8,128)(2,1)S(1)}, u32[]{:S(2)}, u32[]{:S(2)}) %collective-permute-start) | collective-permute-done | bytes 1048608 | tf_op jit(solution)/shard_map/while/body/eval_jaxpr/ppermute | solution.py:28
  320.0 14.5 collective-permute-done.1
  345.7 20.8 collective-permute-done
  395.4 22.5 %collective-permute-done = bf16[512,16,64]{0,2,1:T(8,128)(2,1)S(1)} collective-permute-done((bf16[512,16,64]{0,2,1:T(8,128)(2,1)}, bf16[512,16,64]{0,2,1:T(8,128)(2,1)S(1)}, u32[]{:S(2)}, u32[]{:S(2)}) %collective-permute-start) | collective-permute-done | bytes 1048608 | tf_op jit(solution)/shard_map/while/body/eval_jaxpr/ppermute | solution.py:28
  455.8 15.2 collective-permute-done
  499.8 15.2 collective-permute-done
  543.8 15.2 collective-permute-done
  682.6 437.5 %while.50 = (s32[]{:T(128)}, f32[512,16,64]{0,2,1:T(8,128)}, bf16[512,16,64]{0,2,1:T(8,128)(2,1)}, bf16[512,16,64]{0,2,1:T(8,128)(2,1)}, bf16[512,16,64]{0,2,1:T...) while((s32[]{:T(128)}, f32[512,16,64]{0,2,1:T(8,128)}, ...), condition=%wide.region_25.26_spmd.clone, body=%wide.region_24.25_spmd.clone.sunk | while | flops 2731278336 | bytes 134068808 | solution.py:257
  684.1 15.0 collective-permute-done.3
  746.4 15.2 collective-permute-done.3
  808.9 15.2 collective-permute-done.3
  871.3 15.2 collective-permute-done.3
  933.8 15.2 collective-permute-done.3
  996.3 15.2 collective-permute-done.3
  1058.7 15.2 collective-permute-done.3
  1122.9 13.7 collective-permute-done.6
  1190.7 15.1 fusion.108
  1206.6 38.1 %all-gather.2 = f32[32,2,33]{2,1,0:T(2,128)} all-gather(f32[1,2,33]{2,1,0:T(2,128)S(1)} %convert_bitcast_fusion.2), channel_id=1, replica_groups=mesh['batch'=4,'blk'=8] {'batch','blk'}, dimensions={0}, use_global_device_ids=true | all-gather | bytes 8712 | tf_op jit(solution)/shard_map/all_gather | solution.py:475
  1267.5 36.9 %all-gather.4 = bf16[32,2,1024]{2,1,0:T(2,128)(2,1)S(1)} all-gather(bf16[1,2,1024]{2,1,0:T(2,128)(2,1)S(1)} %get-tuple-element.796), channel_id=1, replica_groups=mesh['batch'=4,'blk'=8] {'batch','blk'}, dimensions={0}, use_global_device_ids=true | all-gather | bytes 135168 | tf_op jit(solution)/shard_map/all_gather | solution.py:470
  1304.5 39.4 %all-gather.3 = f32[32,2,1024]{2,1,0:T(2,128)S(1)} all-gather(f32[1,2,1024]{2,1,0:T(2,128)S(1)} %get-tuple-element.797), channel_id=1, replica_groups=mesh['batch'=4,'blk'=8] {'batch','blk'}, dimensions={0}, use_global_device_ids=true | all-gather | bytes 270336 | tf_op jit(solution)/shard_map/all_gather | solution.py:474
  1344.1 40.2 %all-gather.5 = bf16[32,2,6144]{2,1,0:T(2,128)(2,1)S(1)} all-gather(bf16[1,2,6144]{2,1,0:T(2,128)(2,1)S(1)} %bitcast.283), channel_id=1, replica_groups=mesh['batch'=4,'blk'=8] {'batch','blk'}, dimensions={0}, use_global_device_ids=true | all-gather | bytes 811008 | tf_op jit(solution)/shard_map/all_gather | solution.py:471
  1395.2 138.0 %reduce-scatter.13.cloned.1.call-done = f32[32,1024]{1,0:T(8,128)} async-done(((f32[1024,1024]{1,0:T(8,128)}), f32[32,1024]{1,0:T(8,128)}) %reduce-scatter.13.cloned.1.call-update) | async-done | bytes 131088 | tf_op jit(solution)/shard_map/reduce_scatter | solution.py:492
  1534.7 156.8 %reduce-scatter.11.cloned.1.call-done = f32[32,3072]{1,0:T(8,128)} async-done(((f32[1024,3072]{1,0:T(8,128)}), f32[32,3072]{1,0:T(8,128)}) %reduce-scatter.11.cloned.1.call-update) | async-done | bytes 393232 | tf_op jit(solution)/shard_map/reduce_scatter | solution.py:491
  1694.6 185.0 %reduce-scatter.15.cloned.1.call-done = f32[32,4096]{1,0:T(8,128)} async-done(((f32[1024,4096]{1,0:T(8,128)}), f32[32,4096]{1,0:T(8,128)}) %reduce-scatter.15.cloned.1.call-update) | async-done | bytes 524304 | tf_op jit(solution)/shard_map/reduce_scatter | solution.py:493
  1882.1 184.3 %reduce-scatter.17.cloned.1.call-done = f32[128,1024]{1,0:T(8,128)} async-done(((f32[4096,1024]{1,0:T(8,128)}), f32[128,1024]{1,0:T(8,128)}) %reduce-scatter.17.cloned.1.call-update) | async-done | bytes 524304 | tf_op jit(solution)/shard_map/reduce_scatter | solution.py:494
  2069.5 37.5 %all-reduce = (f32[]{:T(128)}, f32[32]{0:T(128)}, f32[]{:T(128)}) all-reduce(f32[]{:T(128)} %get-tuple-element.758, f32[32]{0:T(128)} %fusion.93, f32[]{:T(128)S(6)} %add.549), channel_id=1, replica_groups=mesh['batch'=4,'blk'=8] {'batch','blk'}, use_global_device_ids=true, to_apply=%region_15.16 | all-reduce | flops 34 | bytes 272 | tf_op jit(solution)/shard_map/psum | solution.py:503
  (675 shorter events, 825.5 us)
Async XLA Ops:
  7.3 140.7 %all-gather.14.cloned.1.call-start = ((), (), s32[]{:S(2)}) async-start(), calls=%async_computation.7 | async-start | bytes 6488064 | tf_op jit(solution)/shard_map/all_gather | solution.py:330
  9.2 174.4 %all-gather.12.cloned.1.call-start = ((), (), s32[]{:S(2)}) async-start(), calls=%async_computation.6 | async-start | bytes 12976128 | tf_op jit(solution)/shard_map/all_gather | solution.py:329
  11.2 578.8 %all-gather.16.cloned.1.call-start = ((), (), s32[]{:S(2)}) async-start(), calls=%async_computation.8 | async-start | bytes 2162688 | tf_op jit(solution)/shard_map/all_gather | solution.py:331
  12.8 585.0 %all-gather.18.cloned.1.call-start = ((), (), s32[]{:S(2)}) async-start(), calls=%async_computation.9 | async-start | bytes 8650752 | tf_op jit(solution)/shard_map/all_gather | solution.py:332
  14.7 594.8 %all-gather.20.cloned.1.call-start = ((), (), s32[]{:S(2)}) async-start(), calls=%async_computation.10 | async-start | bytes 8650752 | tf_op jit(solution)/shard_map/all_gather | solution.py:333
  15.5 1242.6 %reduce-scatter.21.cloned.1.call-start = ((), (), s32[]{:S(2)}) async-start(), calls=%async_computation.16 | async-start | bytes 540672
  235.2 33.9 %collective-permute-start.1 = (bf16[512,16,64]{0,2,1:T(8,128)(2,1)}, bf16[512,16,64]{0,2,1:T(8,128)(2,1)S(1)}, u32[]{:S(2)}, u32[]{:S(2)}) collective-permute-start(bf16[512,16,64]{0,2,1:T(8,128)(2,1)} %get-tuple-element.993), channel_id=1, source_target_pairs={{0,1},{1,2},{2,3},{3,4},{4,5},{5,6},{6,7},{7,0},{8,9},{9,10},{10,1... | collective-permute-start | bytes 3145736 | tf_op jit(solution)/shard_map/while/body/eval_jaxpr/ppermute | solution.py:28
  279.4 55.0 %collective-permute-start.1 = (bf16[512,16,64]{0,2,1:T(8,128)(2,1)}, bf16[512,16,64]{0,2,1:T(8,128)(2,1)S(1)}, u32[]{:S(2)}, u32[]{:S(2)}) collective-permute-start(bf16[512,16,64]{0,2,1:T(8,128)(2,1)} %get-tuple-element.993), channel_id=1, source_target_pairs={{0,1},{1,2},{2,3},{3,4},{4,5},{5,6},{6,7},{7,0},{8,9},{9,10},{10,1... | collective-permute-start | bytes 3145736 | tf_op jit(solution)/shard_map/while/body/eval_jaxpr/ppermute | solution.py:28
  344.7 39.4 %collective-permute-start.1 = (bf16[512,16,64]{0,2,1:T(8,128)(2,1)}, bf16[512,16,64]{0,2,1:T(8,128)(2,1)S(1)}, u32[]{:S(2)}, u32[]{:S(2)}) collective-permute-start(bf16[512,16,64]{0,2,1:T(8,128)(2,1)} %get-tuple-element.993), channel_id=1, source_target_pairs={{0,1},{1,2},{2,3},{3,4},{4,5},{5,6},{6,7},{7,0},{8,9},{9,10},{10,1... | collective-permute-start | bytes 3145736 | tf_op jit(solution)/shard_map/while/body/eval_jaxpr/ppermute | solution.py:28
  394.3 50.2 %collective-permute-start.1 = (bf16[512,16,64]{0,2,1:T(8,128)(2,1)}, bf16[512,16,64]{0,2,1:T(8,128)(2,1)S(1)}, u32[]{:S(2)}, u32[]{:S(2)}) collective-permute-start(bf16[512,16,64]{0,2,1:T(8,128)(2,1)} %get-tuple-element.993), channel_id=1, source_target_pairs={{0,1},{1,2},{2,3},{3,4},{4,5},{5,6},{6,7},{7,0},{8,9},{9,10},{10,1... | collective-permute-start | bytes 3145736 | tf_op jit(solution)/shard_map/while/body/eval_jaxpr/ppermute | solution.py:28
  454.7 33.8 %collective-permute-start.1 = (bf16[512,16,64]{0,2,1:T(8,128)(2,1)}, bf16[512,16,64]{0,2,1:T(8,128)(2,1)S(1)}, u32[]{:S(2)}, u32[]{:S(2)}) collective-permute-start(bf16[512,16,64]{0,2,1:T(8,128)(2,1)} %get-tuple-element.993), channel_id=1, source_target_pairs={{0,1},{1,2},{2,3},{3,4},{4,5},{5,6},{6,7},{7,0},{8,9},{9,10},{10,1... | collective-permute-start | bytes 3145736 | tf_op jit(solution)/shard_map/while/body/eval_jaxpr/ppermute | solution.py:28
  498.7 33.8 %collective-permute-start.1 = (bf16[512,16,64]{0,2,1:T(8,128)(2,1)}, bf16[512,16,64]{0,2,1:T(8,128)(2,1)S(1)}, u32[]{:S(2)}, u32[]{:S(2)}) collective-permute-start(bf16[512,16,64]{0,2,1:T(8,128)(2,1)} %get-tuple-element.993), channel_id=1, source_target_pairs={{0,1},{1,2},{2,3},{3,4},{4,5},{5,6},{6,7},{7,0},{8,9},{9,10},{10,1... | collective-permute-start | bytes 3145736 | tf_op jit(solution)/shard_map/while/body/eval_jaxpr/ppermute | solution.py:28
  542.8 33.8 %collective-permute-start.1 = (bf16[512,16,64]{0,2,1:T(8,128)(2,1)}, bf16[512,16,64]{0,2,1:T(8,128)(2,1)S(1)}, u32[]{:S(2)}, u32[]{:S(2)}) collective-permute-start(bf16[512,16,64]{0,2,1:T(8,128)(2,1)} %get-tuple-element.993), channel_id=1, source_target_pairs={{0,1},{1,2},{2,3},{3,4},{4,5},{5,6},{6,7},{7,0},{8,9},{9,10},{10,1... | collective-permute-start | bytes 3145736 | tf_op jit(solution)/shard_map/while/body/eval_jaxpr/ppermute | solution.py:28
  682.8 46.2 %collective-permute-start.5 = (bf16[512,16,64]{0,2,1:T(8,128)(2,1)}, bf16[512,16,64]{0,2,1:T(8,128)(2,1)}, u32[]{:S(2)}, u32[]{:S(2)}) collective-permute-start(bf16[512,16,64]{0,2,1:T(8,128)(2,1)} %get-tuple-element.1044), channel_id=1, source_target_pairs={{0,1},{1,2},{2,3},{3,4},{4,5},{5,6},{6,7},{7,0},{8,9},{9,10},{10,1... | collective-permute-start | bytes 3145736 | tf_op jit(solution)/shard_map/while/body/eval_jaxpr/ppermute | solution.py:28
  682.9 55.8 %collective-permute-start.4 = (bf16[512,16,64]{0,2,1:T(8,128)(2,1)}, bf16[512,16,64]{0,2,1:T(8,128)(2,1)S(1)}, u32[]{:S(2)}, u32[]{:S(2)}) collective-permute-start(bf16[512,16,64]{0,2,1:T(8,128)(2,1)} %get-tuple-element.1043), channel_id=1, source_target_pairs={{0,1},{1,2},{2,3},{3,4},{4,5},{5,6},{6,7},{7,0},{8,9},{9,10},{10,1... | collective-permute-start | bytes 3145736 | tf_op jit(solution)/shard_map/while/body/eval_jaxpr/ppermute | solution.py:28
  745.2 46.3 %collective-permute-start.5 = (bf16[512,16,64]{0,2,1:T(8,128)(2,1)}, bf16[512,16,64]{0,2,1:T(8,128)(2,1)}, u32[]{:S(2)}, u32[]{:S(2)}) collective-permute-start(bf16[512,16,64]{0,2,1:T(8,128)(2,1)} %get-tuple-element.1044), channel_id=1, source_target_pairs={{0,1},{1,2},{2,3},{3,4},{4,5},{5,6},{6,7},{7,0},{8,9},{9,10},{10,1... | collective-permute-start | bytes 3145736 | tf_op jit(solution)/shard_map/while/body/eval_jaxpr/ppermute | solution.py:28
  745.2 55.9 %collective-permute-start.4 = (bf16[512,16,64]{0,2,1:T(8,128)(2,1)}, bf16[512,16,64]{0,2,1:T(8,128)(2,1)S(1)}, u32[]{:S(2)}, u32[]{:S(2)}) collective-permute-start(bf16[512,16,64]{0,2,1:T(8,128)(2,1)} %get-tuple-element.1043), channel_id=1, source_target_pairs={{0,1},{1,2},{2,3},{3,4},{4,5},{5,6},{6,7},{7,0},{8,9},{9,10},{10,1... | collective-permute-start | bytes 3145736 | tf_op jit(solution)/shard_map/while/body/eval_jaxpr/ppermute | solution.py:28
  807.7 46.3 %collective-permute-start.5 = (bf16[512,16,64]{0,2,1:T(8,128)(2,1)}, bf16[512,16,64]{0,2,1:T(8,128)(2,1)}, u32[]{:S(2)}, u32[]{:S(2)}) collective-permute-start(bf16[512,16,64]{0,2,1:T(8,128)(2,1)} %get-tuple-element.1044), channel_id=1, source_target_pairs={{0,1},{1,2},{2,3},{3,4},{4,5},{5,6},{6,7},{7,0},{8,9},{9,10},{10,1... | collective-permute-start | bytes 3145736 | tf_op jit(solution)/shard_map/while/body/eval_jaxpr/ppermute | solution.py:28
  807.7 55.9 %collective-permute-start.4 = (bf16[512,16,64]{0,2,1:T(8,128)(2,1)}, bf16[512,16,64]{0,2,1:T(8,128)(2,1)S(1)}, u32[]{:S(2)}, u32[]{:S(2)}) collective-permute-start(bf16[512,16,64]{0,2,1:T(8,128)(2,1)} %get-tuple-element.1043), channel_id=1, source_target_pairs={{0,1},{1,2},{2,3},{3,4},{4,5},{5,6},{6,7},{7,0},{8,9},{9,10},{10,1... | collective-permute-start | bytes 3145736 | tf_op jit(solution)/shard_map/while/body/eval_jaxpr/ppermute | solution.py:28
  870.2 46.3 %collective-permute-start.5 = (bf16[512,16,64]{0,2,1:T(8,128)(2,1)}, bf16[512,16,64]{0,2,1:T(8,128)(2,1)}, u32[]{:S(2)}, u32[]{:S(2)}) collective-permute-start(bf16[512,16,64]{0,2,1:T(8,128)(2,1)} %get-tuple-element.1044), channel_id=1, source_target_pairs={{0,1},{1,2},{2,3},{3,4},{4,5},{5,6},{6,7},{7,0},{8,9},{9,10},{10,1... | collective-permute-start | bytes 3145736 | tf_op jit(solution)/shard_map/while/body/eval_jaxpr/ppermute | solution.py:28
  870.2 55.9 %collective-permute-start.4 = (bf16[512,16,64]{0,2,1:T(8,128)(2,1)}, bf16[512,16,64]{0,2,1:T(8,128)(2,1)S(1)}, u32[]{:S(2)}, u32[]{:S(2)}) collective-permute-start(bf16[512,16,64]{0,2,1:T(8,128)(2,1)} %get-tuple-element.1043), channel_id=1, source_target_pairs={{0,1},{1,2},{2,3},{3,4},{4,5},{5,6},{6,7},{7,0},{8,9},{9,10},{10,1... | collective-permute-start | bytes 3145736 | tf_op jit(solution)/shard_map/while/body/eval_jaxpr/ppermute | solution.py:28
  932.6 46.3 %collective-permute-start.5 = (bf16[512,16,64]{0,2,1:T(8,128)(2,1)}, bf16[512,16,64]{0,2,1:T(8,128)(2,1)}, u32[]{:S(2)}, u32[]{:S(2)}) collective-permute-start(bf16[512,16,64]{0,2,1:T(8,128)(2,1)} %get-tuple-element.1044), channel_id=1, source_target_pairs={{0,1},{1,2},{2,3},{3,4},{4,5},{5,6},{6,7},{7,0},{8,9},{9,10},{10,1... | collective-permute-start | bytes 3145736 | tf_op jit(solution)/shard_map/while/body/eval_jaxpr/ppermute | solution.py:28
  932.6 55.9 %collective-permute-start.4 = (bf16[512,16,64]{0,2,1:T(8,128)(2,1)}, bf16[512,16,64]{0,2,1:T(8,128)(2,1)S(1)}, u32[]{:S(2)}, u32[]{:S(2)}) collective-permute-start(bf16[512,16,64]{0,2,1:T(8,128)(2,1)} %get-tuple-element.1043), channel_id=1, source_target_pairs={{0,1},{1,2},{2,3},{3,4},{4,5},{5,6},{6,7},{7,0},{8,9},{9,10},{10,1... | collective-permute-start | bytes 3145736 | tf_op jit(solution)/shard_map/while/body/eval_jaxpr/ppermute | solution.py:28
  995.1 46.3 %collective-permute-start.5 = (bf16[512,16,64]{0,2,1:T(8,128)(2,1)}, bf16[512,16,64]{0,2,1:T(8,128)(2,1)}, u32[]{:S(2)}, u32[]{:S(2)}) collective-permute-start(bf16[512,16,64]{0,2,1:T(8,128)(2,1)} %get-tuple-element.1044), channel_id=1, source_target_pairs={{0,1},{1,2},{2,3},{3,4},{4,5},{5,6},{6,7},{7,0},{8,9},{9,10},{10,1... | collective-permute-start | bytes 3145736 | tf_op jit(solution)/shard_map/while/body/eval_jaxpr/ppermute | solution.py:28
  995.1 55.9 %collective-permute-start.4 = (bf16[512,16,64]{0,2,1:T(8,128)(2,1)}, bf16[512,16,64]{0,2,1:T(8,128)(2,1)S(1)}, u32[]{:S(2)}, u32[]{:S(2)}) collective-permute-start(bf16[512,16,64]{0,2,1:T(8,128)(2,1)} %get-tuple-element.1043), channel_id=1, source_target_pairs={{0,1},{1,2},{2,3},{3,4},{4,5},{5,6},{6,7},{7,0},{8,9},{9,10},{10,1... | collective-permute-start | bytes 3145736 | tf_op jit(solution)/shard_map/while/body/eval_jaxpr/ppermute | solution.py:28
  1057.6 46.3 %collective-permute-start.5 = (bf16[512,16,64]{0,2,1:T(8,128)(2,1)}, bf16[512,16,64]{0,2,1:T(8,128)(2,1)}, u32[]{:S(2)}, u32[]{:S(2)}) collective-permute-start(bf16[512,16,64]{0,2,1:T(8,128)(2,1)} %get-tuple-element.1044), channel_id=1, source_target_pairs={{0,1},{1,2},{2,3},{3,4},{4,5},{5,6},{6,7},{7,0},{8,9},{9,10},{10,1... | collective-permute-start | bytes 3145736 | tf_op jit(solution)/shard_map/while/body/eval_jaxpr/ppermute | solution.py:28
  1057.6 55.9 %collective-permute-start.4 = (bf16[512,16,64]{0,2,1:T(8,128)(2,1)}, bf16[512,16,64]{0,2,1:T(8,128)(2,1)S(1)}, u32[]{:S(2)}, u32[]{:S(2)}) collective-permute-start(bf16[512,16,64]{0,2,1:T(8,128)(2,1)} %get-tuple-element.1043), channel_id=1, source_target_pairs={{0,1},{1,2},{2,3},{3,4},{4,5},{5,6},{6,7},{7,0},{8,9},{9,10},{10,1... | collective-permute-start | bytes 3145736 | tf_op jit(solution)/shard_map/while/body/eval_jaxpr/ppermute | solution.py:28
  1122.9 269.0 %reduce-scatter.19.cloned.1.call-start = ((), (), s32[]{:S(2)}) async-start(), calls=%async_computation.15 | async-start | bytes 540672
  1165.2 368.0 %reduce-scatter.13.cloned.1.call-start = ((), (), s32[]{:S(2)}) async-start(), calls=%async_computation.12 | async-start | bytes 4325376 | tf_op jit(solution)/shard_map/reduce_scatter | solution.py:492
  1170.1 521.5 %reduce-scatter.11.cloned.1.call-start = ((), (), s32[]{:S(2)}) async-start(), calls=%async_computation.11 | async-start | bytes 12976128 | tf_op jit(solution)/shard_map/reduce_scatter | solution.py:491
  1177.8 701.8 %reduce-scatter.15.cloned.1.call-start = ((), (), s32[]{:S(2)}) async-start(), calls=%async_computation.13 | async-start | bytes 17301504 | tf_op jit(solution)/shard_map/reduce_scatter | solution.py:493
  1189.5 876.9 %reduce-scatter.17.cloned.1.call-start = ((), (), s32[]{:S(2)}) async-start(), calls=%async_computation.14 | async-start | bytes 17301504 | tf_op jit(solution)/shard_map/reduce_scatter | solution.py:494
  (156 other events, 5927.5 us)
Sparse Core Ops, SparseCore 0:
  11.7 72.0 all-gather.13
  87.4 96.1 all-gather.11
  187.1 55.1 all-gather.15
  245.7 90.0 all-gather.17
  339.2 103.7 all-gather.19
  1123.0 135.0 reduce-scatter.20
  1261.0 130.8 reduce-scatter.18
  1394.2 138.9 reduce-scatter.12
  1539.2 152.3 reduce-scatter.10
  1693.8 185.7 reduce-scatter.14
  1882.0 184.3 reduce-scatter.16
where the time goes:
time: 2140 us; the launch traced here: 2130 us
  waiting for transfers between devices  1040 us (49%)
  matrix products  503 us (24%)
  blocking collectives  314 us (15%)
  other arithmetic  138 us (6%)
  local copies, waits for them, and re-layouts  106 us (5%)
  between operations  23.3 us (1%)
    ppermute x44, waiting for transfers between devices, from_behind(): lax.ppermute(x, axis, [(i, (i + by) % devices) for i in range(devices)])  340 us
    reduce_scatter x1, waiting for transfers between devices, per_device(): lax.psum_scatter(grad_expand, ('batch', 'blk'), scatter_dimension=0, tile...  185 us
    reduce_scatter x1, waiting for transfers between devices, per_device(): lax.psum_scatter(grad_reduce, ('batch', 'blk'), scatter_dimension=0, tile...  184 us
    reduce_scatter x1, waiting for transfers between devices, per_device(): lax.psum_scatter(grad_triple, ('batch', 'blk'), scatter_dimension=0, tile...  157 us
    reduce_scatter x1, waiting for transfers between devices, per_device(): lax.psum_scatter(grad_project, ('batch', 'blk'), scatter_dimension=0, til...  138 us
    dot_general x8, matrix products, backward_block(): jnp.einsum('qhd,khd->hqk', grad_out, value_part, preferred_element_type=j...  76.4 us
    dot_general x8, matrix products, backward_block(): jnp.einsum('hqk,qhd->khd', chances.astype(jnp.bfloat16), grad_out, prefer...  76.3 us
    reduce_sum x8, other arithmetic, forward_block(): row_total = row_total * rescale + jnp.sum(exponent, axis=-1)  73.6 us
  transfers between devices with their start and end apart: 55, of which 32 were waited for; matrix products, arithmetic and copies ran while one was open for 28% of the time, Pallas kernels for 0%

commit v1 on v0

v1 whole, which is shorter than its diff:
```python
import functools
import math

import jax
import jax.numpy as jnp
from jax import lax
from jax.experimental import pallas as pl
from jax.experimental.pallas import tpu as pltpu
from jax.sharding import Mesh
from jax.sharding import PartitionSpec as P

D = 1024
HEADS = 16
HEAD_DIM = 64
FF = 4096
PATCH_FEAT = 16
FRAME_TOK = 256
SIDE = 16
NB = 32
STEP = 10
LANES = 128
ALL = ("batch", "row", "core")


learn_rates = (0.5, 2.0, 0.05, 0.05, 0.5, 0.05, 0.05, 0.05)
beta_first = 0.9
beta_second = 0.999
decay_rate = 0.01
adam_floor = 1e-08
clip_bound = 0.02
low_type = jnp.bfloat16


def product(left, right):
    return jnp.dot(left, right, preferred_element_type=jnp.float32)


def across(left, right):
    return lax.dot_general(
        left, right, (((0,), (0,)), ((), ())), preferred_element_type=jnp.float32
    )


def against(left, right):
    return lax.dot_general(
        left, right, (((1,), (1,)), ((), ())), preferred_element_type=jnp.float32
    )


def plan(levels, clean_flags):
    alpha_bar = jnp.cos(0.5 * math.pi * (levels.astype(jnp.float32) + 1.0) / (NB + 1.0)) ** 2
    noised = (1 - clean_flags).astype(jnp.float32)
    table_index = jnp.where(clean_flags == 1, 0, levels + 1)
    return (alpha_bar, noised, table_index)


def noised_input(clean_tok, noise_tok, alpha_bar, noised):
    frame_shape = (alpha_bar.shape[0], -1, clean_tok.shape[-1])
    clean_frames = clean_tok.reshape(frame_shape)
    noise_frames = noise_tok.reshape(frame_shape)
    mixed_tok = (
        jnp.sqrt(alpha_bar)[:, None, None] * clean_frames
        + jnp.sqrt(1.0 - alpha_bar)[:, None, None] * noise_frames
    )
    return jnp.where(noised[:, None, None] > 0.5, mixed_tok, clean_frames).reshape(clean_tok.shape)


def layer_norm(hidden):
    centred = hidden - jnp.mean(hidden, axis=-1, keepdims=True)
    variance = jnp.mean(centred * centred, axis=-1, keepdims=True)
    return centred * lax.rsqrt(variance + 1e-06)


def modulate(hidden, shift, scale):
    normed = layer_norm(hidden).reshape(shift.shape[0], -1, hidden.shape[-1])
    return (normed * (1.0 + scale[:, None]) + shift[:, None]).reshape(hidden.shape)


def per_frame(gate, hidden):
    return (hidden.reshape(gate.shape[0], -1, hidden.shape[-1]) * gate[:, None]).reshape(
        hidden.shape
    )


def frame_sum(gate, hidden):
    return jnp.sum(hidden.reshape(gate.shape[0], -1, hidden.shape[-1]), axis=1)


def gelu_tanh(value):
    return jax.nn.gelu(value, approximate=True)


def adamw_update(master, first_moment, second_moment, gradient, factor, step_rate):
    clipped = gradient * factor
    first_new = beta_first * first_moment + (1.0 - beta_first) * clipped
    second_new = beta_second * second_moment + (1.0 - beta_second) * clipped * clipped
    first_hat = first_new / (1.0 - beta_first**STEP)
    second_hat = second_new / (1.0 - beta_second**STEP)
    master_new = master - step_rate * (
        first_hat / (jnp.sqrt(second_hat) + adam_floor) + decay_rate * master
    )
    return (first_new, second_new, master_new)


def lane_places():
    lane = jnp.arange(LANES, dtype=jnp.int32) % HEAD_DIM
    half = HEAD_DIM // 2
    place = lane % half
    time_count = HEAD_DIM // 8
    space_count = 3 * HEAD_DIM // 16
    sign = jnp.where(lane < half, -1.0, 1.0)
    time_freq = 10000.0 ** (-(place.astype(jnp.float32)) / time_count)
    space_place = jnp.where(place < time_count + space_count, place - time_count, place - time_count - space_count)
    space_freq = 100.0 ** (-(space_place.astype(jnp.float32)) / space_count)
    is_time = place < time_count
    is_row = (place >= time_count) & (place < time_count + space_count)
    return sign, time_freq, space_freq, is_time, is_row


def time_tables(frames):
    sign, time_freq, _, is_time, _ = lane_places()
    angle = frames.astype(jnp.float32)[:, None] * time_freq[None]
    return (
        jnp.where(is_time, jnp.cos(angle), 0.0)[:, None],
        jnp.where(is_time, jnp.sin(angle) * sign, 0.0)[:, None],
    )


def space_tables():
    sign, _, space_freq, is_time, is_row = lane_places()
    token = jnp.arange(FRAME_TOK, dtype=jnp.int32)
    row_pos = (token // SIDE).astype(jnp.float32)[:, None]
    col_pos = (token % SIDE).astype(jnp.float32)[:, None]
    angle = jnp.where(is_row[None], row_pos, col_pos) * space_freq[None]
    return (
        jnp.where(is_time, 0.0, jnp.cos(angle)),
        jnp.where(is_time, 0.0, jnp.sin(angle) * sign),
    )


def partner(value):
    half = HEAD_DIM // 2
    width = value.shape[1]
    if width == LANES:
        lane = lax.broadcasted_iota(jnp.int32, value.shape, 1)
        ahead = pltpu.roll(value, width - half, 1)
        behind = pltpu.roll(value, half, 1)
        return jnp.where(lane % HEAD_DIM < half, ahead, behind)
    return jnp.concatenate([value[:, half:], value[:, :half]], axis=1)


def triple_kernel(normed_ref, weight_ref, time_cos, time_sin, space_cos, space_sin, out_ref):
    column = pl.program_id(0)
    width = out_ref.shape[-1]
    acc = product(normed_ref[...], weight_ref[...])
    per_block = acc.shape[1] // LANES
    frames = acc.shape[0] // FRAME_TOK

    def store(piece, values):
        for part in range(LANES // width):
            out_ref[piece * (LANES // width) + part, 0] = values[
                :, part * width : (part + 1) * width
            ].astype(low_type)

    turned = column < 2 * D // acc.shape[1]

    @pl.when(turned)
    def _():
        for piece in range(per_block):
            done = []
            for frame in range(frames):
                value = acc[
                    frame * FRAME_TOK : (frame + 1) * FRAME_TOK,
                    piece * LANES : (piece + 1) * LANES,
                ]
                cosine = time_cos[frame] + space_cos[...]
                sine = time_sin[frame] + space_sin[...]
                done.append(value * cosine + partner(value) * sine)
            store(piece, jnp.concatenate(done, axis=0))

    @pl.when(jnp.logical_not(turned))
    def _():
        for piece in range(per_block):
            store(piece, acc[:, piece * LANES : (piece + 1) * LANES])


def triple_heads(normed, weight, times, spaces, groups):
    tokens = normed.shape[0]
    width = D // groups
    block = 256
    per_block = block // width
    per_part = D // block
    return pl.pallas_call(
        triple_kernel,
        grid=(3 * D // block,),
        in_specs=[
            pl.BlockSpec((tokens, D), lambda j: (0, 0)),
            pl.BlockSpec((D, block), lambda j: (0, j)),
            pl.BlockSpec(times[0].shape, lambda j: (0, 0, 0)),
            pl.BlockSpec(times[1].shape, lambda j: (0, 0, 0)),
            pl.BlockSpec(spaces[0].shape, lambda j: (0, 0)),
            pl.BlockSpec(spaces[1].shape, lambda j: (0, 0)),
        ],
        out_specs=pl.BlockSpec(
            (per_block, 1, tokens, width), lambda j: (j % per_part, j // per_part, 0, 0)
        ),
        out_shape=jax.ShapeDtypeStruct((groups, 3, tokens, width), low_type),
        compiler_params=pltpu.CompilerParams(vmem_limit_bytes=32 * 1024 * 1024),
        name="triple_heads",
    )(normed, weight, *times, *spaces)


def head_stack(value):
    count = value.shape[1] // HEAD_DIM
    if count == 1:
        return value
    lane = lax.broadcasted_iota(jnp.int32, value.shape, 1)
    zero = jnp.zeros_like(value)
    return jnp.concatenate(
        [jnp.where(lane // HEAD_DIM == head, value, zero) for head in range(count)], axis=0
    )


def attend_kernel(
    order_ref, count_ref, query_ref, key_ref, value_ref, out_ref, flat_ref, log_ref, turned_ref
):
    step = pl.program_id(0)
    chunks, per_chunk = key_ref.shape[0], key_ref.shape[1]
    width = key_ref.shape[-1]
    heads = width // HEAD_DIM
    span = heads * FRAME_TOK

    @pl.when(step == 0)
    def _():
        def turn(chunk, carry):
            for part in range(per_chunk):
                turned_ref[chunk, part] = jnp.transpose(value_ref[chunk, part])
            return carry

        lax.fori_loop(0, chunks, turn, 0)

    queries = head_stack(query_ref[...] * jnp.asarray(HEAD_DIM**-0.5, low_type))

    def visit(place, carry):
        top, total, sums = carry
        frame = order_ref[place]
        chunk, part = frame // per_chunk, frame % per_chunk
        scores = against(key_ref[chunk, part], queries)
        new_top = jnp.maximum(top, jnp.max(scores, axis=0, keepdims=True))
        rescale = jnp.exp(top - new_top)
        chances = jnp.exp(scores - new_top)
        total = total * rescale + jnp.sum(chances, axis=0, keepdims=True)
        chances = chances.astype(low_type)
        new_sums = []
        for head in range(heads):
            columns = slice(head * FRAME_TOK, (head + 1) * FRAME_TOK)
            values = turned_ref[chunk, part, head * HEAD_DIM : (head + 1) * HEAD_DIM, :]
            new_sums.append(
                sums[head] * rescale[:, columns] + product(values, chances[:, columns])
            )
        return new_top, total, tuple(new_sums)

    initial = (
        jnp.full((1, span), -1e30, jnp.float32),
        jnp.zeros((1, span), jnp.float32),
        tuple(jnp.zeros((HEAD_DIM, FRAME_TOK), jnp.float32) for _ in range(heads)),
    )
    top, total, sums = lax.fori_loop(0, count_ref[step], visit, initial)
    log_ref[...] = top + jnp.log(total)
    inverse = 1.0 / total
    result = jnp.concatenate(
        [
            sums[head] * inverse[:, head * FRAME_TOK : (head + 1) * FRAME_TOK]
            for head in range(heads)
        ],
        axis=0,
    )
    flat_ref[...] = result
    out_ref[...] = jnp.transpose(result).astype(low_type)


def whole(shape):
    return pl.BlockSpec(shape, lambda *_: (0,) * len(shape))


def attend(order, count, queries, keys, values):
    chunks, per_chunk, _, width = queries.shape
    frames = chunks * per_chunk
    span = width // HEAD_DIM * FRAME_TOK
    return pl.pallas_call(
        attend_kernel,
        grid_spec=pltpu.PrefetchScalarGridSpec(
            num_scalar_prefetch=2,
            grid=(frames,),
            in_specs=[
                pl.BlockSpec(
                    (None, None, FRAME_TOK, width),
                    lambda i, *_: (i // per_chunk, i % per_chunk, 0, 0),
                ),
                whole(keys.shape),
                whole(values.shape),
            ],
            out_specs=[
                pl.BlockSpec(
                    (None, None, FRAME_TOK, width),
                    lambda i, *_: (i // per_chunk, i % per_chunk, 0, 0),
                ),
                pl.BlockSpec((None, width, FRAME_TOK), lambda i, *_: (i, 0, 0)),
                pl.BlockSpec((None, 1, span), lambda i, *_: (i, 0, 0)),
            ],
            scratch_shapes=[
                pltpu.VMEM((keys.shape[0], per_chunk, width, FRAME_TOK), low_type),
            ],
        ),
        out_shape=[
            jax.ShapeDtypeStruct(queries.shape, low_type),
            jax.ShapeDtypeStruct((frames, width, FRAME_TOK), jnp.float32),
            jax.ShapeDtypeStruct((frames, 1, span), jnp.float32),
        ],
        compiler_params=pltpu.CompilerParams(vmem_limit_bytes=48 * 1024 * 1024),
        name="attend",
    )(order, count, queries, keys, values)


def attend_back_kernel(
    order_ref,
    count_ref,
    query_ref,
    key_ref,
    value_ref,
    grad_ref,
    flat_ref,
    log_ref,
    query_cos,
    query_sin,
    key_cos,
    key_sin,
    space_cos,
    space_sin,
    grad_query_ref,
    grad_key_ref,
    grad_value_ref,
    stacked_query,
    stacked_grad,
    row_dot,
    sums_ref,
):
    step = pl.program_id(0)
    frames, width, _ = flat_ref.shape
    per_chunk = query_ref.shape[1]
    heads = width // HEAD_DIM
    scale = HEAD_DIM**-0.5

    @pl.when(step == 0)
    def _():
        def ready(frame, carry):
            chunk, part = frame // per_chunk, frame % per_chunk
            query = query_ref[chunk, part] * jnp.asarray(scale, low_type)
            stacked_query[frame] = head_stack(query)
            grad = grad_ref[chunk, part]
            stacked_grad[frame] = head_stack(grad)
            both = jnp.transpose(grad.astype(jnp.float32)) * flat_ref[frame]
            row_dot[frame] = jnp.concatenate(
                [
                    jnp.sum(both[head * HEAD_DIM : (head + 1) * HEAD_DIM], axis=0, keepdims=True)
                    for head in range(heads)
                ],
                axis=1,
            )
            sums_ref[frame] = jnp.zeros((width, FRAME_TOK), jnp.float32)
            return carry

        lax.fori_loop(0, frames, ready, 0)

    keys = key_ref[...]
    values = value_ref[...]
    turned_keys = jnp.transpose(keys)

    def visit(place, carry):
        grad_keys, grad_values = carry
        frame = order_ref[place]
        queries = stacked_query[frame]
        grads = stacked_grad[frame]
        scores = against(keys, queries)
        chances = jnp.exp(scores - log_ref[frame])
        grad_chances = against(values, grads)
        grad_scores = (chances * (grad_chances - row_dot[frame])).astype(low_type)
        grad_values = grad_values + product(chances.astype(low_type), grads)
        grad_keys = grad_keys + product(grad_scores, queries)
        for head in range(heads):
            rows = slice(head * HEAD_DIM, (head + 1) * HEAD_DIM)
            sums_ref[frame, rows, :] += product(
                turned_keys[rows], grad_scores[:, head * FRAME_TOK : (head + 1) * FRAME_TOK]
            )
        return grad_keys, grad_values

    zero = jnp.zeros((FRAME_TOK, width), jnp.float32)
    grad_keys, grad_values = lax.fori_loop(0, count_ref[step], visit, (zero, zero))
    space_c, space_s = space_cos[:, :width], space_sin[:, :width]
    grad_value_ref[...] = grad_values.astype(low_type)
    grad_key_ref[...] = (
        grad_keys * (key_cos[:, :width] + space_c)
        - partner(grad_keys) * (key_sin[:, :width] + space_s)
    ).astype(low_type)

    @pl.when(step == pl.num_programs(0) - 1)
    def _():
        def finish(frame, carry):
            chunk, part = frame // per_chunk, frame % per_chunk
            value = jnp.transpose(sums_ref[frame]) * scale
            grad_query_ref[chunk, part] = (
                value * (query_cos[frame][:, :width] + space_c)
                - partner(value) * (query_sin[frame][:, :width] + space_s)
            ).astype(low_type)
            return carry

        lax.fori_loop(0, frames, finish, 0)


def attend_back(
    order, count, queries, keys, values, grads, flat, logs, query_times, key_times, spaces
):
    per_chunk, width = queries.shape[1], queries.shape[3]
    frames = flat.shape[0]
    key_frames = keys.shape[0] * per_chunk
    span = width // HEAD_DIM * FRAME_TOK
    key_spec = pl.BlockSpec(
        (None, None, FRAME_TOK, width), lambda i, *_: (i // per_chunk, i % per_chunk, 0, 0)
    )
    key_time = pl.BlockSpec((None, 1, LANES), lambda i, *_: (i, 0, 0))
    return pl.pallas_call(
        attend_back_kernel,
        grid_spec=pltpu.PrefetchScalarGridSpec(
            num_scalar_prefetch=2,
            grid=(key_frames,),
            in_specs=[
                whole(queries.shape),
                key_spec,
                key_spec,
                whole(grads.shape),
                whole(flat.shape),
                whole(logs.shape),
                whole(query_times[0].shape),
                whole(query_times[1].shape),
                key_time,
                key_time,
                whole(spaces[0].shape),
                whole(spaces[1].shape),
            ],
            out_specs=[whole(queries.shape), key_spec, key_spec],
            scratch_shapes=[
                pltpu.VMEM((frames, span, width), low_type),
                pltpu.VMEM((frames, span, width), low_type),
                pltpu.VMEM((frames, 1, span), jnp.float32),
                pltpu.VMEM((frames, width, FRAME_TOK), jnp.float32),
            ],
        ),
        out_shape=[
            jax.ShapeDtypeStruct(queries.shape, low_type),
            jax.ShapeDtypeStruct(keys.shape, low_type),
            jax.ShapeDtypeStruct(keys.shape, low_type),
        ],
        compiler_params=pltpu.CompilerParams(vmem_limit_bytes=56 * 1024 * 1024),
        name="attend_back",
    )(
        order,
        count,
        queries,
        keys,
        values,
        grads,
        flat,
        logs,
        *query_times,
        *key_times,
        *spaces,
    )


def total_sum(value):
    for axis in ("core", "batch", "row"):
        size = lax.axis_size(axis)
        by = 1
        while by < size:
            value = value + lax.ppermute(value, axis, [(i, i ^ by) for i in range(size)])
            by *= 2
    return value


def staged_sum(value):
    batch, row, core = (lax.axis_size(axis) for axis in ALL)
    value = value.reshape((batch, row, core) + value.shape[1:])
    mine = lax.axis_index("core")
    send = lax.dynamic_index_in_dim(value, 1 - mine, 2, keepdims=False).astype(low_type)
    keep = lax.dynamic_index_in_dim(value, mine, 2, keepdims=False)
    swap = [(i, 1 - i) for i in range(core)]
    value = keep + lax.ppermute(send, "core", swap).astype(jnp.float32)
    for axis in ("batch", "row"):
        parts = lax.all_to_all(value.astype(low_type), axis, 0, 0, tiled=True)
        value = jnp.sum(parts.astype(jnp.float32), axis=0)
    return value


def per_device(
    clean_latents,
    noise_sample,
    noise_levels,
    clean_flags,
    span_frame,
    patch_master,
    patch_first,
    patch_second,
    level_master,
    level_first,
    level_second,
    adaptive_master,
    adaptive_first,
    adaptive_second,
    triple_master,
    triple_first,
    triple_second,
    project_master,
    project_first,
    project_second,
    expand_master,
    expand_first,
    expand_second,
    reduce_master,
    reduce_first,
    reduce_second,
    readout_master,
    readout_first,
    readout_second,
):
    masters = (
        patch_master,
        level_master,
        adaptive_master,
        triple_master,
        project_master,
        expand_master,
        reduce_master,
        readout_master,
    )
    firsts = (
        patch_first,
        level_first,
        adaptive_first,
        triple_first,
        project_first,
        expand_first,
        reduce_first,
        readout_first,
    )
    seconds = (
        patch_second,
        level_second,
        adaptive_second,
        triple_second,
        project_second,
        expand_second,
        reduce_second,
        readout_second,
    )
    batch_count, row_count, core_count = (lax.axis_size(axis) for axis in ALL)
    batch_index, row_index, core_index = (lax.axis_index(axis) for axis in ALL)
    devices = batch_count * row_count * core_count
    rows = D // devices
    token_count = clean_latents.shape[1]
    frame_local = token_count // FRAME_TOK

    moved = batch_count == row_count and HEADS % (batch_count * core_count) == 0
    if moved:
        clip_index, chunk_index = row_index, batch_index * core_count + core_index
        head_axes, head_groups = ("batch", "core"), batch_count * core_count
    else:
        clip_index, chunk_index = batch_index, row_index * core_count + core_index
        head_axes, head_groups = ("row",), row_count

    both = jnp.concatenate([clean_latents[0], noise_sample[0]], axis=1)
    if moved:
        turn = [
            (
                (a * row_count + b) * core_count + c,
                (b * row_count + a) * core_count + c,
            )
            for a in range(batch_count)
            for b in range(row_count)
            for c in range(core_count)
        ]
        both = lax.ppermute(both, ALL, turn)
    clean_tok, noise_tok = both[:, :PATCH_FEAT], both[:, PATCH_FEAT:]

    first_weights = jnp.concatenate(
        [
            triple_master.astype(low_type),
            jnp.transpose(patch_master).astype(low_type),
            readout_master.astype(low_type),
            jnp.zeros((rows, LANES - 2 * PATCH_FEAT), low_type),
        ],
        axis=1,
    )
    first_weights = lax.all_gather(first_weights, ALL, axis=0, tiled=True)
    second_weights = jnp.concatenate(
        [project_master.astype(low_type)]
        + [expand_master[:, k * D : (k + 1) * D].astype(low_type) for k in range(FF // D)]
        + [reduce_master.astype(low_type)],
        axis=0,
    )
    second_weights = lax.all_gather(second_weights, ALL, axis=0)

    levels_all = noise_levels.reshape(-1)
    flags_all = clean_flags.reshape(-1)
    _, _, index_all = plan(levels_all, flags_all)
    if moved:
        order_all = lambda v: (
            v.reshape((row_count, batch_count, core_count, frame_local) + v.shape[1:])
            .swapaxes(0, 1)
            .reshape(v.shape)
        )
    else:
        order_all = lambda v: v
    index_all = order_all(index_all)
    hot_all = (index_all[:, None] == jnp.arange(NB + 1, dtype=jnp.int32)[None, :]).astype(
        jnp.float32
    )
    pre_own = jnp.dot(
        hot_all,
        level_master.astype(low_type).astype(jnp.float32),
        precision=lax.Precision.HIGHEST,
    )
    cond_value, silu_back = jax.vjp(jax.nn.silu, pre_own)
    cond_own = cond_value.astype(low_type)
    adaptive_low = adaptive_master.astype(low_type)
    adapt_parts = lax.all_to_all(
        product(cond_own, adaptive_low).reshape(devices, frame_local, 6 * D), ALL, 0, 0, tiled=True
    )
    adapt = jnp.sum(adapt_parts, axis=0)
    shift_one, scale_one, gate_one, shift_two, scale_two, gate_two = jnp.split(adapt, 6, axis=1)

    my_levels = lax.dynamic_slice_in_dim(
        lax.dynamic_index_in_dim(noise_levels, clip_index, 0, keepdims=False),
        chunk_index * frame_local,
        frame_local,
    )
    my_flags = lax.dynamic_slice_in_dim(
        lax.dynamic_index_in_dim(clean_flags, clip_index, 0, keepdims=False),
        chunk_index * frame_local,
        frame_local,
    )
    my_frames = lax.dynamic_slice_in_dim(span_frame, chunk_index * frame_local, frame_local)
    if moved:
        query_frames = key_frames = span_frame
    else:
        by_chunk = span_frame.reshape(row_count, core_count, frame_local)
        query_frames = lax.dynamic_index_in_dim(by_chunk, core_index, 1, keepdims=False).reshape(-1)
        key_frames = by_chunk.swapaxes(0, 1).reshape(-1)
    query_total, key_total = query_frames.shape[0], key_frames.shape[0]
    earlier = jnp.sum(key_frames[None, :] < key_frames[:, None], axis=1)
    key_order = jnp.sum(
        jnp.where(earlier[:, None] == jnp.arange(key_total)[None, :], jnp.arange(key_total)[:, None], 0),
        axis=0,
    ).astype(jnp.int32)
    key_count = jnp.sum(key_frames[None, :] <= query_frames[:, None], axis=1).astype(jnp.int32)
    later = jnp.sum(query_frames[None, :] > query_frames[:, None], axis=1)
    query_order = jnp.sum(
        jnp.where(later[:, None] == jnp.arange(query_total)[None, :], jnp.arange(query_total)[:, None], 0),
        axis=0,
    ).astype(jnp.int32)
    query_count = jnp.sum(query_frames[None, :] >= key_frames[:, None], axis=1).astype(jnp.int32)
    my_times, query_times, key_times = (
        time_tables(my_frames),
        time_tables(query_frames),
        time_tables(key_frames),
    )
    spaces = space_tables()

    alpha_bar, noised, _ = plan(my_levels, my_flags)
    inputs = noised_input(clean_tok, noise_tok, alpha_bar, noised).astype(low_type)
    patch_turned = first_weights[:, 3 * D : 3 * D + PATCH_FEAT]
    readout_weight = first_weights[:, 3 * D + PATCH_FEAT : 3 * D + 2 * PATCH_FEAT]
    triple_weight = first_weights
    hidden_zero = against(inputs, patch_turned)
    normed, first_back = jax.vjp(modulate, hidden_zero, shift_one, scale_one)
    normed_low = normed.astype(low_type)

    heads = triple_heads(normed_low, triple_weight, my_times, spaces, head_groups)
    heads = lax.all_to_all(heads, head_axes, 0, 0, tiled=True)
    width = D // head_groups
    heads = heads.reshape(head_groups, 3, frame_local, FRAME_TOK, width)
    queries, keys, values = heads[:, 0], heads[:, 1], heads[:, 2]
    if not moved:
        keys = lax.all_gather(keys, "core", axis=0, tiled=True)
        values = lax.all_gather(values, "core", axis=0, tiled=True)
    attended, flat, logs = attend(key_order, key_count, queries, keys, values)
    attended = attended.reshape(head_groups, token_count, width)
    attended = lax.all_to_all(attended, head_axes, 0, 0, tiled=True)
    attended_low = attended.swapaxes(0, 1).reshape(token_count, D)

    project_weight = second_weights[:, :rows].reshape(D, D)
    expand_weights = [
        second_weights[:, (1 + k) * rows : (2 + k) * rows].reshape(D, D) for k in range(FF // D)
    ]
    reduce_weight = second_weights[:, (1 + FF // D) * rows :].reshape(FF, D)
    expand_weight = jnp.concatenate(expand_weights, axis=1)

    branch = product(attended_low, project_weight)
    hidden_one = hidden_zero + per_frame(gate_one, branch)
    mixed_tok, second_back = jax.vjp(modulate, hidden_one, shift_two, scale_two)
    mixed_low = mixed_tok.astype(low_type)
    inner = product(mixed_low, expand_weight)
    active, gelu_back = jax.vjp(gelu_tanh, inner)
    active_low = active.astype(low_type)
    outer = product(active_low, reduce_weight)
    hidden_two = hidden_one + per_frame(gate_two, outer)
    final, final_back = jax.vjp(layer_norm, hidden_two)
    final_low = final.astype(low_type)
    predicted = product(final_low, readout_weight)
    residue = predicted - noise_tok
    frame_loss = jnp.mean(jnp.square(residue).reshape(frame_local, -1), axis=1) * noised
    frame_count = jnp.sum((1 - clean_flags).astype(jnp.float32))
    loss_scale = noised * (2.0 / (FRAME_TOK * PATCH_FEAT)) / jnp.maximum(frame_count, 1.0)
    grad_pred = (
        (residue.reshape(frame_local, -1, residue.shape[-1]) * loss_scale[:, None, None])
        .reshape(residue.shape)
        .astype(low_type)
    )
    grad_readout = across(final_low, grad_pred)
    (grad_hidden_two,) = final_back(against(grad_pred, readout_weight))
    grad_outer = per_frame(gate_two, grad_hidden_two).astype(low_type)
    grad_gate_two = frame_sum(gate_two, grad_hidden_two * outer)
    grad_reduce = across(active_low, grad_outer)
    (grad_inner,) = gelu_back(against(grad_outer, reduce_weight))
    grad_inner_low = grad_inner.astype(low_type)
    grad_expand = across(mixed_low, grad_inner_low)
    hidden_part, grad_shift_two, grad_scale_two = second_back(
        against(grad_inner_low, expand_weight)
    )
    grad_hidden_one = grad_hidden_two + hidden_part
    grad_branch = per_frame(gate_one, grad_hidden_one).astype(low_type)
    grad_gate_one = frame_sum(gate_one, grad_hidden_one * branch)
    grad_project = across(attended_low, grad_branch)
    second_grads = jnp.concatenate(
        [grad_project.reshape(devices, rows, D)]
        + [
            grad_expand[:, k * D : (k + 1) * D].reshape(devices, rows, D) for k in range(FF // D)
        ]
        + [grad_reduce.reshape(devices, FF // devices, D)],
        axis=1,
    )
    second_own = lax.psum_scatter(second_grads, ALL, scatter_dimension=0)

    grad_attended = (
        against(grad_branch, project_weight)
        .astype(low_type)
        .reshape(token_count, head_groups, width)
        .swapaxes(0, 1)
    )
    grad_attended = lax.all_to_all(grad_attended, head_axes, 0, 0, tiled=True)
    grad_attended = grad_attended.reshape(queries.shape)
    grad_queries, grad_keys, grad_values = attend_back(
        query_order,
        query_count,
        queries,
        keys,
        values,
        grad_attended,
        flat,
        logs,
        query_times,
        key_times,
        spaces,
    )
    if not moved:
        grad_keys, grad_values = (
            lax.psum_scatter(
                item.astype(jnp.float32), "core", scatter_dimension=0, tiled=True
            ).astype(low_type)
            for item in (grad_keys, grad_values)
        )
    grad_heads = jnp.stack([grad_queries, grad_keys, grad_values], axis=1)
    grad_heads = lax.all_to_all(
        grad_heads.reshape(head_groups, 3, token_count, width), head_axes, 0, 0, tiled=True
    )
    grad_triple_tok = jnp.transpose(grad_heads, (2, 1, 0, 3)).reshape(token_count, 3 * D)
    grad_triple = across(normed_low, grad_triple_tok)
    hidden_part, grad_shift_one, grad_scale_one = first_back(
        against(grad_triple_tok, triple_weight[:, : 3 * D])
    )
    grad_hidden_zero = (grad_hidden_one + hidden_part).astype(low_type)
    grad_patch = across(grad_hidden_zero, inputs)
    first_grads = jnp.concatenate(
        [
            grad_triple,
            grad_patch,
            grad_readout,
            jnp.zeros((D, LANES - 2 * PATCH_FEAT), jnp.float32),
        ],
        axis=1,
    )
    first_own = staged_sum(first_grads.reshape(devices, rows, first_grads.shape[1]))

    grad_adapt_tok = jnp.concatenate(
        [
            grad_shift_one,
            grad_scale_one,
            grad_gate_one,
            grad_shift_two,
            grad_scale_two,
            grad_gate_two,
        ],
        axis=1,
    ).astype(low_type)
    adapt_tok_all = lax.all_gather(grad_adapt_tok, ALL, axis=0, tiled=True)
    adapt_own = across(cond_own, adapt_tok_all)
    (grad_pre,) = silu_back(against(adapt_tok_all, adaptive_low))
    table_own = lax.dot_general(
        hot_all,
        grad_pre,
        (((0,), (0,)), ((), ())),
        precision=lax.Precision.HIGHEST,
        preferred_element_type=jnp.float32,
    )
    expand_own = jnp.concatenate(
        [second_own[(1 + k) * rows : (2 + k) * rows] for k in range(FF // D)], axis=1
    )
    reduced = (
        jnp.transpose(first_own[:, 3 * D : 3 * D + PATCH_FEAT]),
        table_own,
        adapt_own,
        first_own[:, : 3 * D],
        second_own[:rows],
        expand_own,
        second_own[(1 + FF // D) * rows :],
        first_own[:, 3 * D + PATCH_FEAT : 3 * D + 2 * PATCH_FEAT],
    )
    squares = sum((jnp.sum(gradient * gradient) for gradient in reduced))
    level_hits = (my_levels[:, None] == jnp.arange(NB, dtype=jnp.int32)[None, :]).astype(
        jnp.float32
    )
    bucket_local = jnp.sum(level_hits * frame_loss[:, None], axis=0)
    sums = jnp.zeros((8, LANES), jnp.float32)
    sums = sums.at[0, :NB].set(bucket_local)
    sums = sums.at[1, 0].set(squares)
    sums = sums.at[2, 0].set(jnp.sum(frame_loss))
    sums = total_sum(sums)
    clip_norm = jnp.sqrt(sums[1, 0])
    factor = jnp.minimum(1.0, clip_bound / clip_norm)
    new = [
        adamw_update(
            masters[item], firsts[item], seconds[item], reduced[item], factor, learn_rates[item]
        )
        for item in range(8)
    ]
    return (sums[2, 0], frame_count, sums[0, :NB], clip_norm) + tuple(
        item for triple in new for item in triple
    )


def solution(mesh):
    in_specs = (
        P("batch", ("row", "core"), None),
        P("batch", ("row", "core"), None),
        P(),
        P(),
        P(),
        P(None, ALL),
        P(None, ALL),
        P(None, ALL),
        P(None, ALL),
        P(None, ALL),
        P(None, ALL),
        P(ALL, None),
        P(ALL, None),
        P(ALL, None),
        P(ALL, None),
        P(ALL, None),
        P(ALL, None),
        P(ALL, None),
        P(ALL, None),
        P(ALL, None),
        P(ALL, None),
        P(ALL, None),
        P(ALL, None),
        P(ALL, None),
        P(ALL, None),
        P(ALL, None),
        P(ALL, None),
        P(ALL, None),
        P(ALL, None),
    )
    out_specs = (
        P(),
        P(),
        P(),
        P(),
        P(None, ALL),
        P(None, ALL),
        P(None, ALL),
        P(None, ALL),
        P(None, ALL),
        P(None, ALL),
        P(ALL, None),
        P(ALL, None),
        P(ALL, None),
        P(ALL, None),
        P(ALL, None),
        P(ALL, None),
        P(ALL, None),
        P(ALL, None),
        P(ALL, None),
        P(ALL, None),
        P(ALL, None),
        P(ALL, None),
        P(ALL, None),
        P(ALL, None),
        P(ALL, None),
        P(ALL, None),
        P(ALL, None),
        P(ALL, None),
    )
    batch_size, blk_size = mesh.shape["batch"], mesh.shape["blk"]
    inner = Mesh(mesh.devices.reshape(batch_size, blk_size // 2, 2), ALL)
    return jax.shard_map(
        per_device, mesh=inner, in_specs=in_specs, out_specs=out_specs, check_vma=False
    )
```

time: 2140 us -> 832 us (0.39)
  waiting for transfers between devices: 1040 us -> 267 us
  matrix products: 503 us -> 98.9 us
  blocking collectives: 314 us -> 67.7 us
  Pallas kernels: 0 us -> 160 us
  other arithmetic: 138 us -> 58.7 us
  starting transfers between devices: 2.44 us -> 39.1 us
    reduce_scatter x4 -> x1, waiting for transfers between devices: 664 us -> 11.6 us  [per_device(): second_own = lax.psum_scatter(second_grads, ALL, scatter_dimension=0)]
    dot_general x57 -> x2, matrix products: 383 us -> 1.01 us  [the longest x1 0.81 us: per_device(): lax.dot_general(hot_all, grad_pre, (((0,), (0,)), ((), ())), precision=la...]
    ppermute x44 -> x7, waiting for transfers between devices: 340 us -> 17.9 us  [the longest x5 11.8 us: total_sum(): lax.ppermute(value, axis, [(i, i ^ by) for i in range(size)])]
    all_to_all x0 -> x7, waiting for transfers between devices: none -> 216 us  [the longest x1 53.9 us: per_device(): heads = lax.all_to_all(heads, head_axes, 0, 0, tiled=True)]
    all_gather x7 -> x1, blocking collectives: 276 us -> 67.7 us  [per_device(): adapt_tok_all = lax.all_gather(grad_adapt_tok, ALL, axis=0, tiled=True)]
    pallas_call x0 -> x3, Pallas kernels: none -> 160 us  [the longest x1 80.1 us: attend_back(): pl.pallas_call(attend_back_kernel, grid_spec=pltpu.PrefetchScalarGridSpec...]
    reduce_sum x10 -> x7, other arithmetic: 75.9 us -> 6.47 us  [the longest x2 3.94 us: staged_sum(): value = jnp.sum(parts.astype(jnp.float32), axis=0)]
    while x133 -> x0, local copies, waits for them, and re-layouts: 56.8 us -> none
  transfers between devices with their start and end apart: 55 -> 17, of which waited for: 32 -> 13; matrix products, arithmetic and copies ran while one was open for 28% -> 14% of each run, Pallas kernels for 0% -> 19%
where the time goes in v1:
time: 832 us; the launch traced here: 824 us
  waiting for transfers between devices  267 us (32%)
  Pallas kernels  160 us (19%)
  local copies, waits for them, and re-layouts  110 us (13%)
  matrix products  98.9 us (12%)
  blocking collectives  67.7 us (8%)
  other arithmetic  58.7 us (7%)
  starting transfers between devices  39.1 us (5%)
  between operations  23.1 us (3%)
    pallas_call x1, Pallas kernels, attend_back(): pl.pallas_call(attend_back_kernel, grid_spec=pltpu.PrefetchScalarGridSpec...  80.1 us
    pallas_call x1, Pallas kernels, attend(): pl.pallas_call(attend_kernel, grid_spec=pltpu.PrefetchScalarGridSpec(num_...  69.8 us
    all_gather x1, blocking collectives, per_device(): adapt_tok_all = lax.all_gather(grad_adapt_tok, ALL, axis=0, tiled=True)  67.7 us
    all_to_all x1, waiting for transfers between devices, per_device(): heads = lax.all_to_all(heads, head_axes, 0, 0, tiled=True)  53.9 us
    all_to_all x1, waiting for transfers between devices, per_device(): lax.all_to_all(grad_heads.reshape(head_groups, 3, token_count, width), he...  50.4 us
    all_to_all x2, waiting for transfers between devices, staged_sum(): parts = lax.all_to_all(value.astype(low_type), axis, 0, 0, tiled=True)  49.8 us
    all_to_all x1, waiting for transfers between devices, per_device(): lax.all_to_all(product(cond_own, adaptive_low).reshape(devices, frame_loc...  47.7 us
    dot_general x7, matrix products, against(): lax.dot_general(left, right, (((1,), (1,)), ((), ())), preferred_element_...  34.7 us
  transfers between devices with their start and end apart: 17, of which 13 were waited for; matrix products, arithmetic and copies ran while one was open for 14% of the time, Pallas kernels for 19%

profile of v1, /device:TPU:0, one launch (start us, length us, event | category | flops | bytes accessed | tf_op | source)
XLA Modules:
  0.0 824.2 jit_solution(18115612415811447997)
XLA Ops:
  17.2 7.3 all-to-all-start
  27.9 47.7 %all-to-all-done = f32[32,2,6144]{2,1,0:T(2,128)S(1)} async-done(((f32[32,2,6144]{2,1,0:T(2,128)}), f32[32,2,6144]{2,1,0:T(2,128)S(1)}, u32[]{:S(2)}, u32[]{:S(2)}) %all-to-all-start) | async-done | bytes 1572896 | tf_op jit(solution)/shard_map/all_to_all | solution.py:635
  76.2 21.5 %all-gather.5.cloned.1.call-done.weight_ref = bf16[1024,3200]{1,0:T(8,128)(2,1)} async-done(((bf16[32,3200]{1,0:T(8,128)(2,1)}), bf16[1024,3200]{1,0:T(8,128)(2,1)}) %all-gather.5.cloned.1.call-update) | async-done | bytes 6553616 | tf_op jit(solution)/shard_map/all_gather | solution.py:603
  103.6 10.2 %triple_heads.1 = bf16[8,3,512,128]{3,2,1,0:T(8,128)(2,1)} custom-call(bf16[512,1024]{1,0:T(8,128)(2,1)S(1)} %get-tuple-element.238.normed_ref, bf16[1024,3200]{1,0:T(8,128)(2,1)S(1)} %copy-done.3, f32[2,1,128]{2,1,0:T(1,128)S(1)} %get-tuple-element.275.time_cos, f32[2,1,128]{2,1,0:T(1,128)S(1)} %get-tuple-element.274.time_sin, ...), custom_call_target="tpu_custom_call" | custom-call | tf_op jit(solution)/shard_map/triple_heads/pallas_call | solution.py:193
  119.3 53.9 %all-to-all-done.1 = bf16[8,3,512,128]{3,2,1,0:T(8,128)(2,1)S(1)} async-done(((bf16[8,3,512,128]{3,2,1,0:T(8,128)(2,1)}), bf16[8,3,512,128]{3,2,1,0:T(8,128)(2,1)S(1)}, u32[]{:S(2)}, u32[]{:S(2)}) %all-to-all-start.1) | async-done | bytes 3145760 | tf_op jit(solution)/shard_map/all_to_all | solution.py:688
  173.6 69.8 %attend.1 = (bf16[8,2,256,128]{3,2,1,0:T(8,128)(2,1)S(1)}, f32[16,128,256]{2,1,0:T(8,128)}, f32[16,1,512]{2,1,0:T(1,128)S(1)}) custom-call(s32[16]{0:T(128)S(1)} %select_reduce_fusion.1.order_ref, s32[16]{0:T(128)S(1)} %get-tuple-element.194.count_ref, bf16[8,2,256,128]{3,2,1,0:T(8,128)(2,1)S(1)} %get-tuple-element.253.query_ref, ...), custom_call_target="tpu_custom_call" | custom-call | tf_op jit(solution)/shard_map/attend/pallas_call | solution.py:290
  251.2 8.4 %slice.227 = bf16[32,128,1024]{2,1,0:T(8,128)(2,1)} slice(bf16[32,288,1024]{2,1,0:T(8,128)(2,1)} %bitcast.213), slice={[0:32], [160:288], [0:1024]} | slice | bytes 16777216 | tf_op jit(solution)/shard_map/slice | solution.py:704
  259.6 7.8 fusion.110
  276.4 13.0 %fusion.14 = (bf16[4096,512]{0,1:T(8,128)(2,1)}, f32[512,4096]{1,0:T(8,128)}) fusion(bf16[512,1024]{1,0:T(8,128)(2,1)S(1)} %get-tuple-element.234, bf16[1024,1024]{1,0:T(8,128)(2,1)S(1)} %bitcast.224, bf16[1024,1024]{1,0:T(8,128)(2,1)S(1)} %bitcast.227, bf16[1024,1024]{1,0:T(8,128)(2,1)} %bitcast.228, bf16[1024,1024]{1,0:T(8,128)(2,1)S(1)} %bitcast.222), kind=kOutput, calls=%fused_computation.18 | convolution fusion | flops 4347396096 | bytes 22020096 | tf_op jit(solution)/shard_map/dot_general | solution.py:35
  289.4 12.5 %fusion.106 = (f32[512]{0:T(512)S(1)}, f32[512,1024]{1,0:T(8,128)S(1)}, f32[512,1024]{1,0:T(8,128)}) fusion(f32[512,1024]{1,0:T(8,128)S(1)} %get-tuple-element.237, f32[2,1024]{1,0:T(2,128)S(1)} %get-tuple-element.262, bf16[4096,1024]{1,0:T(8,128)(2,1)} %bitcast.209, f32[512,4096]{1,0:T(8,128)} %get-tuple-element.291), kind=kOutput, calls=%fused_computation.269 | convolution fusion | flops 4315414016 | bytes 23078912 | tf_op jit(solution)/shard_map/dot_general | solution.py:35
  309.1 12.7 %fusion.6 = bf16[512,4096]{1,0:T(8,128)(2,1)} fusion(f32[512,4096]{1,0:T(8,128)} %get-tuple-element.291, bf16[512,1024]{1,0:T(8,128)(2,1)S(1)} %fusion.24, bf16[4096,1024]{1,0:T(8,128)(2,1)S(1)} %bitcast.212), kind=kOutput, calls=%fused_computation.10 | convolution fusion | flops 4336910336 | bytes 22020096 | tf_op jit(solution)/shard_map/dot_general | solution.py:45
  321.8 9.4 %multiply_reduce_fusion.1 = (f32[512]{0:T(512)S(1)}, f32[512,1024]{1,0:T(8,128)}) fusion(f32[512,1024]{1,0:T(8,128)S(1)} %get-tuple-element.237, f32[2,1024]{1,0:T(2,128)S(1)} %get-tuple-element.264, f32[512]{0:T(512)S(1)} %broadcast_multiply_fusion.2, bf16[512,4096]{1,0:T(8,128)(2,1)} %fusion.6, bf16[1024,1024]{1,0:T(8,128)(2,1)S(1)} %bitcast.225, ...), kind=kOutput, calls=%fused_computation.59 | convolution fusion | flops 4330618368 | bytes 16789504 | tf_op jit(solution)/shard_map/dot_general | solution.py:45
  331.2 8.2 fusion.117
  339.3 6.5 copy.176
  355.7 5.9 fusion.111
  361.5 5.0 convolution_dynamic-update-slice_fusion.1
  381.7 8.3 %convolution_dynamic-update-slice_fusion = f32[32,288,1024]{2,1,0:T(8,128)} fusion(f32[32,288,1024]{2,1,0:T(8,128)} %constant_dynamic-update-slice_fusion.6, bf16[32,128,512]{2,1,0:T(8,128)(2,1)S(1)} %bitcast.232, bf16[512,1024]{1,0:T(8,128)(2,1)S(1)} %copy-done.42), kind=kOutput, calls=%fused_computation.3 | convolution fusion | flops 4294967296 | bytes 22020096 | tf_op jit(solution)/shard_map/dot_general | solution.py:39
  400.2 13.9 %all-to-all-done.3 = bf16[8,512,128]{2,1,0:T(8,128)(2,1)} async-done(((bf16[8,512,128]{2,1,0:T(8,128)(2,1)}), bf16[8,512,128]{2,1,0:T(8,128)(2,1)}, u32[]{:S(2)}, u32[]{:S(2)}) %all-to-all-start.3) | async-done | bytes 1048608 | tf_op jit(solution)/shard_map/all_to_all | solution.py:759
  414.1 80.1 %attend_back.1 = (bf16[8,2,256,128]{3,2,1,0:T(8,128)(2,1)}, bf16[8,2,256,128]{3,2,1,0:T(8,128)(2,1)}, bf16[8,2,256,128]{3,2,1,0:T(8,128)(2,1)}) custom-call(s32[16]{0:T(128)} %select_reduce_fusion.order_ref, s32[16]{0:T(128)} %get-tuple-element.192.count_ref, bf16[8,2,256,128]{3,2,1,0:T(8,128)(2,1)} %copy-done.2, bf16[8,2,256,128]{3,2,1,0:T(8,128)(2,1)} %copy-done.1, ...), custom_call_target="tpu_custom_call" | custom-call | tf_op jit(solution)/shard_map/attend_back/pallas_call | solution.py:431
  510.7 50.4 %all-to-all-done.4 = bf16[8,3,512,128]{2,3,1,0:T(8,128)(2,1)} async-done(((bf16[8,3,512,128]{2,3,1,0:T(8,128)(2,1)}), bf16[8,3,512,128]{2,3,1,0:T(8,128)(2,1)}, u32[]{:S(2)}, u32[]{:S(2)}) %all-to-all-start.4) | async-done | bytes 3145760 | tf_op jit(solution)/shard_map/all_to_all | solution.py:782
  561.1 4.9 copy.167
  566.0 5.8 dot_general.85
  574.8 5.9 fusion.16
  585.0 6.6 fusion.116
  591.6 15.0 %concatenate.36 = f32[1024,3200]{1,0:T(8,128)} concatenate(f32[1024,3072]{1,0:T(8,128)} %fusion.116, f32[1024,16]{1,0:T(8,128)S(1)} %fusion.31, f32[1024,16]{1,0:T(8,128)S(1)} %copy-done.40, f32[1024,96]{1,0:T(8,128)S(1)} %broadcast_in_dim.240), dimensions={1} | concatenate | bytes 26214400 | tf_op jit(solution)/shard_map/concatenate | solution.py:792
  606.6 5.0 fusion.18
  611.7 6.1 collective-permute-done.1
  617.7 5.3 fusion.15
  633.1 49.8 %all-to-all-done.5 = bf16[4,4,32,3200]{3,2,1,0:T(8,128)(2,1)} async-done(((bf16[4,4,32,3200]{3,2,1,0:T(8,128)(2,1)}), bf16[4,4,32,3200]{3,2,1,0:T(8,128)(2,1)}, u32[]{:S(2)}, u32[]{:S(2)}) %all-to-all-start.5) | async-done | bytes 3276832 | tf_op jit(solution)/shard_map/all_to_all | solution.py:499
  686.7 5.3 all-to-all-start.6
  692.1 67.7 %all-gather.1 = bf16[32,2,6144]{2,1,0:T(2,128)(2,1)S(1)} all-gather(bf16[1,2,6144]{2,1,0:T(2,128)(2,1)S(1)} %bitcast.238), channel_id=1, replica_groups=mesh['batch'=4,'row'=4,'core'=2] {'batch','row','core'}, dimensions={0}, use_global_device_ids=true | all-gather | bytes 811008 | tf_op jit(solution)/shard_map/all_gather | solution.py:814
  767.1 11.6 %reduce-scatter.2.cloned.1.call-done = f32[1,288,1024]{2,1,0:T(8,128)} async-done(((f32[32,288,1024]{2,1,0:T(8,128)}), f32[1,288,1024]{2,1,0:T(8,128)}) %reduce-scatter.2.cloned.1.call-update) | async-done | bytes 1179664 | tf_op jit(solution)/shard_map/reduce_scatter | solution.py:751
  (345 shorter events, 159.6 us)
Async XLA Ops:
  7.2 90.4 %all-gather.5.cloned.1.call-start = ((), (), s32[]{:S(2)}) async-start(), calls=%async_computation.8 | async-start | bytes 6758400 | tf_op jit(solution)/shard_map/all_gather | solution.py:603
  10.9 240.3 %all-gather.7.cloned.1.call-start = ((), (), s32[]{:S(2)}) async-start(), calls=%async_computation.10 | async-start | bytes 19464192 | tf_op jit(solution)/shard_map/all_gather | solution.py:610
  17.2 58.4 %all-to-all-start = ((f32[32,2,6144]{2,1,0:T(2,128)}), f32[32,2,6144]{2,1,0:T(2,128)S(1)}, u32[]{:S(2)}, u32[]{:S(2)}) async-start(f32[32,2,6144]{2,1,0:T(2,128)} %reshape.770), calls=%async_computation | async-start | bytes 3145728 | tf_op jit(solution)/shard_map/all_to_all | solution.py:635
  24.6 3.3 collective-permute-start
  26.8 48.8 %copy-start.83 = (s32[2]{0:T(128)}, s32[2]{0:T(128)S(1)}, u32[]{:S(2)}) copy-start(s32[2]{0:T(128)S(1)} %get-tuple-element.297) | copy-start | bytes 28
  26.8 72.4 %copy-start.79 = (s32[1,2]{1,0:T(1,128)}, s32[1,2]{1,0:T(1,128)S(1)}, u32[]{:S(2)}) copy-start(s32[1,2]{1,0:T(1,128)S(1)} %get-tuple-element.231) | copy-start | bytes 28
  27.7 73.9 %copy-start.6 = (f32[256,128]{1,0:T(8,128)}, f32[256,128]{1,0:T(8,128)S(1)}, u32[]{:S(2)}) copy-start(f32[256,128]{1,0:T(8,128)S(1)} %get-tuple-element.270.space_sin) | copy-start | bytes 393220
  27.7 73.9 %copy-start.7 = (f32[256,128]{1,0:T(8,128)}, f32[256,128]{1,0:T(8,128)S(1)}, u32[]{:S(2)}) copy-start(f32[256,128]{1,0:T(8,128)S(1)} %get-tuple-element.271.space_cos) | copy-start | bytes 393220
  27.8 71.7 %copy-start.50 = (bf16[512,16]{0,1:T(8,128)(2,1)}, bf16[512,16]{0,1:T(8,128)(2,1)S(1)}, u32[]{:S(2)}) copy-start(bf16[512,16]{0,1:T(8,128)(2,1)S(1)} %select_convert_fusion) | copy-start | bytes 49156
  114.8 58.4 %all-to-all-start.1 = ((bf16[8,3,512,128]{3,2,1,0:T(8,128)(2,1)}), bf16[8,3,512,128]{3,2,1,0:T(8,128)(2,1)S(1)}, u32[]{:S(2)}, u32[]{:S(2)}) async-start(bf16[8,3,512,128]{3,2,1,0:T(8,128)(2,1)} %triple_heads.1), calls=%async_computation.1 | async-start | bytes 6291456 | tf_op jit(solution)/shard_map/all_to_all | solution.py:688
  173.6 73.7 %copy-start = (bf16[8,2,256,128]{3,2,1,0:T(8,128)(2,1)}, bf16[8,2,256,128]{3,2,1,0:T(8,128)(2,1)S(1)}, u32[]{:S(2)}) copy-start(bf16[8,2,256,128]{3,2,1,0:T(8,128)(2,1)S(1)} %get-tuple-element.251.value_ref) | copy-start | bytes 3145732
  173.6 73.7 %copy-start.1 = (bf16[8,2,256,128]{3,2,1,0:T(8,128)(2,1)}, bf16[8,2,256,128]{3,2,1,0:T(8,128)(2,1)S(1)}, u32[]{:S(2)}) copy-start(bf16[8,2,256,128]{3,2,1,0:T(8,128)(2,1)S(1)} %get-tuple-element.252.key_ref) | copy-start | bytes 3145732
  173.6 73.6 %copy-start.2 = (bf16[8,2,256,128]{3,2,1,0:T(8,128)(2,1)}, bf16[8,2,256,128]{3,2,1,0:T(8,128)(2,1)S(1)}, u32[]{:S(2)}) copy-start(bf16[8,2,256,128]{3,2,1,0:T(8,128)(2,1)S(1)} %get-tuple-element.253.query_ref) | copy-start | bytes 3145732
  247.3 20.1 %all-to-all-start.2 = ((bf16[8,512,128]{1,2,0:T(8,128)(2,1)}), bf16[8,512,128]{1,2,0:T(8,128)(2,1)S(1)}, u32[]{:S(2)}, u32[]{:S(2)}) async-start(bf16[8,512,128]{1,2,0:T(8,128)(2,1)} %copy.160), calls=%async_computation.2 | async-start | bytes 2097152 | tf_op jit(solution)/shard_map/all_to_all | solution.py:697
  250.8 527.9 %reduce-scatter.2.cloned.1.call-start = ((), (), s32[]{:S(2)}) async-start(), calls=%async_computation.9 | async-start | bytes 38928384 | tf_op jit(solution)/shard_map/reduce_scatter | solution.py:751
  272.0 49.8 %copy-start.12 = (f32[512,1024]{1,0:T(8,128)}, f32[512,1024]{1,0:T(8,128)S(1)}, u32[]{:S(2)}) copy-start(f32[512,1024]{1,0:T(8,128)S(1)} %get-tuple-element.237) | copy-start | bytes 6291460
  394.4 19.7 %all-to-all-start.3 = ((bf16[8,512,128]{2,1,0:T(8,128)(2,1)}), bf16[8,512,128]{2,1,0:T(8,128)(2,1)}, u32[]{:S(2)}, u32[]{:S(2)}) async-start(bf16[8,512,128]{2,1,0:T(8,128)(2,1)} %bitcast.233), calls=%async_computation.3 | async-start | bytes 2097152 | tf_op jit(solution)/shard_map/all_to_all | solution.py:759
  505.0 56.1 %all-to-all-start.4 = ((bf16[8,3,512,128]{2,3,1,0:T(8,128)(2,1)}), bf16[8,3,512,128]{2,3,1,0:T(8,128)(2,1)}, u32[]{:S(2)}, u32[]{:S(2)}) async-start(bf16[8,3,512,128]{2,3,1,0:T(8,128)(2,1)} %pad_maximum_fusion.1), calls=%async_computation.4 | async-start | bytes 6291456 | tf_op jit(solution)/shard_map/all_to_all | solution.py:782
  611.6 6.1 collective-permute-start.1
  623.0 59.8 %all-to-all-start.5 = ((bf16[4,4,32,3200]{3,2,1,0:T(8,128)(2,1)}), bf16[4,4,32,3200]{3,2,1,0:T(8,128)(2,1)}, u32[]{:S(2)}, u32[]{:S(2)}) async-start(bf16[4,4,32,3200]{3,2,1,0:T(8,128)(2,1)} %fusion.15), calls=%async_computation.5 | async-start | bytes 6553600 | tf_op jit(solution)/shard_map/all_to_all | solution.py:499
  686.7 73.4 %copy-start.33 = (f32[32,6144]{1,0:T(8,128)S(1)}, f32[32,6144]{1,0:T(8,128)}, u32[]{:S(2)}) copy-start(f32[32,6144]{1,0:T(8,128)} %param.46) | copy-start | bytes 2359300
  686.7 75.6 %all-to-all-start.6 = ((bf16[4,32,3200]{2,1,0:T(8,128)(2,1)}), bf16[4,32,3200]{2,1,0:T(8,128)(2,1)S(1)}, u32[]{:S(2)}, u32[]{:S(2)}) async-start(bf16[4,32,3200]{2,1,0:T(8,128)(2,1)} %reduce_sum.425), calls=%async_computation.6 | async-start | bytes 1638400 | tf_op jit(solution)/shard_map/all_to_all | solution.py:499
  692.0 68.4 %copy-start.57 = (f32[64,32]{0,1:T(8,128)S(1)}, f32[64,32]{0,1:T(8,128)}, u32[]{:S(2)}) copy-start(f32[64,32]{0,1:T(8,128)} %copy-done.56) | copy-start | bytes 24580
  692.0 68.4 %copy-start.82 = (s32[64]{0:T(128)S(1)}, s32[64]{0:T(128)}, u32[]{:S(2)}) copy-start(s32[64]{0:T(128)} %copy-done.81) | copy-start | bytes 772
  762.2 43.3 %copy-start.61 = (f32[16,32]{1,0:T(8,128)S(1)}, f32[16,32]{1,0:T(8,128)}, u32[]{:S(2)}) copy-start(f32[16,32]{1,0:T(8,128)} %param.40) | copy-start | bytes 6148
  762.3 43.3 %copy-start.74 = (f32[16,32]{1,0:T(8,128)S(1)}, f32[16,32]{1,0:T(8,128)}, u32[]{:S(2)}) copy-start(f32[16,32]{1,0:T(8,128)} %param.42) | copy-start | bytes 6148
  762.3 43.3 %copy-start.75 = (f32[16,32]{1,0:T(8,128)S(1)}, f32[16,32]{1,0:T(8,128)}, u32[]{:S(2)}) copy-start(f32[16,32]{1,0:T(8,128)} %param.41) | copy-start | bytes 6148
  786.5 1.2 collective-permute-start.2
  787.7 3.6 collective-permute-start.3
  791.3 3.6 collective-permute-start.4
  795.0 3.6 collective-permute-start.5
  798.6 4.5 collective-permute-start.6
  (72 other events, 446.3 us)
Sparse Core Ops, SparseCore 0:
  11.5 86.1 all-gather.4
  101.3 141.1 all-gather.6
  390.2 388.4 reduce-scatter.1

commit v2 on v1

--- a/solution.py
+++ b/solution.py
@@ -74,20 +74,6 @@
 def modulate(hidden, shift, scale):
     normed = layer_norm(hidden).reshape(shift.shape[0], -1, hidden.shape[-1])
     return (normed * (1.0 + scale[:, None]) + shift[:, None]).reshape(hidden.shape)
-
-
-def per_frame(gate, hidden):
-    return (hidden.reshape(gate.shape[0], -1, hidden.shape[-1]) * gate[:, None]).reshape(
-        hidden.shape
-    )
-
-
-def frame_sum(gate, hidden):
-    return jnp.sum(hidden.reshape(gate.shape[0], -1, hidden.shape[-1]), axis=1)
-
-
-def gelu_tanh(value):
-    return jax.nn.gelu(value, approximate=True)
 
 
 def adamw_update(master, first_moment, second_moment, gradient, factor, step_rate):
@@ -158,9 +144,12 @@
 
     def store(piece, values):
         for part in range(LANES // width):
-            out_ref[piece * (LANES // width) + part, 0] = values[
-                :, part * width : (part + 1) * width
-            ].astype(low_type)
+            place = piece * (LANES // width) + part
+            done = values[:, part * width : (part + 1) * width].astype(low_type)
+            if len(out_ref.shape) == 3:
+                out_ref[place] = done
+            else:
+                out_ref[place, 0] = done
 
     turned = column < 2 * D // acc.shape[1]
 
@@ -190,6 +179,16 @@
     block = 256
     per_block = block // width
     per_part = D // block
+    if width == LANES:
+        out_specs = pl.BlockSpec(
+            (per_block, tokens, width), lambda j: (j % per_part, 0, j // per_part)
+        )
+        out_shape = jax.ShapeDtypeStruct((groups, tokens, 3 * width), low_type)
+    else:
+        out_specs = pl.BlockSpec(
+            (per_block, 1, tokens, width), lambda j: (j % per_part, j // per_part, 0, 0)
+        )
+        out_shape = jax.ShapeDtypeStruct((groups, 3, tokens, width), low_type)
     return pl.pallas_call(
         triple_kernel,
         grid=(3 * D // block,),
@@ -201,11 +200,10 @@
             pl.BlockSpec(spaces[0].shape, lambda j: (0, 0)),
             pl.BlockSpec(spaces[1].shape, lambda j: (0, 0)),
         ],
-        out_specs=pl.BlockSpec(
-            (per_block, 1, tokens, width), lambda j: (j % per_part, j // per_part, 0, 0)
-        ),
-        out_shape=jax.ShapeDtypeStruct((groups, 3, tokens, width), low_type),
+        out_specs=out_specs,
+        out_shape=out_shape,
         compiler_params=pltpu.CompilerParams(vmem_limit_bytes=32 * 1024 * 1024),
+        cost_estimate=about(10),
         name="triple_heads",
     )(normed, weight, *times, *spaces)
 
@@ -221,8 +219,31 @@
     )
 
 
+UNROLL = 4
+
+
+def unrolled(count, body, carry):
+    def several(base, now):
+        for offset in range(UNROLL):
+            now = body(base * UNROLL + offset, now)
+        return now
+
+    whole_part = count // UNROLL
+    carry = lax.fori_loop(0, whole_part, several, carry)
+    return lax.fori_loop(whole_part * UNROLL, count, body, carry)
+
+
 def attend_kernel(
-    order_ref, count_ref, query_ref, key_ref, value_ref, out_ref, flat_ref, log_ref, turned_ref
+    order_ref,
+    count_ref,
+    query_ref,
+    key_ref,
+    value_ref,
+    out_ref,
+    flat_ref,
+    log_ref,
+    turned_ref,
+    scores_ref,
 ):
     step = pl.program_id(0)
     chunks, per_chunk = key_ref.shape[0], key_ref.shape[1]
@@ -239,33 +260,45 @@
 
         lax.fori_loop(0, chunks, turn, 0)
 
-    queries = head_stack(query_ref[...] * jnp.asarray(HEAD_DIM**-0.5, low_type))
-
-    def visit(place, carry):
-        top, total, sums = carry
+    queries = jnp.transpose(head_stack(query_ref[...] * jnp.asarray(HEAD_DIM**-0.5, low_type)))
+    count = count_ref[step]
+
+    def by_eight(value):
+        return value.reshape(FRAME_TOK // 8, 8, span)
+
+    def score(place, top):
         frame = order_ref[place]
-        chunk, part = frame // per_chunk, frame % per_chunk
-        scores = against(key_ref[chunk, part], queries)
-        new_top = jnp.maximum(top, jnp.max(scores, axis=0, keepdims=True))
-        rescale = jnp.exp(top - new_top)
-        chances = jnp.exp(scores - new_top)
-        total = total * rescale + jnp.sum(chances, axis=0, keepdims=True)
+        scores = product(key_ref[frame // per_chunk, frame % per_chunk], queries)
+        scores_ref[place] = scores
+        return jnp.maximum(top, jnp.max(by_eight(scores), axis=0))
+
+    top = unrolled(count, score, jnp.full((8, span), -1e30, jnp.float32))
+    top = jnp.max(top, axis=0, keepdims=True)
+
+    def weigh(place, carry):
+        total, sums = carry
+        frame = order_ref[place]
+        chances = jnp.exp(scores_ref[place] - top)
+        total = total + jnp.sum(by_eight(chances), axis=0)
         chances = chances.astype(low_type)
         new_sums = []
         for head in range(heads):
+            values = turned_ref[
+                frame // per_chunk,
+                frame % per_chunk,
+                head * HEAD_DIM : (head + 1) * HEAD_DIM,
+                :,
+            ]
             columns = slice(head * FRAME_TOK, (head + 1) * FRAME_TOK)
-            values = turned_ref[chunk, part, head * HEAD_DIM : (head + 1) * HEAD_DIM, :]
-            new_sums.append(
-                sums[head] * rescale[:, columns] + product(values, chances[:, columns])
-            )
-        return new_top, total, tuple(new_sums)
+            new_sums.append(sums[head] + product(values, chances[:, columns]))
+        return total, tuple(new_sums)
 
     initial = (
-        jnp.full((1, span), -1e30, jnp.float32),
-        jnp.zeros((1, span), jnp.float32),
+        jnp.zeros((8, span), jnp.float32),
         tuple(jnp.zeros((HEAD_DIM, FRAME_TOK), jnp.float32) for _ in range(heads)),
     )
-    top, total, sums = lax.fori_loop(0, count_ref[step], visit, initial)
+    total, sums = unrolled(count, weigh, initial)
+    total = jnp.sum(total, axis=0, keepdims=True)
     log_ref[...] = top + jnp.log(total)
     inverse = 1.0 / total
     result = jnp.concatenate(
@@ -279,14 +312,27 @@
     out_ref[...] = jnp.transpose(result).astype(low_type)
 
 
+def about(microseconds):
+    return pl.CostEstimate(
+        flops=microseconds * 1_100_000_000, bytes_accessed=1 << 20, transcendentals=0
+    )
+
+
 def whole(shape):
     return pl.BlockSpec(shape, lambda *_: (0,) * len(shape))
 
 
-def attend(order, count, queries, keys, values):
-    chunks, per_chunk, _, width = queries.shape
+def lanes_of(items, width):
+    joint = items[0].shape[-1] != width
+    return [place if joint else 0 for place in range(3)]
+
+
+def attend(order, count, items, width):
+    chunks, per_chunk = items[0].shape[:2]
+    key_chunks = items[1].shape[0]
     frames = chunks * per_chunk
     span = width // HEAD_DIM * FRAME_TOK
+    lane = lanes_of(items, width)
     return pl.pallas_call(
         attend_kernel,
         grid_spec=pltpu.PrefetchScalarGridSpec(
@@ -295,10 +341,14 @@
             in_specs=[
                 pl.BlockSpec(
                     (None, None, FRAME_TOK, width),
-                    lambda i, *_: (i // per_chunk, i % per_chunk, 0, 0),
+                    lambda i, *_: (i // per_chunk, i % per_chunk, 0, lane[0]),
                 ),
-                whole(keys.shape),
-                whole(values.shape),
+                pl.BlockSpec(
+                    (key_chunks, per_chunk, FRAME_TOK, width), lambda i, *_: (0, 0, 0, lane[1])
+                ),
+                pl.BlockSpec(
+                    (key_chunks, per_chunk, FRAME_TOK, width), lambda i, *_: (0, 0, 0, lane[2])
+                ),
             ],
             out_specs=[
                 pl.BlockSpec(
@@ -309,17 +359,19 @@
                 pl.BlockSpec((None, 1, span), lambda i, *_: (i, 0, 0)),
             ],
             scratch_shapes=[
-                pltpu.VMEM((keys.shape[0], per_chunk, width, FRAME_TOK), low_type),
+                pltpu.VMEM((key_chunks, per_chunk, width, FRAME_TOK), low_type),
+                pltpu.VMEM((key_chunks * per_chunk, FRAME_TOK, span), jnp.float32),
             ],
         ),
         out_shape=[
-            jax.ShapeDtypeStruct(queries.shape, low_type),
+            jax.ShapeDtypeStruct((chunks, per_chunk, FRAME_TOK, width), low_type),
             jax.ShapeDtypeStruct((frames, width, FRAME_TOK), jnp.float32),
             jax.ShapeDtypeStruct((frames, 1, span), jnp.float32),
         ],
         compiler_params=pltpu.CompilerParams(vmem_limit_bytes=48 * 1024 * 1024),
+        cost_estimate=about(45),
         name="attend",
-    )(order, count, queries, keys, values)
+    )(order, count, *items)
 
 
 def attend_back_kernel(
@@ -337,14 +389,9 @@
     key_sin,
     space_cos,
     space_sin,
-    grad_query_ref,
-    grad_key_ref,
-    grad_value_ref,
-    stacked_query,
-    stacked_grad,
-    row_dot,
-    sums_ref,
+    *rest,
 ):
+    outs, (stacked_query, stacked_grad, row_dot, sums_ref) = rest[:-4], rest[-4:]
     step = pl.program_id(0)
     frames, width, _ = flat_ref.shape
     per_chunk = query_ref.shape[1]
@@ -376,67 +423,101 @@
     values = value_ref[...]
     turned_keys = jnp.transpose(keys)
 
-    def visit(place, carry):
+    def several(base, count, carry):
         grad_keys, grad_values = carry
-        frame = order_ref[place]
-        queries = stacked_query[frame]
-        grads = stacked_grad[frame]
-        scores = against(keys, queries)
-        chances = jnp.exp(scores - log_ref[frame])
-        grad_chances = against(values, grads)
-        grad_scores = (chances * (grad_chances - row_dot[frame])).astype(low_type)
-        grad_values = grad_values + product(chances.astype(low_type), grads)
-        grad_keys = grad_keys + product(grad_scores, queries)
-        for head in range(heads):
-            rows = slice(head * HEAD_DIM, (head + 1) * HEAD_DIM)
-            sums_ref[frame, rows, :] += product(
-                turned_keys[rows], grad_scores[:, head * FRAME_TOK : (head + 1) * FRAME_TOK]
-            )
+        frames_now = [order_ref[base + i] for i in range(count)]
+        updates = []
+        scores = [against(keys, stacked_query[frame]) for frame in frames_now]
+        grad_chances = [against(values, stacked_grad[frame]) for frame in frames_now]
+        for frame, score, grad_chance in zip(frames_now, scores, grad_chances):
+            chances = jnp.exp(score - log_ref[frame])
+            grad_scores = (chances * (grad_chance - row_dot[frame])).astype(low_type)
+            grad_values = grad_values + product(chances.astype(low_type), stacked_grad[frame])
+            grad_keys = grad_keys + product(grad_scores, stacked_query[frame])
+            for head in range(heads):
+                rows = slice(head * HEAD_DIM, (head + 1) * HEAD_DIM)
+                updates.append(
+                    product(
+                        turned_keys[rows],
+                        grad_scores[:, head * FRAME_TOK : (head + 1) * FRAME_TOK],
+                    )
+                )
+        for i, frame in enumerate(frames_now):
+            for head in range(heads):
+                rows = slice(head * HEAD_DIM, (head + 1) * HEAD_DIM)
+                sums_ref[frame, rows, :] += updates[i * heads + head]
         return grad_keys, grad_values
 
     zero = jnp.zeros((FRAME_TOK, width), jnp.float32)
-    grad_keys, grad_values = lax.fori_loop(0, count_ref[step], visit, (zero, zero))
+    total = count_ref[step]
+    carry = lax.fori_loop(
+        0, total // UNROLL, lambda i, c: several(i * UNROLL, UNROLL, c), (zero, zero)
+    )
+    grad_keys, grad_values = lax.fori_loop(
+        total // UNROLL * UNROLL, total, lambda i, c: several(i, 1, c), carry
+    )
     space_c, space_s = space_cos[:, :width], space_sin[:, :width]
-    grad_value_ref[...] = grad_values.astype(low_type)
-    grad_key_ref[...] = (
-        grad_keys * (key_cos[:, :width] + space_c)
-        - partner(grad_keys) * (key_sin[:, :width] + space_s)
-    ).astype(low_type)
+
+    def store(part, frame, value):
+        place = (frame // per_chunk, frame % per_chunk)
+        if len(outs) == 1:
+            outs[0][place + (slice(None), slice(part * width, (part + 1) * width))] = value
+        else:
+            outs[part][place] = value
+
+    store(2, step, grad_values.astype(low_type))
+    store(
+        1,
+        step,
+        (
+            grad_keys * (key_cos[:, :width] + space_c)
+            - partner(grad_keys) * (key_sin[:, :width] + space_s)
+        ).astype(low_type),
+    )
 
     @pl.when(step == pl.num_programs(0) - 1)
     def _():
         def finish(frame, carry):
-            chunk, part = frame // per_chunk, frame % per_chunk
             value = jnp.transpose(sums_ref[frame]) * scale
-            grad_query_ref[chunk, part] = (
-                value * (query_cos[frame][:, :width] + space_c)
-                - partner(value) * (query_sin[frame][:, :width] + space_s)
-            ).astype(low_type)
+            store(
+                0,
+                frame,
+                (
+                    value * (query_cos[frame][:, :width] + space_c)
+                    - partner(value) * (query_sin[frame][:, :width] + space_s)
+                ).astype(low_type),
+            )
             return carry
 
         lax.fori_loop(0, frames, finish, 0)
 
 
-def attend_back(
-    order, count, queries, keys, values, grads, flat, logs, query_times, key_times, spaces
-):
-    per_chunk, width = queries.shape[1], queries.shape[3]
+def attend_back(order, count, items, grads, flat, logs, query_times, key_times, spaces):
+    per_chunk, width = grads.shape[1], grads.shape[3]
     frames = flat.shape[0]
-    key_frames = keys.shape[0] * per_chunk
+    key_frames = items[1].shape[0] * per_chunk
     span = width // HEAD_DIM * FRAME_TOK
-    key_spec = pl.BlockSpec(
-        (None, None, FRAME_TOK, width), lambda i, *_: (i // per_chunk, i % per_chunk, 0, 0)
-    )
+    lane = lanes_of(items, width)
+
+    def key_spec(place):
+        return pl.BlockSpec(
+            (None, None, FRAME_TOK, width), lambda i, *_: (i // per_chunk, i % per_chunk, 0, place)
+        )
+
     key_time = pl.BlockSpec((None, 1, LANES), lambda i, *_: (i, 0, 0))
+    if lane[1]:
+        shapes = [items[0].shape]
+    else:
+        shapes = [item.shape for item in items]
     return pl.pallas_call(
         attend_back_kernel,
         grid_spec=pltpu.PrefetchScalarGridSpec(
             num_scalar_prefetch=2,
             grid=(key_frames,),
             in_specs=[
-                whole(queries.shape),
-                key_spec,
-                key_spec,
+                whole(grads.shape),
+                key_spec(lane[1]),
+                key_spec(lane[2]),
                 whole(grads.shape),
                 whole(flat.shape),
                 whole(logs.shape),
@@ -447,7 +528,7 @@
                 whole(spaces[0].shape),
                 whole(spaces[1].shape),
             ],
-            out_specs=[whole(queries.shape), key_spec, key_spec],
+            out_specs=[whole(shape) for shape in shapes],
             scratch_shapes=[
                 pltpu.VMEM((frames, span, width), low_type),
                 pltpu.VMEM((frames, span, width), low_type),
@@ -455,50 +536,383 @@
                 pltpu.VMEM((frames, width, FRAME_TOK), jnp.float32),
             ],
         ),
+        out_shape=[jax.ShapeDtypeStruct(shape, low_type) for shape in shapes],
+        compiler_params=pltpu.CompilerParams(vmem_limit_bytes=56 * 1024 * 1024),
+        cost_estimate=about(65),
+        name="attend_back",
+    )(order, count, *items, grads, flat, logs, *query_times, *key_times, *spaces)
+
+
+def norm_parts(hidden):
+    centred = hidden - jnp.mean(hidden, axis=-1, keepdims=True)
+    variance = jnp.mean(centred * centred, axis=-1, keepdims=True)
+    inverse = lax.rsqrt(variance + 1e-06)
+    return centred * inverse, inverse
+
+
+def norm_back(normed, inverse, grad):
+    along = jnp.mean(grad * normed, axis=-1, keepdims=True)
+    return inverse * (grad - jnp.mean(grad, axis=-1, keepdims=True) - normed * along)
+
+
+def row_sum(value):
+    return jnp.sum(value, axis=0, keepdims=True)
+
+
+def flat_weight(ref):
+    return ref[...].reshape(-1, ref.shape[-1])
+
+
+def project_kernel(
+    heads_ref, weight_ref, hidden_ref, mods_ref, attended_ref, branch_ref, next_ref, mixed_ref
+):
+    attended = jnp.concatenate([heads_ref[group] for group in range(heads_ref.shape[0])], axis=1)
+    attended_ref[...] = attended
+    branch = product(attended, flat_weight(weight_ref))
+    branch_ref[...] = branch
+    hidden = hidden_ref[...] + mods_ref[2:3] * branch
+    next_ref[...] = hidden
+    normed, _ = norm_parts(hidden)
+    mixed_ref[...] = (normed * (1.0 + mods_ref[4:5]) + mods_ref[3:4]).astype(low_type)
+
+
+def project_norm(heads, weights, hidden, mods):
+    groups, tokens, width = heads.shape
+    devices, height, _ = weights.shape
+    rows = D // devices
+    by_frame = pl.BlockSpec((FRAME_TOK, D), lambda i: (i, 0))
+    wide = jax.ShapeDtypeStruct((tokens, D), jnp.float32)
+    low = jax.ShapeDtypeStruct((tokens, D), low_type)
+    return pl.pallas_call(
+        project_kernel,
+        grid=(tokens // FRAME_TOK,),
+        in_specs=[
+            pl.BlockSpec((groups, FRAME_TOK, width), lambda i: (0, i, 0)),
+            pl.BlockSpec((devices, rows, D), lambda i: (0, FF // D, 0)),
+            by_frame,
+            pl.BlockSpec((None, 6, D), lambda i: (i, 0, 0)),
+        ],
+        out_specs=[by_frame] * 4,
+        out_shape=[low, wide, wide, low],
+        compiler_params=pltpu.CompilerParams(vmem_limit_bytes=40 * 1024 * 1024),
+        cost_estimate=about(4),
+        name="project_norm",
+    )(heads, weights, hidden, mods)
+
+
+GELU_OUT = math.sqrt(2.0 / math.pi)
+GELU_CUBE = 0.044715
+
+
+def forward_kernel(
+    scale_ref,
+    mixed_ref,
+    expand_ref,
+    reduce_ref,
+    hidden_ref,
+    mods_ref,
+    readout_ref,
+    noise_ref,
+    inner_ref,
+    active_ref,
+    grad_hidden_ref,
+    grad_outer_ref,
+    grad_readout_ref,
+    grad_gate_ref,
+    loss_ref,
+    outer_ref,
+):
+    step = pl.program_id(0)
+    frames = mods_ref.shape[0]
+    inner = product(mixed_ref[...], flat_weight(expand_ref))
+    inner_ref[...] = inner
+    bend = jnp.tanh(GELU_OUT * (inner + GELU_CUBE * (inner * inner * inner)))
+    active = (0.5 * inner * (1.0 + bend)).astype(low_type)
+    active_ref[...] = active
+    part = product(active, flat_weight(reduce_ref))
+
+    @pl.when(step == 0)
+    def _():
+        outer_ref[...] = part
+
+    @pl.when(step > 0)
+    def _():
+        outer_ref[...] += part
+
+    @pl.when(step == pl.num_programs(0) - 1)
+    def _():
+        readout = readout_ref[...][:, PATCH_FEAT : 2 * PATCH_FEAT]
+        grad_readout = jnp.zeros((D, PATCH_FEAT), jnp.float32)
+        for frame in range(frames):
+            tokens = slice(frame * FRAME_TOK, (frame + 1) * FRAME_TOK)
+            outer = outer_ref[tokens]
+            gate = mods_ref[frame, 5:6]
+            final, inverse = norm_parts(hidden_ref[tokens] + gate * outer)
+            final_low = final.astype(low_type)
+            residue = product(final_low, readout) - noise_ref[tokens]
+            loss_ref[frame] = jnp.zeros((1, LANES), jnp.float32) + jnp.sum(residue * residue)
+            grad_pred = (residue * scale_ref[frame]).astype(low_type)
+            grad_readout += across(final_low, grad_pred)
+            grad_hidden = norm_back(final, inverse, against(grad_pred, readout))
+            grad_hidden_ref[tokens] = grad_hidden
+            grad_outer_ref[tokens] = (gate * grad_hidden).astype(low_type)
+            grad_gate_ref[frame] = row_sum(grad_hidden * outer)
+        grad_readout_ref[...] = grad_readout
+
+
+def feed_forward(loss_scale, mixed, weights, hidden, mods, first_weights, noise):
+    tokens = mixed.shape[0]
+    devices, height, _ = weights.shape
+    rows = D // devices
+    frames = mods.shape[0]
+    pieces = FF // D
+    wide = jax.ShapeDtypeStruct((tokens, D), jnp.float32)
+    by_piece = pl.BlockSpec((tokens, D), lambda k, *_: (0, k))
+    return pl.pallas_call(
+        forward_kernel,
+        grid_spec=pltpu.PrefetchScalarGridSpec(
+            num_scalar_prefetch=1,
+            grid=(pieces,),
+            in_specs=[
+                whole((tokens, D)),
+                pl.BlockSpec((devices, rows, D), lambda k, *_: (0, pieces + 1 + k, 0)),
+                pl.BlockSpec((devices // pieces, pieces * rows, D), lambda k, *_: (k, 0, 0)),
+                whole((tokens, D)),
+                whole(mods.shape),
+                pl.BlockSpec((D, LANES), lambda k, *_: (0, 3 * D // LANES)),
+                whole((tokens, PATCH_FEAT)),
+            ],
+            out_specs=[
+                by_piece,
+                by_piece,
+                whole((tokens, D)),
+                whole((tokens, D)),
+                whole((D, PATCH_FEAT)),
+                whole((frames, 1, D)),
+                whole((frames, 1, LANES)),
+            ],
+            scratch_shapes=[pltpu.VMEM((tokens, D), jnp.float32)],
+        ),
         out_shape=[
-            jax.ShapeDtypeStruct(queries.shape, low_type),
-            jax.ShapeDtypeStruct(keys.shape, low_type),
-            jax.ShapeDtypeStruct(keys.shape, low_type),
+            jax.ShapeDtypeStruct((tokens, FF), jnp.float32),
+            jax.ShapeDtypeStruct((tokens, FF), low_type),
+            wide,
+            jax.ShapeDtypeStruct((tokens, D), low_type),
+            jax.ShapeDtypeStruct((D, PATCH_FEAT), jnp.float32),
+            jax.ShapeDtypeStruct((frames, 1, D), jnp.float32),
+            jax.ShapeDtypeStruct((frames, 1, LANES), jnp.float32),
         ],
         compiler_params=pltpu.CompilerParams(vmem_limit_bytes=56 * 1024 * 1024),
-        name="attend_back",
-    )(
-        order,
-        count,
-        queries,
-        keys,
-        values,
-        grads,
-        flat,
-        logs,
-        *query_times,
-        *key_times,
-        *spaces,
-    )
+        cost_estimate=about(20),
+        name="feed_forward",
+    )(loss_scale, mixed, weights, weights, hidden, mods, first_weights, noise)
+
+
+def backward_kernel(
+    grad_outer_ref,
+    reduce_ref,
+    expand_ref,
+    inner_ref,
+    hidden_ref,
+    grad_hidden_ref,
+    branch_ref,
+    mods_ref,
+    project_ref,
+    grad_inner_ref,
+    grad_one_ref,
+    grad_branch_ref,
+    heads_ref,
+    grad_mods_ref,
+    grad_mixed_ref,
+):
+    step = pl.program_id(0)
+    frames = mods_ref.shape[0]
+    groups, _, width = heads_ref.shape
+    inner = inner_ref[...]
+    square = inner * inner
+    bend = jnp.tanh(GELU_OUT * (inner + GELU_CUBE * (square * inner)))
+    slope = 0.5 * (1.0 + bend) + 0.5 * inner * (1.0 - bend * bend) * (
+        GELU_OUT * (1.0 + 3.0 * GELU_CUBE * square)
+    )
+    grad_active = against(grad_outer_ref[...], flat_weight(reduce_ref))
+    grad_inner = (grad_active * slope).astype(low_type)
+    grad_inner_ref[...] = grad_inner
+    part = against(grad_inner, flat_weight(expand_ref))
+
+    @pl.when(step == 0)
+    def _():
+        grad_mixed_ref[...] = part
+
+    @pl.when(step > 0)
+    def _():
+        grad_mixed_ref[...] += part
+
+    @pl.when(step == pl.num_programs(0) - 1)
+    def _():
+        project = flat_weight(project_ref)
+        for frame in range(frames):
+            tokens = slice(frame * FRAME_TOK, (frame + 1) * FRAME_TOK)
+            normed, inverse = norm_parts(hidden_ref[tokens])
+            grad_mixed = grad_mixed_ref[tokens]
+            grad_mods_ref[frame, 1:2] = row_sum(grad_mixed)
+            grad_mods_ref[frame, 2:3] = row_sum(grad_mixed * normed)
+            grad_one = grad_hidden_ref[tokens] + norm_back(
+                normed, inverse, grad_mixed * (1.0 + mods_ref[frame, 4:5])
+            )
+            grad_one_ref[tokens] = grad_one
+            grad_mods_ref[frame, 0:1] = row_sum(grad_one * branch_ref[tokens])
+            grad_branch = (mods_ref[frame, 2:3] * grad_one).astype(low_type)
+            grad_branch_ref[tokens] = grad_branch
+            grad_attended = against(grad_branch, project).astype(low_type)
+            for group in range(groups):
+                heads_ref[group, tokens] = grad_attended[:, group * width : (group + 1) * width]
+
+
+def feed_backward(grad_outer, weights, inner, hidden, grad_hidden, branch, mods, groups):
+    tokens = hidden.shape[0]
+    devices, height, _ = weights.shape
+    rows = D // devices
+    frames = mods.shape[0]
+    pieces = FF // D
+    by_piece = pl.BlockSpec((tokens, D), lambda k: (0, k))
+    return pl.pallas_call(
+        backward_kernel,
+        grid=(pieces,),
+        in_specs=[
+            whole((tokens, D)),
+            pl.BlockSpec((devices // pieces, pieces * rows, D), lambda k: (k, 0, 0)),
+            pl.BlockSpec((devices, rows, D), lambda k: (0, pieces + 1 + k, 0)),
+            by_piece,
+            whole((tokens, D)),
+            whole((tokens, D)),
+            whole((tokens, D)),
+            whole(mods.shape),
+            pl.BlockSpec((devices, rows, D), lambda k: (0, pieces, 0)),
+        ],
+        out_specs=[
+            by_piece,
+            whole((tokens, D)),
+            whole((tokens, D)),
+            whole((groups, tokens, D // groups)),
+            whole((frames, 3, D)),
+        ],
+        out_shape=[
+            jax.ShapeDtypeStruct((tokens, FF), low_type),
+            jax.ShapeDtypeStruct((tokens, D), jnp.float32),
+            jax.ShapeDtypeStruct((tokens, D), low_type),
+            jax.ShapeDtypeStruct((groups, tokens, D // groups), low_type),
+            jax.ShapeDtypeStruct((frames, 3, D), jnp.float32),
+        ],
+        scratch_shapes=[pltpu.VMEM((tokens, D), jnp.float32)],
+        compiler_params=pltpu.CompilerParams(vmem_limit_bytes=58 * 1024 * 1024),
+        cost_estimate=about(22),
+        name="feed_backward",
+    )(grad_outer, weights, weights, inner, hidden, grad_hidden, branch, mods, weights)
+
+
+def grads_kernel(
+    active_ref, grad_outer_ref, attended_ref, grad_branch_ref, mixed_ref, grad_inner_ref, out_ref
+):
+    cores, lines, height, _ = out_ref.shape
+    pieces = FF // D
+    rows = height // (2 * pieces + 1)
+
+    def store(start, count, value):
+        value = value.astype(low_type)
+        for line in range(lines):
+            for core in range(cores):
+                at = (line * cores + core) * count
+                out_ref[core, line, start : start + count] = value[at : at + count]
+
+    store(0, pieces * rows, across(active_ref[...], grad_outer_ref[...]))
+    store(pieces * rows, rows, across(attended_ref[...], grad_branch_ref[...]))
+    for piece in range(pieces):
+        store(
+            (pieces + 1 + piece) * rows,
+            rows,
+            across(mixed_ref[...], grad_inner_ref[:, piece * D : (piece + 1) * D]),
+        )
+
+
+def weight_grads(sizes, active, grad_outer, attended, grad_branch, mixed, grad_inner):
+    batch, row, core = sizes
+    tokens = mixed.shape[0]
+    rows = D // (batch * row * core)
+    height = rows * (2 * (FF // D) + 1)
+    part = pl.BlockSpec((tokens, D // batch), lambda i: (0, i))
+    return pl.pallas_call(
+        grads_kernel,
+        grid=(batch,),
+        in_specs=[
+            pl.BlockSpec((tokens, FF // batch), lambda i: (0, i)),
+            whole((tokens, D)),
+            part,
+            whole((tokens, D)),
+            part,
+            whole((tokens, FF)),
+        ],
+        out_specs=pl.BlockSpec((None, core, row, height, D), lambda i: (i, 0, 0, 0, 0)),
+        out_shape=jax.ShapeDtypeStruct((batch, core, row, height, D), low_type),
+        compiler_params=pltpu.CompilerParams(vmem_limit_bytes=56 * 1024 * 1024),
+        cost_estimate=about(28),
+        name="weight_grads",
+    )(active, grad_outer, attended, grad_branch, mixed, grad_inner)
+
+
+def place_bits():
+    bits = []
+    for axis in ("core", "row", "batch"):
+        by = 1
+        while by < lax.axis_size(axis):
+            bits.append((axis, by))
+            by *= 2
+    return bits
+
+
+def swapped(value, axis, by):
+    return lax.ppermute(value, axis, [(i, i ^ by) for i in range(lax.axis_size(axis))])
+
+
+def gather_near(value):
+    for axis, by in place_bits():
+        value = jnp.concatenate([value, swapped(value, axis, by)], axis=0)
+    return value
+
+
+def halved_sum(value):
+    bits = place_bits()
+    value = value.reshape((2,) * len(bits) + value.shape[1:])
+    for count, (axis, by) in enumerate(bits):
+        mine = (lax.axis_index(axis) // by) % 2
+        at = len(bits) - 1 - count
+        send = lax.dynamic_index_in_dim(value, 1 - mine, at, keepdims=False)
+        keep = lax.dynamic_index_in_dim(value, mine, at, keepdims=False)
+        value = keep + swapped(send, axis, by)
+    return value
 
 
 def total_sum(value):
-    for axis in ("core", "batch", "row"):
-        size = lax.axis_size(axis)
-        by = 1
-        while by < size:
-            value = value + lax.ppermute(value, axis, [(i, i ^ by) for i in range(size)])
-            by *= 2
+    for axis, by in place_bits():
+        value = value + swapped(value, axis, by)
     return value
 
 
-def staged_sum(value):
-    batch, row, core = (lax.axis_size(axis) for axis in ALL)
-    value = value.reshape((batch, row, core) + value.shape[1:])
-    mine = lax.axis_index("core")
-    send = lax.dynamic_index_in_dim(value, 1 - mine, 2, keepdims=False).astype(low_type)
-    keep = lax.dynamic_index_in_dim(value, mine, 2, keepdims=False)
-    swap = [(i, 1 - i) for i in range(core)]
-    value = keep + lax.ppermute(send, "core", swap).astype(jnp.float32)
-    for axis in ("batch", "row"):
-        parts = lax.all_to_all(value.astype(low_type), axis, 0, 0, tiled=True)
-        value = jnp.sum(parts.astype(jnp.float32), axis=0)
-    return value
+def exchange_sum(value, axes):
+    count = value.shape[0]
+    mine = lax.axis_index(axes)
+    total = lax.dynamic_index_in_dim(value, mine, 0, keepdims=False)
+    value = value.astype(low_type)
+    parts = [
+        lax.ppermute(
+            lax.dynamic_index_in_dim(value, mine ^ offset, 0, keepdims=False),
+            axes,
+            [(i, i ^ offset) for i in range(count)],
+        )
+        for offset in range(1, count)
+    ]
+    for part in parts:
+        total = total + part.astype(jnp.float32)
+    return total
 
 
 def per_device(
@@ -573,9 +987,12 @@
     if moved:
         clip_index, chunk_index = row_index, batch_index * core_count + core_index
         head_axes, head_groups = ("batch", "core"), batch_count * core_count
+        rest_axes = ("row",)
     else:
         clip_index, chunk_index = batch_index, row_index * core_count + core_index
         head_axes, head_groups = ("row",), row_count
+        rest_axes = ("batch", "core")
+    owner_index = (batch_index * row_count + row_index) * core_count + core_index
 
     both = jnp.concatenate([clean_latents[0], noise_sample[0]], axis=1)
     if moved:
@@ -602,9 +1019,8 @@
     )
     first_weights = lax.all_gather(first_weights, ALL, axis=0, tiled=True)
     second_weights = jnp.concatenate(
-        [project_master.astype(low_type)]
-        + [expand_master[:, k * D : (k + 1) * D].astype(low_type) for k in range(FF // D)]
-        + [reduce_master.astype(low_type)],
+        [reduce_master.astype(low_type), project_master.astype(low_type)]
+        + [expand_master[:, k * D : (k + 1) * D].astype(low_type) for k in range(FF // D)],
         axis=0,
     )
     second_weights = lax.all_gather(second_weights, ALL, axis=0)
@@ -621,22 +1037,33 @@
     else:
         order_all = lambda v: v
     index_all = order_all(index_all)
-    hot_all = (index_all[:, None] == jnp.arange(NB + 1, dtype=jnp.int32)[None, :]).astype(
-        jnp.float32
-    )
-    pre_own = jnp.dot(
-        hot_all,
-        level_master.astype(low_type).astype(jnp.float32),
-        precision=lax.Precision.HIGHEST,
-    )
-    cond_value, silu_back = jax.vjp(jax.nn.silu, pre_own)
-    cond_own = cond_value.astype(low_type)
+    place = jnp.arange(devices, dtype=jnp.int32)
+    index_near = jnp.sum(
+        jnp.where(
+            ((owner_index ^ place)[:, None] == place[None, :])[..., None],
+            index_all.reshape(1, devices, frame_local),
+            0,
+        ),
+        axis=1,
+    ).reshape(-1)
+    table_low = level_master.astype(low_type).astype(jnp.float32)
+
+    def table_rows(index):
+        hot = (index[:, None] == jnp.arange(NB + 1, dtype=jnp.int32)[None, :]).astype(jnp.float32)
+        return hot, jnp.dot(hot, table_low, precision=lax.Precision.HIGHEST)
+
+    _, pre_own = table_rows(index_all)
+    hot_near, pre_near = table_rows(index_near)
+    cond_near, silu_back = jax.vjp(jax.nn.silu, pre_near)
+    cond_near = cond_near.astype(low_type)
+    cond_own = jax.nn.silu(pre_own).astype(low_type)
     adaptive_low = adaptive_master.astype(low_type)
     adapt_parts = lax.all_to_all(
         product(cond_own, adaptive_low).reshape(devices, frame_local, 6 * D), ALL, 0, 0, tiled=True
     )
     adapt = jnp.sum(adapt_parts, axis=0)
-    shift_one, scale_one, gate_one, shift_two, scale_two, gate_two = jnp.split(adapt, 6, axis=1)
+    shift_one, scale_one = adapt[:, :D], adapt[:, D : 2 * D]
+    mods = adapt.reshape(frame_local, 6, D)
 
     my_levels = lax.dynamic_slice_in_dim(
         lax.dynamic_index_in_dim(noise_levels, clip_index, 0, keepdims=False),
@@ -678,92 +1105,81 @@
     alpha_bar, noised, _ = plan(my_levels, my_flags)
     inputs = noised_input(clean_tok, noise_tok, alpha_bar, noised).astype(low_type)
     patch_turned = first_weights[:, 3 * D : 3 * D + PATCH_FEAT]
-    readout_weight = first_weights[:, 3 * D + PATCH_FEAT : 3 * D + 2 * PATCH_FEAT]
     triple_weight = first_weights
     hidden_zero = against(inputs, patch_turned)
     normed, first_back = jax.vjp(modulate, hidden_zero, shift_one, scale_one)
     normed_low = normed.astype(low_type)
 
+    width = D // head_groups
     heads = triple_heads(normed_low, triple_weight, my_times, spaces, head_groups)
     heads = lax.all_to_all(heads, head_axes, 0, 0, tiled=True)
-    width = D // head_groups
-    heads = heads.reshape(head_groups, 3, frame_local, FRAME_TOK, width)
-    queries, keys, values = heads[:, 0], heads[:, 1], heads[:, 2]
-    if not moved:
-        keys = lax.all_gather(keys, "core", axis=0, tiled=True)
-        values = lax.all_gather(values, "core", axis=0, tiled=True)
-    attended, flat, logs = attend(key_order, key_count, queries, keys, values)
+    if moved:
+        heads = heads.reshape(head_groups, frame_local, FRAME_TOK, 3 * width)
+        items = (heads, heads, heads)
+    else:
+        heads = heads.reshape(head_groups, 3, frame_local, FRAME_TOK, width)
+        items = (heads[:, 0],) + tuple(
+            lax.all_gather(heads[:, part], "core", axis=0, tiled=True) for part in (1, 2)
+        )
+    attended, flat, logs = attend(key_order, key_count, items, width)
     attended = attended.reshape(head_groups, token_count, width)
     attended = lax.all_to_all(attended, head_axes, 0, 0, tiled=True)
-    attended_low = attended.swapaxes(0, 1).reshape(token_count, D)
-
-    project_weight = second_weights[:, :rows].reshape(D, D)
-    expand_weights = [
-        second_weights[:, (1 + k) * rows : (2 + k) * rows].reshape(D, D) for k in range(FF // D)
-    ]
-    reduce_weight = second_weights[:, (1 + FF // D) * rows :].reshape(FF, D)
-    expand_weight = jnp.concatenate(expand_weights, axis=1)
-
-    branch = product(attended_low, project_weight)
-    hidden_one = hidden_zero + per_frame(gate_one, branch)
-    mixed_tok, second_back = jax.vjp(modulate, hidden_one, shift_two, scale_two)
-    mixed_low = mixed_tok.astype(low_type)
-    inner = product(mixed_low, expand_weight)
-    active, gelu_back = jax.vjp(gelu_tanh, inner)
-    active_low = active.astype(low_type)
-    outer = product(active_low, reduce_weight)
-    hidden_two = hidden_one + per_frame(gate_two, outer)
-    final, final_back = jax.vjp(layer_norm, hidden_two)
-    final_low = final.astype(low_type)
-    predicted = product(final_low, readout_weight)
-    residue = predicted - noise_tok
-    frame_loss = jnp.mean(jnp.square(residue).reshape(frame_local, -1), axis=1) * noised
+    attended, normed_low = lax.optimization_barrier((attended, normed_low))
+    normed_clip = lax.all_gather(normed_low, head_axes, axis=0, tiled=True)
+    attended_low, branch, hidden_one, mixed_low = project_norm(
+        attended, second_weights, hidden_zero, mods
+    )
     frame_count = jnp.sum((1 - clean_flags).astype(jnp.float32))
     loss_scale = noised * (2.0 / (FRAME_TOK * PATCH_FEAT)) / jnp.maximum(frame_count, 1.0)
-    grad_pred = (
-        (residue.reshape(frame_local, -1, residue.shape[-1]) * loss_scale[:, None, None])
-        .reshape(residue.shape)
-        .astype(low_type)
-    )
-    grad_readout = across(final_low, grad_pred)
-    (grad_hidden_two,) = final_back(against(grad_pred, readout_weight))
-    grad_outer = per_frame(gate_two, grad_hidden_two).astype(low_type)
-    grad_gate_two = frame_sum(gate_two, grad_hidden_two * outer)
-    grad_reduce = across(active_low, grad_outer)
-    (grad_inner,) = gelu_back(against(grad_outer, reduce_weight))
-    grad_inner_low = grad_inner.astype(low_type)
-    grad_expand = across(mixed_low, grad_inner_low)
-    hidden_part, grad_shift_two, grad_scale_two = second_back(
-        against(grad_inner_low, expand_weight)
-    )
-    grad_hidden_one = grad_hidden_two + hidden_part
-    grad_branch = per_frame(gate_one, grad_hidden_one).astype(low_type)
-    grad_gate_one = frame_sum(gate_one, grad_hidden_one * branch)
-    grad_project = across(attended_low, grad_branch)
-    second_grads = jnp.concatenate(
-        [grad_project.reshape(devices, rows, D)]
-        + [
-            grad_expand[:, k * D : (k + 1) * D].reshape(devices, rows, D) for k in range(FF // D)
-        ]
-        + [grad_reduce.reshape(devices, FF // devices, D)],
-        axis=1,
-    )
-    second_own = lax.psum_scatter(second_grads, ALL, scatter_dimension=0)
-
-    grad_attended = (
-        against(grad_branch, project_weight)
-        .astype(low_type)
-        .reshape(token_count, head_groups, width)
-        .swapaxes(0, 1)
+    (
+        inner,
+        active_low,
+        grad_hidden_two,
+        grad_outer,
+        grad_readout,
+        grad_gate_two,
+        squared,
+    ) = feed_forward(
+        loss_scale, mixed_low, second_weights, hidden_one, mods, first_weights, noise_tok
+    )
+    frame_loss = squared[:, 0, 0] * (1.0 / (FRAME_TOK * PATCH_FEAT)) * noised
+    grad_inner_low, grad_hidden_one, grad_branch, grad_attended, grad_mods = feed_backward(
+        grad_outer,
+        second_weights,
+        inner,
+        hidden_one,
+        grad_hidden_two,
+        branch,
+        mods,
+        head_groups,
     )
     grad_attended = lax.all_to_all(grad_attended, head_axes, 0, 0, tiled=True)
-    grad_attended = grad_attended.reshape(queries.shape)
-    grad_queries, grad_keys, grad_values = attend_back(
+    grad_attended = grad_attended.reshape(head_groups, frame_local, FRAME_TOK, width)
+    early_adapt = jnp.concatenate(
+        [grad_mods.reshape(frame_local, 3 * D), grad_gate_two.reshape(frame_local, D)], axis=1
+    ).astype(low_type)
+    early_adapt = gather_near(early_adapt)
+
+    second_grads = weight_grads(
+        (batch_count, row_count, core_count),
+        active_low,
+        grad_outer,
+        attended_low,
+        grad_branch,
+        mixed_low,
+        grad_inner_low,
+    )
+    second_own = lax.psum_scatter(
+        second_grads.reshape((-1,) + second_grads.shape[2:]),
+        ("batch", "core"),
+        scatter_dimension=0,
+    )
+    second_own = lax.psum_scatter(second_own, "row", scatter_dimension=0).astype(jnp.float32)
+
+    grads = attend_back(
         query_order,
         query_count,
-        queries,
-        keys,
-        values,
+        items,
         grad_attended,
         flat,
         logs,
@@ -771,68 +1187,83 @@
         key_times,
         spaces,
     )
-    if not moved:
-        grad_keys, grad_values = (
+    if moved:
+        grad_heads = grads[0].reshape(head_groups, token_count, 3 * width)
+    else:
+        grad_heads = [grads[0]] + [
             lax.psum_scatter(
                 item.astype(jnp.float32), "core", scatter_dimension=0, tiled=True
             ).astype(low_type)
-            for item in (grad_keys, grad_values)
+            for item in grads[1:]
+        ]
+        grad_heads = jnp.concatenate(grad_heads, axis=-1).reshape(
+            head_groups, token_count, 3 * width
         )
-    grad_heads = jnp.stack([grad_queries, grad_keys, grad_values], axis=1)
-    grad_heads = lax.all_to_all(
-        grad_heads.reshape(head_groups, 3, token_count, width), head_axes, 0, 0, tiled=True
-    )
-    grad_triple_tok = jnp.transpose(grad_heads, (2, 1, 0, 3)).reshape(token_count, 3 * D)
-    grad_triple = across(normed_low, grad_triple_tok)
+    grad_triple = across(
+        normed_clip.reshape(-1, D), grad_heads.reshape(head_groups * token_count, 3 * width)
+    )
+    grad_heads = lax.all_to_all(grad_heads, head_axes, 0, 0, tiled=True)
+    grad_triple_tok = (
+        grad_heads.reshape(head_groups, token_count, 3, width)
+        .transpose(1, 2, 0, 3)
+        .reshape(token_count, 3 * D)
+    )
     hidden_part, grad_shift_one, grad_scale_one = first_back(
         against(grad_triple_tok, triple_weight[:, : 3 * D])
     )
+    late_adapt = gather_near(
+        jnp.concatenate([grad_shift_one, grad_scale_one], axis=1).astype(low_type)
+    )
     grad_hidden_zero = (grad_hidden_one + hidden_part).astype(low_type)
     grad_patch = across(grad_hidden_zero, inputs)
-    first_grads = jnp.concatenate(
-        [
-            grad_triple,
-            grad_patch,
-            grad_readout,
-            jnp.zeros((D, LANES - 2 * PATCH_FEAT), jnp.float32),
-        ],
-        axis=1,
-    )
-    first_own = staged_sum(first_grads.reshape(devices, rows, first_grads.shape[1]))
-
-    grad_adapt_tok = jnp.concatenate(
-        [
-            grad_shift_one,
-            grad_scale_one,
-            grad_gate_one,
-            grad_shift_two,
-            grad_scale_two,
-            grad_gate_two,
-        ],
-        axis=1,
-    ).astype(low_type)
-    adapt_tok_all = lax.all_gather(grad_adapt_tok, ALL, axis=0, tiled=True)
-    adapt_own = across(cond_own, adapt_tok_all)
-    (grad_pre,) = silu_back(against(adapt_tok_all, adaptive_low))
+    small_own = halved_sum(
+        jnp.concatenate([grad_patch, grad_readout], axis=1).reshape(devices, -1, LANES)
+    ).reshape(rows, 2 * PATCH_FEAT)
+
+    grad_triple = grad_triple.reshape(batch_count, row_count, core_count, rows, 3 * width)
+    if moved:
+        grad_triple = grad_triple.transpose(1, 0, 2, 3, 4)
+    else:
+        grad_triple = grad_triple.transpose(0, 2, 1, 3, 4)
+    rest_count = devices // head_groups
+    triple_own = exchange_sum(
+        grad_triple.reshape(rest_count, head_groups, rows, 3 * width), rest_axes
+    )
+    triple_own = lax.all_to_all(triple_own, head_axes, 0, 0, tiled=True)
+    triple_own = (
+        triple_own.reshape(head_groups, rows, 3, width).transpose(1, 2, 0, 3).reshape(rows, 3 * D)
+    )
+    early_columns = 2 * D
+    adapt_own = jnp.concatenate(
+        [across(cond_near, late_adapt), across(cond_near, early_adapt)], axis=1
+    )
+    grad_cond = against(late_adapt, adaptive_low[:, :early_columns]) + against(
+        early_adapt, adaptive_low[:, early_columns:]
+    )
+    (grad_pre,) = silu_back(grad_cond)
     table_own = lax.dot_general(
-        hot_all,
+        hot_near,
         grad_pre,
         (((0,), (0,)), ((), ())),
         precision=lax.Precision.HIGHEST,
         preferred_element_type=jnp.float32,
     )
     expand_own = jnp.concatenate(
-        [second_own[(1 + k) * rows : (2 + k) * rows] for k in range(FF // D)], axis=1
+        [
+            second_own[(FF // D + 1 + k) * rows : (FF // D + 2 + k) * rows]
+            for k in range(FF // D)
+        ],
+        axis=1,
     )
     reduced = (
-        jnp.transpose(first_own[:, 3 * D : 3 * D + PATCH_FEAT]),
+        jnp.transpose(small_own[:, :PATCH_FEAT]),
         table_own,
         adapt_own,
-        first_own[:, : 3 * D],
-        second_own[:rows],
+        triple_own,
+        second_own[FF // D * rows : (FF // D + 1) * rows],
         expand_own,
-        second_own[(1 + FF // D) * rows :],
-        first_own[:, 3 * D + PATCH_FEAT : 3 * D + 2 * PATCH_FEAT],
+        second_own[: FF // D * rows],
+        small_own[:, PATCH_FEAT:],
     )
     squares = sum((jnp.sum(gradient * gradient) for gradient in reduced))
     level_hits = (my_levels[:, None] == jnp.arange(NB, dtype=jnp.int32)[None, :]).astype(

time: 832 us -> 646 us (0.78)
  matrix products: 98.9 us -> 21.3 us
  local copies, waits for them, and re-layouts: 110 us -> 56.9 us
  blocking collectives: 67.7 us -> 17.8 us
  waiting for transfers between devices: 267 us -> 241 us
  Pallas kernels: 160 us -> 183 us
  other arithmetic: 58.7 us -> 39.5 us
  starting transfers between devices: 39.1 us -> 55.6 us
    all_to_all x4 -> x2, waiting for transfers between devices: 100 us -> 0.01 us  [the longest x1 0.01 us: per_device(): grad_heads = lax.all_to_all(grad_heads, head_axes, 0, 0, tiled=True)]
    all_gather x1 -> x0, blocking collectives: 67.7 us -> none  [per_device(): adapt_tok_all = lax.all_gather(grad_adapt_tok, ALL, axis=0, tiled=True)]
    ppermute x6 -> x23, waiting for transfers between devices: 17.9 us -> 84.6 us  [the longest x20 69.6 us: swapped(): lax.ppermute(value, axis, [(i, i ^ by) for i in range(lax.axis_size(axis))])]
    pallas_call x0 -> x4, Pallas kernels: none -> 64 us  [the longest x1 23.1 us: feed_backward(): pl.pallas_call(backward_kernel, grid=(pieces,), in_specs=[whole((tokens,...]
    dot_general x5 -> x1, matrix products: 32.1 us -> 0.4 us  [product(): return jnp.dot(left, right, preferred_element_type=jnp.float32)]
    pallas_call x1, Pallas kernels: 69.8 us -> 43.2 us  [attend(): pl.pallas_call(attend_kernel, grid_spec=pltpu.PrefetchScalarGridSpec(num_...]
    ppermute x6 -> x23, starting transfers between devices: 4.71 us -> 31.2 us  [the longest x20 26.8 us: swapped(): lax.ppermute(value, axis, [(i, i ^ by) for i in range(lax.axis_size(axis))])]
    dot_general x7 -> x4, matrix products: 34.7 us -> 10.4 us  [against(): lax.dot_general(left, right, (((1,), (1,)), ((), ())), preferred_element_...]
  transfers between devices with their start and end apart: 17 -> 34, of which waited for: 13 -> 23; matrix products, arithmetic and copies ran while one was open for 14% -> 12% of each run, Pallas kernels for 19% -> 29%
where the time goes in v2:
time: 646 us; the launch traced here: 638 us
  waiting for transfers between devices  241 us (37%)
  Pallas kernels  183 us (28%)
  local copies, waits for them, and re-layouts  56.9 us (9%)
  starting transfers between devices  55.6 us (9%)
  other arithmetic  39.5 us (6%)
  between operations  23.2 us (4%)
  matrix products  21.3 us (3%)
  blocking collectives  17.8 us (3%)
    ppermute x20, waiting for transfers between devices, swapped(): lax.ppermute(value, axis, [(i, i ^ by) for i in range(lax.axis_size(axis))])  69.6 us
    pallas_call x1, Pallas kernels, attend_back(): pl.pallas_call(attend_back_kernel, grid_spec=pltpu.PrefetchScalarGridSpec...  66.1 us
    all_to_all x1, waiting for transfers between devices, per_device(): heads = lax.all_to_all(heads, head_axes, 0, 0, tiled=True)  53.9 us
    all_to_all x1, waiting for transfers between devices, per_device(): lax.all_to_all(product(cond_own, adaptive_low).reshape(devices, frame_loc...  48.3 us
    pallas_call x1, Pallas kernels, attend(): pl.pallas_call(attend_kernel, grid_spec=pltpu.PrefetchScalarGridSpec(num_...  43.2 us
    all_gather x1, waiting for transfers between devices, per_device(): first_weights = lax.all_gather(first_weights, ALL, axis=0, tiled=True)  30.6 us
    ppermute x20, starting transfers between devices, swapped(): lax.ppermute(value, axis, [(i, i ^ by) for i in range(lax.axis_size(axis))])  26.8 us
    pallas_call x1, Pallas kernels, feed_backward(): pl.pallas_call(backward_kernel, grid=(pieces,), in_specs=[whole((tokens,...  23.1 us
  transfers between devices with their start and end apart: 34, of which 23 were waited for; matrix products, arithmetic and copies ran while one was open for 12% of the time, Pallas kernels for 29%

profile of v2, /device:TPU:0, one launch (start us, length us, event | category | flops | bytes accessed | tf_op | source)
XLA Modules:
  0.0 638.5 jit_solution(4169006661689148578)
XLA Ops:
  16.4 7.3 %all-to-all-start = ((f32[32,2,6144]{2,1,0:T(2,128)}), f32[32,2,6144]{2,1,0:T(2,128)S(1)}, u32[]{:S(2)}, u32[]{:S(2)}) async-start(f32[32,2,6144]{2,1,0:T(2,128)} %reshape.688), calls=%async_computation | async-start | bytes 3145728 | tf_op jit(solution)/shard_map/all_to_all | solution.py:1061
  27.3 48.3 %all-to-all-done = f32[32,2,6144]{2,1,0:T(2,128)S(1)} async-done(((f32[32,2,6144]{2,1,0:T(2,128)}), f32[32,2,6144]{2,1,0:T(2,128)S(1)}, u32[]{:S(2)}, u32[]{:S(2)}) %all-to-all-start) | async-done | bytes 1572896 | tf_op jit(solution)/shard_map/all_to_all | solution.py:1061
  76.2 30.6 %all-gather.5.cloned.1.call-done.weight_ref.readout_ref = bf16[1024,3200]{1,0:T(8,128)(2,1)} async-done(((bf16[32,3200]{1,0:T(8,128)(2,1)}), bf16[1024,3200]{1,0:T(8,128)(2,1)}) %all-gather.5.cloned.1.call-update) | async-done | bytes 6553616 | tf_op jit(solution)/shard_map/all_gather | solution.py:1020
  111.2 3.2 copy-done.5
  114.4 9.8 %triple_heads.1 = bf16[8,512,384]{2,1,0:T(8,128)(2,1)S(1)} custom-call(bf16[512,1024]{1,0:T(8,128)(2,1)S(1)} %get-tuple-element.101.normed_ref, bf16[1024,3200]{1,0:T(8,128)(2,1)S(1)} %copy-done.5, f32[2,1,128]{2,1,0:T(1,128)S(1)} %get-tuple-element.282.time_cos, f32[2,1,128]{2,1,0:T(1,128)S(1)} %get-tuple-element.281.time_sin, ...), custom_call_target="tpu_custom_call" | custom-call | flops 11000000512 | bytes 1048576 | tf_op jit(solution)/shard_map/triple_heads/pallas_call | solution.py:192
  125.9 4.4 all-to-all-start.1
  131.2 53.9 %all-to-all-done.1 = bf16[8,512,384]{2,1,0:T(8,128)(2,1)} async-done(((bf16[8,512,384]{2,1,0:T(8,128)(2,1)}), bf16[8,512,384]{2,1,0:T(8,128)(2,1)}, u32[]{:S(2)}, u32[]{:S(2)}) %all-to-all-start.1) | async-done | bytes 3145760 | tf_op jit(solution)/shard_map/all_to_all | solution.py:1115
  185.1 43.2 %attend.1 = (bf16[8,2,256,128]{3,2,1,0:T(8,128)(2,1)S(1)}, f32[16,128,256]{2,1,0:T(8,128)S(1)}, f32[16,1,512]{2,1,0:T(1,128)S(1)}) custom-call(s32[16]{0:T(128)S(1)} %select_reduce_fusion.2.order_ref, s32[16]{0:T(128)S(1)} %get-tuple-element.222.count_ref, bf16[8,2,256,384]{3,2,1,0:T(8,128)(2,1)} %bitcast.9.query_ref.key_ref.value_ref, ...), custom_call_target="tpu_custom_call" | custom-call | flops 49500000256 | bytes 1048576 | tf_op jit(solution)/shard_map/attend/pallas_call | solution.py:336
  230.3 17.8 %all_to_all.30.heads_ref = bf16[8,512,128]{2,1,0:T(8,128)(2,1)S(1)} all-to-all(bf16[8,512,128]{2,1,0:T(8,128)(2,1)S(1)} %bitcast.165), channel_id=1, replica_groups=mesh['batch'=4,'row'=4,'core'=2] {'batch','core'}, dimensions={0} | all-to-all | bytes 2097152 | tf_op jit(solution)/shard_map/all_to_all | solution.py:1126
  251.2 3.7 project_norm.1
  259.6 20.5 %feed_forward.1 = (f32[512,4096]{1,0:T(8,128)}, bf16[512,4096]{1,0:T(8,128)(2,1)}, f32[512,1024]{1,0:T(8,128)}, bf16[512,1024]{1,0:T(8,128)(2,1)}, f32[1024,16]{...) custom-call(f32[2]{0:T(128)} %fusion.49.scale_ref, bf16[512,1024]{1,0:T(8,128)(2,1)} %copy-done.9, ...), custom_call_target="tpu_custom_call" | custom-call | flops 22000001024 | bytes 1048576 | tf_op jit(solution)/shard_map/feed_forward/pallas_call | solution.py:671
  280.1 23.1 %feed_backward.1 = (bf16[512,4096]{1,0:T(8,128)(2,1)}, f32[512,1024]{1,0:T(8,128)}, bf16[512,1024]{1,0:T(8,128)(2,1)}, bf16[8,512,128]{2,1,0:T(8,128)(2,1)}, f32[2,3,1024]{2,1,0:T(4,128)}) custom-call(bf16[512,1024]{1,0:T(8,128)(2,1)} %get-tuple-element.90.grad_outer_ref, bf16[32,288,1024]{2,1,0:T(8,128)(2,1)} %bitcast.170, ...), custom_call_target="tpu_custom_call" | custom-call | flops 24199999488 | bytes 1048576 | tf_op jit(solution)/shard_map/feed_backward/pallas_call | solution.py:778
  303.2 16.6 %weight_grads.1 = bf16[4,2,4,288,1024]{4,3,2,1,0:T(8,128)(2,1)} custom-call(bf16[512,4096]{1,0:T(8,128)(2,1)} %get-tuple-element.102.active_ref, bf16[512,1024]{1,0:T(8,128)(2,1)} %get-tuple-element.90.grad_outer_ref, bf16[512,1024]{1,0:T(8,128)(2,1)} %copy-done.8, bf16[512,1024]{1,0:T(8,128)(2,1)} %get-tuple-element.104.grad_branch_ref, ...), custom_call_target="tpu_custom_call" | custom-call | flops 30799998976 | bytes 1048576 | tf_op jit(solution)/shard_map/weight_grads/pallas_call | solution.py:843
  324.7 3.6 all-to-all-start.3
  331.2 3.9 collective-permute-done.13
  336.9 7.1 %all-to-all-done.3 = bf16[8,512,128]{2,1,0:T(8,128)(2,1)S(1)} async-done(((bf16[8,512,128]{2,1,0:T(8,128)(2,1)}), bf16[8,512,128]{2,1,0:T(8,128)(2,1)S(1)}, u32[]{:S(2)}, u32[]{:S(2)}) %all-to-all-start.3) | async-done | bytes 1048608 | tf_op jit(solution)/shard_map/all_to_all | solution.py:1156
  345.1 66.1 %attend_back.1 = bf16[8,2,256,384]{3,2,1,0:T(8,128)(2,1)} custom-call(s32[16]{0:T(128)} %select_reduce_fusion.1.order_ref, s32[16]{0:T(128)} %get-tuple-element.220.count_ref, bf16[8,2,256,384]{3,2,1,0:T(8,128)(2,1)} %bitcast.9.query_ref.key_ref.value_ref, bf16[8,2,256,384]{3,2,1,0:T(8,128)(2,1)} %bitcast.9.query_ref.key_ref.value_ref, ...), custom_call_target="tpu_custom_call" | custom-call | flops 71499997184 | bytes 1048576 | tf_op jit(solution)/shard_map/attend_back/pallas_call | solution.py:512
  411.3 4.7 copy.202
  415.9 4.6 all-to-all-start.4
  420.9 11.4 %copy.211 = bf16[1024,4096]{1,0:T(8,128)(2,1)} copy(bf16[1024,4096]{0,1:T(8,128)(2,1)} %bitcast.173) | data formatting | bytes 16777216 | tf_op jit(solution)/shard_map/dot_general | solution.py:39
  438.5 44.7 %collective-permute-done.15 = bf16[32,4096]{1,0:T(8,128)(2,1)S(1)} collective-permute-done((bf16[32,4096]{1,0:T(8,128)(2,1)S(1)}, bf16[32,4096]{1,0:T(8,128)(2,1)S(1)}, u32[]{:S(2)}, u32[]{:S(2)}) %collective-permute-start.15) | collective-permute-done | bytes 262176 | tf_op jit(solution)/shard_map/ppermute | solution.py:873
  483.7 7.9 %convolution_bitcast_fusion = f32[4,4,2,32,384]{4,3,2,0,1:T(8,128)S(1)} fusion(bf16[4,4,2,32,4096]{4,3,2,1,0:T(8,128)(2,1)} %bitcast.174, bf16[4096,384,1,1,1]{1,0,4,3,2:T(8,128)(2,1)} %bitcast.178), kind=kOutput, calls=%fused_computation.13 | convolution fusion | flops 3221225472 | bytes 13107200 | tf_op jit(solution)/shard_map/dot_general | solution.py:39
  491.9 3.4 collective-permute-start.18
  497.2 4.4 collective-permute-done.18
  501.6 10.6 %collective-permute-done.17 = bf16[8,32,384]{2,1,0:T(8,128)(2,1)S(1)} collective-permute-done((bf16[8,32,384]{2,1,0:T(8,128)(2,1)S(1)}, bf16[8,32,384]{2,1,0:T(8,128)(2,1)S(1)}, u32[]{:S(2)}, u32[]{:S(2)}) %collective-permute-start.17) | collective-permute-done | bytes 196640 | tf_op jit(solution)/shard_map/ppermute | solution.py:906
  513.1 3.5 all-to-all-start.5
  516.6 5.1 copy.203
  521.8 5.8 dot_general.45
  527.6 7.9 %fusion.54 = (bf16[2,1024]{1,0:T(2,128)(2,1)S(1)}, bf16[2,1024]{1,0:T(2,128)(2,1)S(1)}, f32[2,256,1024]{2,1,0:T(8,128)S(1)}) fusion(f32[512,1024]{1,0:T(8,128)} %get-tuple-element.253, f32[2,1024]{1,0:T(2,128)S(1)} %copy-done.49, bf16[2,256,3072]{2,1,0:T(8,128)(2,1)} %dot_general.45, bf16[1024,3200]{1,0:T(8,128)(2,1)} %all-gather.5.cloned.1.call-done.weight_ref.readout_ref), kind=kOutput, calls=%fused_computation.205 | convolution fusion | flops 3223318528 | bytes 13647872 | tf_op jit(solution)/shard_map/dot_general | solution.py:45
  550.2 3.8 collective-permute-done.3
  571.8 15.4 %reduce-scatter.5.cloned.1.call-done = bf16[1,288,1024]{2,1,0:T(8,128)(2,1)} async-done(((bf16[4,288,1024]{2,1,0:T(8,128)(2,1)}), bf16[1,288,1024]{2,1,0:T(8,128)(2,1)}) %reduce-scatter.5.cloned.1.call-update) | async-done | bytes 589840 | tf_op jit(solution)/shard_map/reduce_scatter | solution.py:1177
  620.7 3.3 multiply_subtract_fusion
  (363 shorter events, 115.5 us)
Async XLA Ops:
  7.3 99.5 %all-gather.5.cloned.1.call-start = ((), (), s32[]{:S(2)}) async-start(), calls=%async_computation.8 | async-start | bytes 6758400 | tf_op jit(solution)/shard_map/all_gather | solution.py:1020
  10.8 240.4 %all-gather.9.cloned.1.call-start = ((), (), s32[]{:S(2)}) async-start(), calls=%async_computation.12 | async-start | bytes 19464192 | tf_op jit(solution)/shard_map/all_gather | solution.py:1026
  16.4 59.2 %all-to-all-start = ((f32[32,2,6144]{2,1,0:T(2,128)}), f32[32,2,6144]{2,1,0:T(2,128)S(1)}, u32[]{:S(2)}, u32[]{:S(2)}) async-start(f32[32,2,6144]{2,1,0:T(2,128)} %reshape.688), calls=%async_computation | async-start | bytes 3145728 | tf_op jit(solution)/shard_map/all_to_all | solution.py:1061
  23.9 2.4 collective-permute-start
  125.9 59.1 %all-to-all-start.1 = ((bf16[8,512,384]{2,1,0:T(8,128)(2,1)}), bf16[8,512,384]{2,1,0:T(8,128)(2,1)}, u32[]{:S(2)}, u32[]{:S(2)}) async-start(bf16[8,512,384]{2,1,0:T(8,128)(2,1)} %copy-done.1), calls=%async_computation.1 | async-start | bytes 6291456 | tf_op jit(solution)/shard_map/all_to_all | solution.py:1115
  130.4 290.5 %all-gather.7.cloned.1.call-start = ((), (), s32[]{:S(2)}) async-start(), calls=%async_computation.9 | async-start | bytes 9437184 | tf_op jit(solution)/shard_map/all_gather | solution.py:1128
  248.1 289.3 %reduce-scatter.3.cloned.1.call-start = ((), (), s32[]{:S(2)}) async-start(), calls=%async_computation.10 | async-start | bytes 21233664 | tf_op jit(solution)/shard_map/reduce_scatter | solution.py:1172
  322.8 5.4 collective-permute-start.12
  324.7 19.4 %all-to-all-start.3 = ((bf16[8,512,128]{2,1,0:T(8,128)(2,1)}), bf16[8,512,128]{2,1,0:T(8,128)(2,1)S(1)}, u32[]{:S(2)}, u32[]{:S(2)}) async-start(bf16[8,512,128]{2,1,0:T(8,128)(2,1)} %get-tuple-element.95), calls=%async_computation.3 | async-start | bytes 2097152 | tf_op jit(solution)/shard_map/all_to_all | solution.py:1156
  328.3 6.8 %collective-permute-start.13 = (bf16[8,4096]{1,0:T(8,128)(2,1)S(1)}, bf16[8,4096]{1,0:T(8,128)(2,1)S(1)}, u32[]{:S(2)}, u32[]{:S(2)}) collective-permute-start(bf16[8,4096]{1,0:T(8,128)(2,1)S(1)} %pad_maximum_fusion.6), channel_id=1, source_target_pairs={{0,4},{2,6},{4,0},{6,2},{1,5},{3,7},{5,1},{7,3},{8,12},{10,14},{12... | collective-permute-start | bytes 196616 | tf_op jit(solution)/shard_map/ppermute | solution.py:873
  335.2 97.6 %collective-permute-start.14 = (bf16[16,4096]{1,0:T(8,128)(2,1)S(1)}, bf16[16,4096]{1,0:T(8,128)(2,1)S(1)}, u32[]{:S(2)}, u32[]{:S(2)}) collective-permute-start(bf16[16,4096]{1,0:T(8,128)(2,1)S(1)} %pad_maximum_fusion.3), channel_id=1, source_target_pairs={{0,8},{8,0},{16,24},{24,16},{1,9},{9,1},{17,25},{25,17},{2,10},{10... | collective-permute-start | bytes 393224 | tf_op jit(solution)/shard_map/ppermute | solution.py:873
  415.9 97.2 %all-to-all-start.4 = ((bf16[8,512,384]{1,2,0:T(8,128)(2,1)}), bf16[8,512,384]{1,2,0:T(8,128)(2,1)}, u32[]{:S(2)}, u32[]{:S(2)}) async-start(bf16[8,512,384]{1,2,0:T(8,128)(2,1)} %copy.202), calls=%async_computation.4 | async-start | bytes 6291456 | tf_op jit(solution)/shard_map/all_to_all | solution.py:1205
  432.9 50.4 %collective-permute-start.15 = (bf16[32,4096]{1,0:T(8,128)(2,1)S(1)}, bf16[32,4096]{1,0:T(8,128)(2,1)S(1)}, u32[]{:S(2)}, u32[]{:S(2)}) collective-permute-start(bf16[32,4096]{1,0:T(8,128)(2,1)S(1)} %concatenate.84), channel_id=1, source_target_pairs={{0,16},{8,24},{16,0},{24,8},{1,17},{9,25},{17,1},{25,9},{2,18},{10... | collective-permute-start | bytes 786440 | tf_op jit(solution)/shard_map/ppermute | solution.py:873
  491.9 9.7 %collective-permute-start.18 = (bf16[8,32,384]{2,1,0:T(8,128)(2,1)S(1)}, bf16[8,32,384]{2,1,0:T(8,128)(2,1)S(1)}, u32[]{:S(2)}, u32[]{:S(2)}) collective-permute-start(bf16[8,32,384]{2,1,0:T(8,128)(2,1)S(1)} %get-tuple-element.265), channel_id=1, source_target_pairs={{0,6},{2,4},{4,2},{6,0},{1,7},{3,5},{5,3},{7,1},{8,14},{10,12},{12... | collective-permute-start | bytes 589832 | tf_op jit(solution)/shard_map/ppermute | solution.py:906
  495.3 17.0 %collective-permute-start.17 = (bf16[8,32,384]{2,1,0:T(8,128)(2,1)S(1)}, bf16[8,32,384]{2,1,0:T(8,128)(2,1)S(1)}, u32[]{:S(2)}, u32[]{:S(2)}) collective-permute-start(bf16[8,32,384]{2,1,0:T(8,128)(2,1)S(1)} %get-tuple-element.266), channel_id=1, source_target_pairs={{0,4},{2,6},{4,0},{6,2},{1,5},{3,7},{5,1},{7,3},{8,12},{10,14},{12... | collective-permute-start | bytes 589832 | tf_op jit(solution)/shard_map/ppermute | solution.py:906
  495.3 17.0 %collective-permute-start.16 = (bf16[8,32,384]{2,1,0:T(8,128)(2,1)S(1)}, bf16[8,32,384]{2,1,0:T(8,128)(2,1)S(1)}, u32[]{:S(2)}, u32[]{:S(2)}) collective-permute-start(bf16[8,32,384]{2,1,0:T(8,128)(2,1)S(1)} %get-tuple-element.264), channel_id=1, source_target_pairs={{0,2},{2,0},{4,6},{6,4},{1,3},{3,1},{5,7},{7,5},{8,10},{10,8},{12,... | collective-permute-start | bytes 589832 | tf_op jit(solution)/shard_map/ppermute | solution.py:906
  513.1 47.4 %all-to-all-start.5 = ((f32[8,32,384]{2,1,0:T(8,128)}), f32[8,32,384]{2,1,0:T(8,128)S(1)}, u32[]{:S(2)}, u32[]{:S(2)}) async-start(f32[8,32,384]{2,1,0:T(8,128)} %fusion.12), calls=%async_computation.5 | async-start | bytes 786432 | tf_op jit(solution)/shard_map/all_to_all | solution.py:1232
  516.6 70.5 %reduce-scatter.5.cloned.1.call-start = ((), (), s32[]{:S(2)}) async-start(), calls=%async_computation.11 | async-start | bytes 2949120 | tf_op jit(solution)/shard_map/reduce_scatter | solution.py:1177
  541.2 1.3 collective-permute-start.1
  542.6 4.6 collective-permute-start.2
  542.9 4.8 collective-permute-start.7
  547.1 6.9 %collective-permute-start.3 = (f32[2,2,8,128]{3,2,1,0:T(8,128)S(1)}, f32[2,2,8,128]{3,2,1,0:T(8,128)S(1)}, u32[]{:S(2)}, u32[]{:S(2)}) collective-permute-start(f32[2,2,8,128]{3,2,1,0:T(8,128)S(1)} %dynamic-slice_bitcast_fusion.4), channel_id=1, source_target_pairs={{0,4},{2,6},{4,0},{6,2},{1,5},{3,7},{5,1},{7,3},{8,12},{10,14},{12... | collective-permute-start | bytes 49160 | tf_op jit(solution)/shard_map/ppermute | solution.py:873
  547.7 9.3 %collective-permute-start.8 = (bf16[8,2048]{1,0:T(8,128)(2,1)S(1)}, bf16[8,2048]{1,0:T(8,128)(2,1)S(1)}, u32[]{:S(2)}, u32[]{:S(2)}) collective-permute-start(bf16[8,2048]{1,0:T(8,128)(2,1)S(1)} %pad_maximum_fusion.7), channel_id=1, source_target_pairs={{0,4},{2,6},{4,0},{6,2},{1,5},{3,7},{5,1},{7,3},{8,12},{10,14},{12... | collective-permute-start | bytes 98312 | tf_op jit(solution)/shard_map/ppermute | solution.py:873
  554.1 4.8 collective-permute-start.4
  557.1 4.3 collective-permute-start.9
  558.9 4.4 collective-permute-start.5
  561.5 5.0 collective-permute-start.10
  597.9 1.4 collective-permute-start.19
  599.9 3.6 collective-permute-start.20
  603.5 4.5 collective-permute-start.21
  608.0 3.6 collective-permute-start.22
  611.7 3.6 collective-permute-start.23
  (83 other events, 987.7 us)
Sparse Core Ops, SparseCore 0:
  11.5 95.2 all-gather.4
  110.4 140.7 all-gather.8
  253.1 52.5 all-gather.6
  320.0 162.5 reduce-scatter.2
  537.6 49.5 reduce-scatter.4

commit v3 on v2

--- a/solution.py
+++ b/solution.py
@@ -63,17 +63,6 @@
         + jnp.sqrt(1.0 - alpha_bar)[:, None, None] * noise_frames
     )
     return jnp.where(noised[:, None, None] > 0.5, mixed_tok, clean_frames).reshape(clean_tok.shape)
-
-
-def layer_norm(hidden):
-    centred = hidden - jnp.mean(hidden, axis=-1, keepdims=True)
-    variance = jnp.mean(centred * centred, axis=-1, keepdims=True)
-    return centred * lax.rsqrt(variance + 1e-06)
-
-
-def modulate(hidden, shift, scale):
-    normed = layer_norm(hidden).reshape(shift.shape[0], -1, hidden.shape[-1])
-    return (normed * (1.0 + scale[:, None]) + shift[:, None]).reshape(hidden.shape)
 
 
 def adamw_update(master, first_moment, second_moment, gradient, factor, step_rate):
@@ -135,21 +124,62 @@
     return jnp.concatenate([value[:, half:], value[:, :half]], axis=1)
 
 
-def triple_kernel(normed_ref, weight_ref, time_cos, time_sin, space_cos, space_sin, out_ref):
+def norm_parts(hidden):
+    centred = hidden - jnp.mean(hidden, axis=-1, keepdims=True)
+    variance = jnp.mean(centred * centred, axis=-1, keepdims=True)
+    inverse = lax.rsqrt(variance + 1e-06)
+    return centred * inverse, inverse
+
+
+def norm_back(normed, inverse, grad):
+    along = jnp.mean(grad * normed, axis=-1, keepdims=True)
+    return inverse * (grad - jnp.mean(grad, axis=-1, keepdims=True) - normed * along)
+
+
+def row_sum(value):
+    return jnp.sum(value, axis=0, keepdims=True)
+
+
+def triple_kernel(
+    inputs_ref,
+    extra_ref,
+    mods_ref,
+    weight_ref,
+    time_cos,
+    time_sin,
+    space_cos,
+    space_sin,
+    hidden_ref,
+    normed_ref,
+    out_ref,
+):
     column = pl.program_id(0)
     width = out_ref.shape[-1]
+    frames = mods_ref.shape[0]
+
+    @pl.when(column == 0)
+    def _():
+        patch = extra_ref[...][:, :PATCH_FEAT]
+        for frame in range(frames):
+            tokens = slice(frame * FRAME_TOK, (frame + 1) * FRAME_TOK)
+            hidden = against(inputs_ref[tokens], patch)
+            hidden_ref[tokens] = hidden
+            normed, _ = norm_parts(hidden)
+            normed_ref[tokens] = (
+                normed * (1.0 + mods_ref[frame, 1:2]) + mods_ref[frame, 0:1]
+            ).astype(low_type)
+
     acc = product(normed_ref[...], weight_ref[...])
     per_block = acc.shape[1] // LANES
-    frames = acc.shape[0] // FRAME_TOK
 
     def store(piece, values):
         for part in range(LANES // width):
-            place = piece * (LANES // width) + part
+            at = piece * (LANES // width) + part
             done = values[:, part * width : (part + 1) * width].astype(low_type)
             if len(out_ref.shape) == 3:
-                out_ref[place] = done
+                out_ref[at] = done
             else:
-                out_ref[place, 0] = done
+                out_ref[at, 0] = done
 
     turned = column < 2 * D // acc.shape[1]
 
@@ -173,39 +203,118 @@
             store(piece, acc[:, piece * LANES : (piece + 1) * LANES])
 
 
-def triple_heads(normed, weight, times, spaces, groups):
-    tokens = normed.shape[0]
+BLOCK = 256
+
+
+def heads_layout(groups, tokens):
     width = D // groups
-    block = 256
-    per_block = block // width
-    per_part = D // block
+    per_block = BLOCK // width
+    per_part = D // BLOCK
     if width == LANES:
-        out_specs = pl.BlockSpec(
+        return (groups, tokens, 3 * width), pl.BlockSpec(
             (per_block, tokens, width), lambda j: (j % per_part, 0, j // per_part)
         )
-        out_shape = jax.ShapeDtypeStruct((groups, tokens, 3 * width), low_type)
-    else:
-        out_specs = pl.BlockSpec(
-            (per_block, 1, tokens, width), lambda j: (j % per_part, j // per_part, 0, 0)
-        )
-        out_shape = jax.ShapeDtypeStruct((groups, 3, tokens, width), low_type)
+    return (groups, 3, tokens, width), pl.BlockSpec(
+        (per_block, 1, tokens, width), lambda j: (j % per_part, j // per_part, 0, 0)
+    )
+
+
+def triple_heads(inputs, mods, weight, times, spaces, groups):
+    tokens = inputs.shape[0]
+    shape, spec = heads_layout(groups, tokens)
     return pl.pallas_call(
         triple_kernel,
-        grid=(3 * D // block,),
+        grid=(3 * D // BLOCK,),
         in_specs=[
-            pl.BlockSpec((tokens, D), lambda j: (0, 0)),
-            pl.BlockSpec((D, block), lambda j: (0, j)),
-            pl.BlockSpec(times[0].shape, lambda j: (0, 0, 0)),
-            pl.BlockSpec(times[1].shape, lambda j: (0, 0, 0)),
-            pl.BlockSpec(spaces[0].shape, lambda j: (0, 0)),
-            pl.BlockSpec(spaces[1].shape, lambda j: (0, 0)),
+            whole(inputs.shape),
+            pl.BlockSpec((D, LANES), lambda j: (0, 3 * D // LANES)),
+            whole(mods.shape),
+            pl.BlockSpec((D, BLOCK), lambda j: (0, j)),
+            whole(times[0].shape),
+            whole(times[1].shape),
+            whole(spaces[0].shape),
+            whole(spaces[1].shape),
         ],
-        out_specs=out_specs,
-        out_shape=out_shape,
-        compiler_params=pltpu.CompilerParams(vmem_limit_bytes=32 * 1024 * 1024),
-        cost_estimate=about(10),
+        out_specs=[whole((tokens, D)), whole((tokens, D)), spec],
+        out_shape=[
+            jax.ShapeDtypeStruct((tokens, D), jnp.float32),
+            jax.ShapeDtypeStruct((tokens, D), low_type),
+            jax.ShapeDtypeStruct(shape, low_type),
+        ],
+        compiler_params=pltpu.CompilerParams(vmem_limit_bytes=40 * 1024 * 1024),
+        cost_estimate=about(12),
         name="triple_heads",
-    )(normed, weight, *times, *spaces)
+    )(inputs, weight, mods, weight, *times, *spaces)
+
+
+def triple_back_kernel(
+    grads_ref,
+    weight_ref,
+    hidden_ref,
+    grad_one_ref,
+    mods_ref,
+    inputs_ref,
+    grad_mods_ref,
+    grad_patch_ref,
+    sum_ref,
+):
+    step = pl.program_id(0)
+    frames = mods_ref.shape[0]
+    pieces = range(grads_ref.shape[0])
+    if len(grads_ref.shape) == 3:
+        grads = jnp.concatenate([grads_ref[piece] for piece in pieces], axis=1)
+    else:
+        grads = jnp.concatenate([grads_ref[piece, 0] for piece in pieces], axis=1)
+    part = against(grads, weight_ref[...])
+
+    @pl.when(step == 0)
+    def _():
+        sum_ref[...] = part
+
+    @pl.when(step > 0)
+    def _():
+        sum_ref[...] += part
+
+    @pl.when(step == pl.num_programs(0) - 1)
+    def _():
+        grad_patch = jnp.zeros((D, PATCH_FEAT), jnp.float32)
+        for frame in range(frames):
+            tokens = slice(frame * FRAME_TOK, (frame + 1) * FRAME_TOK)
+            normed, inverse = norm_parts(hidden_ref[tokens])
+            grad_normed = sum_ref[tokens]
+            grad_mods_ref[frame, 0:1] = row_sum(grad_normed)
+            grad_mods_ref[frame, 1:2] = row_sum(grad_normed * normed)
+            grad_hidden = grad_one_ref[tokens] + norm_back(
+                normed, inverse, grad_normed * (1.0 + mods_ref[frame, 1:2])
+            )
+            grad_patch += across(grad_hidden.astype(low_type), inputs_ref[tokens])
+        grad_patch_ref[...] = grad_patch
+
+
+def triple_back(grads, weight, hidden, grad_one, mods, inputs, groups):
+    tokens = inputs.shape[0]
+    frames = mods.shape[0]
+    return pl.pallas_call(
+        triple_back_kernel,
+        grid=(3 * D // BLOCK,),
+        in_specs=[
+            heads_layout(groups, tokens)[1],
+            pl.BlockSpec((D, BLOCK), lambda j: (0, j)),
+            whole(hidden.shape),
+            whole(hidden.shape),
+            whole(mods.shape),
+            whole(inputs.shape),
+        ],
+        out_specs=[whole((frames, 2, D)), whole((D, PATCH_FEAT))],
+        out_shape=[
+            jax.ShapeDtypeStruct((frames, 2, D), jnp.float32),
+            jax.ShapeDtypeStruct((D, PATCH_FEAT), jnp.float32),
+        ],
+        scratch_shapes=[pltpu.VMEM((tokens, D), jnp.float32)],
+        compiler_params=pltpu.CompilerParams(vmem_limit_bytes=40 * 1024 * 1024),
+        cost_estimate=about(12),
+        name="triple_back",
+    )(grads, weight, hidden, grad_one, mods, inputs)
 
 
 def head_stack(value):
@@ -541,22 +650,6 @@
         cost_estimate=about(65),
         name="attend_back",
     )(order, count, *items, grads, flat, logs, *query_times, *key_times, *spaces)
-
-
-def norm_parts(hidden):
-    centred = hidden - jnp.mean(hidden, axis=-1, keepdims=True)
-    variance = jnp.mean(centred * centred, axis=-1, keepdims=True)
-    inverse = lax.rsqrt(variance + 1e-06)
-    return centred * inverse, inverse
-
-
-def norm_back(normed, inverse, grad):
-    along = jnp.mean(grad * normed, axis=-1, keepdims=True)
-    return inverse * (grad - jnp.mean(grad, axis=-1, keepdims=True) - normed * along)
-
-
-def row_sum(value):
-    return jnp.sum(value, axis=0, keepdims=True)
 
 
 def flat_weight(ref):
@@ -859,52 +952,34 @@
     )(active, grad_outer, attended, grad_branch, mixed, grad_inner)
 
 
-def place_bits():
-    bits = []
-    for axis in ("core", "row", "batch"):
-        by = 1
-        while by < lax.axis_size(axis):
-            bits.append((axis, by))
-            by *= 2
-    return bits
-
-
-def swapped(value, axis, by):
-    return lax.ppermute(value, axis, [(i, i ^ by) for i in range(lax.axis_size(axis))])
-
-
-def gather_near(value):
-    for axis, by in place_bits():
-        value = jnp.concatenate([value, swapped(value, axis, by)], axis=0)
+def swapped(value, axis, offset):
+    return lax.ppermute(value, axis, [(i, i ^ offset) for i in range(lax.axis_size(axis))])
+
+
+def gather_near(value, axes=("core", "batch", "row")):
+    for axis in axes:
+        others = [swapped(value, axis, offset) for offset in range(1, lax.axis_size(axis))]
+        value = jnp.concatenate([value] + others, axis=0)
     return value
 
 
-def halved_sum(value):
-    bits = place_bits()
-    value = value.reshape((2,) * len(bits) + value.shape[1:])
-    for count, (axis, by) in enumerate(bits):
-        mine = (lax.axis_index(axis) // by) % 2
-        at = len(bits) - 1 - count
-        send = lax.dynamic_index_in_dim(value, 1 - mine, at, keepdims=False)
-        keep = lax.dynamic_index_in_dim(value, mine, at, keepdims=False)
-        value = keep + swapped(send, axis, by)
-    return value
-
-
-def total_sum(value):
-    for axis, by in place_bits():
-        value = value + swapped(value, axis, by)
-    return value
-
-
-def exchange_sum(value, axes):
-    count = value.shape[0]
+def near_owner(index):
+    batch, row, core = (lax.axis_size(axis) for axis in ALL)
+    places = (
+        (index // core % batch) ^ lax.axis_index("batch"),
+        (index // (core * batch)) ^ lax.axis_index("row"),
+        (index % core) ^ lax.axis_index("core"),
+    )
+    return (places[0] * row + places[1]) * core + places[2]
+
+
+def exchange_sum(value, axes, at=0, sent=jnp.float32):
+    count = value.shape[at]
     mine = lax.axis_index(axes)
-    total = lax.dynamic_index_in_dim(value, mine, 0, keepdims=False)
-    value = value.astype(low_type)
+    total = lax.dynamic_index_in_dim(value, mine, at, keepdims=False)
     parts = [
         lax.ppermute(
-            lax.dynamic_index_in_dim(value, mine ^ offset, 0, keepdims=False),
+            lax.dynamic_index_in_dim(value, mine ^ offset, at, keepdims=False).astype(sent),
             axes,
             [(i, i ^ offset) for i in range(count)],
         )
@@ -913,6 +988,17 @@
     for part in parts:
         total = total + part.astype(jnp.float32)
     return total
+
+
+def total_sum(value):
+    for axis in ("core", "batch", "row"):
+        parts = [value] + [
+            swapped(value, axis, offset) for offset in range(1, lax.axis_size(axis))
+        ]
+        while len(parts) > 1:
+            parts = [parts[i] + parts[i + 1] for i in range(0, len(parts), 2)]
+        value = parts[0]
+    return value
 
 
 def per_device(
@@ -992,7 +1078,6 @@
         clip_index, chunk_index = batch_index, row_index * core_count + core_index
         head_axes, head_groups = ("row",), row_count
         rest_axes = ("batch", "core")
-    owner_index = (batch_index * row_count + row_index) * core_count + core_index
 
     both = jnp.concatenate([clean_latents[0], noise_sample[0]], axis=1)
     if moved:
@@ -1037,10 +1122,10 @@
     else:
         order_all = lambda v: v
     index_all = order_all(index_all)
-    place = jnp.arange(devices, dtype=jnp.int32)
+    every = jnp.arange(devices, dtype=jnp.int32)
     index_near = jnp.sum(
         jnp.where(
-            ((owner_index ^ place)[:, None] == place[None, :])[..., None],
+            (near_owner(every)[:, None] == every[None, :])[..., None],
             index_all.reshape(1, devices, frame_local),
             0,
         ),
@@ -1058,12 +1143,9 @@
     cond_near = cond_near.astype(low_type)
     cond_own = jax.nn.silu(pre_own).astype(low_type)
     adaptive_low = adaptive_master.astype(low_type)
-    adapt_parts = lax.all_to_all(
-        product(cond_own, adaptive_low).reshape(devices, frame_local, 6 * D), ALL, 0, 0, tiled=True
-    )
-    adapt = jnp.sum(adapt_parts, axis=0)
-    shift_one, scale_one = adapt[:, :D], adapt[:, D : 2 * D]
-    mods = adapt.reshape(frame_local, 6, D)
+    adapt = product(cond_own, adaptive_low).reshape(devices, frame_local, 6 * D)
+    mods = jnp.sum(lax.all_to_all(adapt, ALL, 0, 0, tiled=True), axis=0)
+    mods = mods.reshape(frame_local, 6, D)
 
     my_levels = lax.dynamic_slice_in_dim(
         lax.dynamic_index_in_dim(noise_levels, clip_index, 0, keepdims=False),
@@ -1104,14 +1186,10 @@
 
     alpha_bar, noised, _ = plan(my_levels, my_flags)
     inputs = noised_input(clean_tok, noise_tok, alpha_bar, noised).astype(low_type)
-    patch_turned = first_weights[:, 3 * D : 3 * D + PATCH_FEAT]
-    triple_weight = first_weights
-    hidden_zero = against(inputs, patch_turned)
-    normed, first_back = jax.vjp(modulate, hidden_zero, shift_one, scale_one)
-    normed_low = normed.astype(low_type)
-
     width = D // head_groups
-    heads = triple_heads(normed_low, triple_weight, my_times, spaces, head_groups)
+    hidden_zero, normed_low, heads = triple_heads(
+        inputs, mods, first_weights, my_times, spaces, head_groups
+    )
     heads = lax.all_to_all(heads, head_axes, 0, 0, tiled=True)
     if moved:
         heads = heads.reshape(head_groups, frame_local, FRAME_TOK, 3 * width)
@@ -1158,7 +1236,9 @@
     early_adapt = jnp.concatenate(
         [grad_mods.reshape(frame_local, 3 * D), grad_gate_two.reshape(frame_local, D)], axis=1
     ).astype(low_type)
-    early_adapt = gather_near(early_adapt)
+    early_adapt = gather_near(early_adapt, ("core", "batch"))
+    grad_attended, early_adapt = lax.optimization_barrier((grad_attended, early_adapt))
+    early_adapt = gather_near(early_adapt, ("row",))
 
     second_grads = weight_grads(
         (batch_count, row_count, core_count),
@@ -1203,23 +1283,8 @@
         normed_clip.reshape(-1, D), grad_heads.reshape(head_groups * token_count, 3 * width)
     )
     grad_heads = lax.all_to_all(grad_heads, head_axes, 0, 0, tiled=True)
-    grad_triple_tok = (
-        grad_heads.reshape(head_groups, token_count, 3, width)
-        .transpose(1, 2, 0, 3)
-        .reshape(token_count, 3 * D)
-    )
-    hidden_part, grad_shift_one, grad_scale_one = first_back(
-        against(grad_triple_tok, triple_weight[:, : 3 * D])
-    )
-    late_adapt = gather_near(
-        jnp.concatenate([grad_shift_one, grad_scale_one], axis=1).astype(low_type)
-    )
-    grad_hidden_zero = (grad_hidden_one + hidden_part).astype(low_type)
-    grad_patch = across(grad_hidden_zero, inputs)
-    small_own = halved_sum(
-        jnp.concatenate([grad_patch, grad_readout], axis=1).reshape(devices, -1, LANES)
-    ).reshape(rows, 2 * PATCH_FEAT)
-
+    if not moved:
+        grad_heads = grad_heads.reshape(head_groups, token_count, 3, width).swapaxes(1, 2)
     grad_triple = grad_triple.reshape(batch_count, row_count, core_count, rows, 3 * width)
     if moved:
         grad_triple = grad_triple.transpose(1, 0, 2, 3, 4)
@@ -1227,8 +1292,23 @@
         grad_triple = grad_triple.transpose(0, 2, 1, 3, 4)
     rest_count = devices // head_groups
     triple_own = exchange_sum(
-        grad_triple.reshape(rest_count, head_groups, rows, 3 * width), rest_axes
-    )
+        grad_triple.reshape(rest_count, head_groups, rows, 3 * width),
+        rest_axes,
+        sent=low_type,
+    )
+    grad_heads, triple_own, early_adapt = lax.optimization_barrier(
+        (grad_heads, triple_own, early_adapt)
+    )
+    grad_shift, grad_patch = triple_back(
+        grad_heads, first_weights, hidden_zero, grad_hidden_one, mods, inputs, head_groups
+    )
+    late_adapt = gather_near(grad_shift.reshape(frame_local, 2 * D).astype(low_type))
+    small = jnp.concatenate([grad_patch, grad_readout], axis=1)
+    small = small.reshape(batch_count, row_count, core_count, -1, LANES)
+    small = exchange_sum(small, "core", 2)
+    small = exchange_sum(small, "batch")
+    small_own = exchange_sum(small, "row").reshape(rows, 2 * PATCH_FEAT)
+
     triple_own = lax.all_to_all(triple_own, head_axes, 0, 0, tiled=True)
     triple_own = (
         triple_own.reshape(head_groups, rows, 3, width).transpose(1, 2, 0, 3).reshape(rows, 3 * D)

time: 646 us -> 595 us (0.921)
  waiting for transfers between devices: 241 us -> 193 us
  Pallas kernels: 183 us -> 199 us
  local copies, waits for them, and re-layouts: 56.9 us -> 44.8 us
  matrix products: 21.3 us -> 11.2 us
  starting transfers between devices: 55.6 us -> 65.6 us
  other arithmetic: 39.5 us -> 32.9 us
    ppermute x23 -> x31, waiting for transfers between devices: 84.6 us -> 27.4 us  [the longest x21 26.8 us: swapped(): lax.ppermute(value, axis, [(i, i ^ offset) for i in range(lax.axis_size(a...]
    reduce_scatter x1, waiting for transfers between devices: 0.01 us -> 24.8 us  [per_device(): lax.psum_scatter(second_grads.reshape((-1,) + second_grads.shape[2:]), ('...]
    reduce_scatter x1, waiting for transfers between devices: 15.4 us -> 0.02 us  [per_device(): lax.psum_scatter(second_own, 'row', scatter_dimension=0).astype(jnp.float32)]
    pallas_call x1 -> x2, Pallas kernels: 9.82 us -> 25.1 us  [the longest x1 13.8 us: triple_back(): pl.pallas_call(triple_back_kernel, grid=(3 * D // BLOCK,), in_specs=[head...]
    ppermute x23 -> x31, starting transfers between devices: 31.2 us -> 41.5 us  [the longest x21 26.8 us: swapped(): lax.ppermute(value, axis, [(i, i ^ offset) for i in range(lax.axis_size(a...]
    dot_general x4 -> x2, matrix products: 10.4 us -> 0.45 us  [against(): lax.dot_general(left, right, (((1,), (1,)), ((), ())), preferred_element_...]
    all_to_all x1, waiting for transfers between devices: 7.14 us -> 0.01 us  [per_device(): grad_attended = lax.all_to_all(grad_attended, head_axes, 0, 0, tiled=True)]
    unnamed x175 -> x170, local copies, waits for them, and re-layouts: 17.3 us -> 17.6 us
  transfers between devices with their start and end apart: 34 -> 42, of which waited for: 23 -> 20; matrix products, arithmetic and copies ran while one was open for 12% -> 8% of each run, Pallas kernels for 29% -> 34%
where the time goes in v3:
time: 595 us; the launch traced here: 587 us
  Pallas kernels  199 us (33%)
  waiting for transfers between devices  193 us (32%)
  starting transfers between devices  65.6 us (11%)
  local copies, waits for them, and re-layouts  44.8 us (8%)
  other arithmetic  32.9 us (6%)
  between operations  23 us (4%)
  blocking collectives  17.8 us (3%)
  matrix products  11.2 us (2%)
    pallas_call x1, Pallas kernels, attend_back(): pl.pallas_call(attend_back_kernel, grid_spec=pltpu.PrefetchScalarGridSpec...  66.6 us
    all_to_all x1, waiting for transfers between devices, per_device(): heads = lax.all_to_all(heads, head_axes, 0, 0, tiled=True)  53.4 us
    all_to_all x1, waiting for transfers between devices, per_device(): mods = jnp.sum(lax.all_to_all(adapt, ALL, 0, 0, tiled=True), axis=0)  47.4 us
    pallas_call x1, Pallas kernels, attend(): pl.pallas_call(attend_kernel, grid_spec=pltpu.PrefetchScalarGridSpec(num_...  43.2 us
    all_gather x1, waiting for transfers between devices, per_device(): first_weights = lax.all_gather(first_weights, ALL, axis=0, tiled=True)  30.7 us
    ppermute x21, waiting for transfers between devices, swapped(): lax.ppermute(value, axis, [(i, i ^ offset) for i in range(lax.axis_size(a...  26.8 us
    ppermute x21, starting transfers between devices, swapped(): lax.ppermute(value, axis, [(i, i ^ offset) for i in range(lax.axis_size(a...  26.8 us
    reduce_scatter x1, waiting for transfers between devices, per_device(): lax.psum_scatter(second_grads.reshape((-1,) + second_grads.shape[2:]), ('...  24.8 us
  transfers between devices with their start and end apart: 42, of which 20 were waited for; matrix products, arithmetic and copies ran while one was open for 8% of the time, Pallas kernels for 34%

profile of v3, /device:TPU:0, one launch (start us, length us, event | category | flops | bytes accessed | tf_op | source)
XLA Modules:
  0.0 587.4 jit_solution(1689975495353728461)
XLA Ops:
  16.9 7.3 %all-to-all-start = ((f32[32,2,6144]{2,1,0:T(2,128)}), f32[32,2,6144]{2,1,0:T(2,128)S(1)}, u32[]{:S(2)}, u32[]{:S(2)}) async-start(f32[32,2,6144]{2,1,0:T(2,128)} %reshape.689), calls=%async_computation | async-start | bytes 3145728 | tf_op jit(solution)/shard_map/all_to_all | solution.py:1147
  28.0 47.4 %all-to-all-done = f32[32,2,6144]{2,1,0:T(2,128)S(1)} async-done(((f32[32,2,6144]{2,1,0:T(2,128)}), f32[32,2,6144]{2,1,0:T(2,128)S(1)}, u32[]{:S(2)}, u32[]{:S(2)}) %all-to-all-start) | async-done | bytes 1572896 | tf_op jit(solution)/shard_map/all_to_all | solution.py:1147
  76.0 30.7 %all-gather.5.cloned.1.call-done.extra_ref.weight_ref.readout_ref = bf16[1024,3200]{1,0:T(8,128)(2,1)} async-done(((bf16[32,3200]{1,0:T(8,128)(2,1)}), bf16[1024,3200]{1,0:T(8,128)(2,1)}) %all-gather.5.cloned.1.call-update) | async-done | bytes 6553616 | tf_op jit(solution)/shard_map/all_gather | solution.py:1105
  106.7 2.9 copy-done.10
  109.5 11.3 %triple_heads.1 = (f32[512,1024]{1,0:T(8,128)S(1)}, bf16[512,1024]{1,0:T(8,128)(2,1)S(1)}, bf16[8,512,384]{2,1,0:T(8,128)(2,1)}) custom-call(bf16[512,16]{1,0:T(8,128)(2,1)S(1)} %get-tuple-element.281.inputs_ref, bf16[1024,3200]{1,0:T(8,128)(2,1)S(1)} %copy-done.10, f32[2,6,1024]{2,1,0:T(8,128)S(1)} %reshape.690.mods_ref, bf16[1024,3200]{1,0:T(8,128)(2,1)S(1)} %copy-done.10, ...), custom_call_target="tpu_custom_call" | custom-call | flops 13200000000 | bytes 1048576 | tf_op jit(solution)/shard_map/triple_heads/pallas_call | solution.py:225
  121.9 4.5 all-to-all-start.1
  127.7 53.4 %all-to-all-done.1 = bf16[8,512,384]{2,1,0:T(8,128)(2,1)} async-done(((bf16[8,512,384]{2,1,0:T(8,128)(2,1)}), bf16[8,512,384]{2,1,0:T(8,128)(2,1)}, u32[]{:S(2)}, u32[]{:S(2)}) %all-to-all-start.1) | async-done | bytes 3145760 | tf_op jit(solution)/shard_map/all_to_all | solution.py:1193
  181.1 43.2 %attend.1 = (bf16[8,2,256,128]{3,2,1,0:T(8,128)(2,1)S(1)}, f32[16,128,256]{2,1,0:T(8,128)S(1)}, f32[16,1,512]{2,1,0:T(1,128)S(1)}) custom-call(s32[16]{0:T(128)S(1)} %get-tuple-element.307.order_ref, s32[16]{0:T(128)S(1)} %get-tuple-element.240.count_ref, bf16[8,2,256,384]{3,2,1,0:T(8,128)(2,1)} %bitcast.7.query_ref.key_ref.value_ref, ...), custom_call_target="tpu_custom_call" | custom-call | flops 49500000256 | bytes 1048576 | tf_op jit(solution)/shard_map/attend/pallas_call | solution.py:445
  224.9 17.8 %all_to_all.30.heads_ref = bf16[8,512,128]{2,1,0:T(8,128)(2,1)S(1)} all-to-all(bf16[8,512,128]{2,1,0:T(8,128)(2,1)S(1)} %bitcast.144), channel_id=1, replica_groups=mesh['batch'=4,'row'=4,'core'=2] {'batch','core'}, dimensions={0} | all-to-all | bytes 2097152 | tf_op jit(solution)/shard_map/all_to_all | solution.py:1204
  245.1 6.7 %all-gather.9.cloned.1.call-done = bf16[9216,1024]{1,0:T(8,128)(2,1)} async-done(((bf16[288,1024]{1,0:T(8,128)(2,1)}), bf16[9216,1024]{1,0:T(8,128)(2,1)}) %all-gather.9.cloned.1.call-update) | async-done | bytes 18874384 | tf_op jit(solution)/shard_map/all_gather | solution.py:1111
  251.8 3.7 project_norm.1
  260.2 20.5 %feed_forward.1 = (f32[512,4096]{1,0:T(8,128)}, bf16[512,4096]{1,0:T(8,128)(2,1)}, f32[512,1024]{1,0:T(8,128)}, bf16[512,1024]{1,0:T(8,128)(2,1)}, f32[1024,16]{...) custom-call(f32[2]{0:T(128)} %fusion.56.scale_ref, bf16[512,1024]{1,0:T(8,128)(2,1)} %copy-done.14, ...), custom_call_target="tpu_custom_call" | custom-call | flops 22000001024 | bytes 1048576 | tf_op jit(solution)/shard_map/feed_forward/pallas_call | solution.py:764
  280.6 23.3 %feed_backward.1 = (bf16[512,4096]{1,0:T(8,128)(2,1)}, f32[512,1024]{1,0:T(8,128)}, bf16[512,1024]{1,0:T(8,128)(2,1)}, bf16[8,512,128]{2,1,0:T(8,128)(2,1)}, f32[2,3,1024]{2,1,0:T(4,128)}) custom-call(bf16[512,1024]{1,0:T(8,128)(2,1)} %get-tuple-element.103.grad_outer_ref, bf16[32,288,1024]{2,1,0:T(8,128)(2,1)} %bitcast.149, ...), custom_call_target="tpu_custom_call" | custom-call | flops 24199999488 | bytes 1048576 | tf_op jit(solution)/shard_map/feed_backward/pallas_call | solution.py:871
  304.0 16.6 %weight_grads.1 = bf16[4,2,4,288,1024]{4,3,2,1,0:T(8,128)(2,1)} custom-call(bf16[512,4096]{1,0:T(8,128)(2,1)} %get-tuple-element.122.active_ref, bf16[512,1024]{1,0:T(8,128)(2,1)} %get-tuple-element.103.grad_outer_ref, bf16[512,1024]{1,0:T(8,128)(2,1)} %copy-done.13, bf16[512,1024]{1,0:T(8,128)(2,1)} %get-tuple-element.124.grad_branch_ref, ...), custom_call_target="tpu_custom_call" | custom-call | flops 30799998976 | bytes 1048576 | tf_op jit(solution)/shard_map/weight_grads/pallas_call | solution.py:936
  322.2 3.7 all-to-all-start.3
  331.4 10.0 %collective-permute-done.2 = bf16[4,4096]{1,0:T(4,128)(2,1)S(1)} collective-permute-done((bf16[4,4096]{1,0:T(4,128)(2,1)S(1)}, bf16[4,4096]{1,0:T(4,128)(2,1)S(1)}, u32[]{:S(2)}, u32[]{:S(2)}) %collective-permute-start.2) | collective-permute-done | bytes 32800 | tf_op jit(solution)/shard_map/ppermute | solution.py:956
  343.8 66.6 %attend_back.1 = bf16[8,2,256,384]{3,2,1,0:T(8,128)(2,1)} custom-call(s32[16]{0:T(128)} %get-tuple-element.306.order_ref, s32[16]{0:T(128)} %get-tuple-element.238.count_ref, bf16[8,2,256,384]{3,2,1,0:T(8,128)(2,1)} %bitcast.7.query_ref.key_ref.value_ref, bf16[8,2,256,384]{3,2,1,0:T(8,128)(2,1)} %bitcast.7.query_ref.key_ref.value_ref, ...), custom_call_target="tpu_custom_call" | custom-call | flops 71499997184 | bytes 1048576 | tf_op jit(solution)/shard_map/attend_back/pallas_call | solution.py:621
  410.4 3.8 all-to-all-start.4
  414.5 11.4 %copy.186 = bf16[1024,4096]{1,0:T(8,128)(2,1)} copy(bf16[1024,4096]{0,1:T(8,128)(2,1)} %bitcast.152) | data formatting | bytes 16777216 | tf_op jit(solution)/shard_map/dot_general | solution.py:39
  428.6 2.8 collective-permute-start.10
  433.0 8.2 %convolution_bitcast_fusion = f32[4,4,2,32,384]{4,3,2,0,1:T(8,128)S(1)} fusion(bf16[4,4,2,32,4096]{4,3,2,1,0:T(8,128)(2,1)} %bitcast.153, bf16[4096,384,1,1,1]{1,0,4,3,2:T(8,128)(2,1)} %bitcast.157), kind=kOutput, calls=%fused_computation | convolution fusion | flops 3221225472 | bytes 13107200 | tf_op jit(solution)/shard_map/dot_general | solution.py:39
  447.5 24.8 %reduce-scatter.3.cloned.1.call-done = bf16[1,4,288,1024]{3,2,1,0:T(8,128)(2,1)} async-done(((bf16[8,4,288,1024]{3,2,1,0:T(8,128)(2,1)}), bf16[1,4,288,1024]{3,2,1,0:T(8,128)(2,1)}) %reduce-scatter.3.cloned.1.call-update) | async-done | bytes 2359312 | tf_op jit(solution)/shard_map/reduce_scatter | solution.py:1252
  474.5 2.7 all-to-all-done.4.grads_ref
  480.4 13.8 %triple_back.1 = (f32[2,2,1024]{2,1,0:T(2,128)S(1)}, f32[1024,16]{1,0:T(8,128)S(1)}) custom-call(bf16[8,512,384]{2,1,0:T(8,128)(2,1)S(1)} %all-to-all-done.4.grads_ref, bf16[1024,3200]{1,0:T(8,128)(2,1)} %all-gather.5.cloned.1.call-done.extra_ref.weight_ref.readout_ref, f32[512,1024]{1,0:T(8,128)S(1)} %copy-done.1, f32[512,1024]{1,0:T(8,128)S(1)} %copy-done.15, ...), custom_call_target="tpu_custom_call" | custom-call | flops 13200000000 | bytes 1048576 | tf_op jit(solution)/shard_map/triple_back/pallas_call | solution.py:297
  498.1 4.0 collective-permute-start.14
  512.3 3.5 all-to-all-start.5
  516.2 2.9 collective-permute-start.23
  521.9 3.5 collective-permute-done.22
  551.2 2.7 collective-permute-done.28
  554.5 3.7 collective-permute-start.30
  560.6 3.0 collective-permute-done.31
  569.7 3.3 multiply_subtract_fusion
  (348 shorter events, 100.7 us)
Async XLA Ops:
  7.3 99.4 %all-gather.5.cloned.1.call-start = ((), (), s32[]{:S(2)}) async-start(), calls=%async_computation.8 | async-start | bytes 6758400 | tf_op jit(solution)/shard_map/all_gather | solution.py:1105
  10.8 241.0 %all-gather.9.cloned.1.call-start = ((), (), s32[]{:S(2)}) async-start(), calls=%async_computation.12 | async-start | bytes 19464192 | tf_op jit(solution)/shard_map/all_gather | solution.py:1111
  16.9 58.5 %all-to-all-start = ((f32[32,2,6144]{2,1,0:T(2,128)}), f32[32,2,6144]{2,1,0:T(2,128)S(1)}, u32[]{:S(2)}, u32[]{:S(2)}) async-start(f32[32,2,6144]{2,1,0:T(2,128)} %reshape.689), calls=%async_computation | async-start | bytes 3145728 | tf_op jit(solution)/shard_map/all_to_all | solution.py:1147
  121.9 59.2 %all-to-all-start.1 = ((bf16[8,512,384]{2,1,0:T(8,128)(2,1)}), bf16[8,512,384]{2,1,0:T(8,128)(2,1)}, u32[]{:S(2)}, u32[]{:S(2)}) async-start(bf16[8,512,384]{2,1,0:T(8,128)(2,1)} %get-tuple-element.95), calls=%async_computation.1 | async-start | bytes 6291456 | tf_op jit(solution)/shard_map/all_to_all | solution.py:1193
  126.3 288.1 %all-gather.7.cloned.1.call-start = ((), (), s32[]{:S(2)}) async-start(), calls=%async_computation.9 | async-start | bytes 9437184 | tf_op jit(solution)/shard_map/all_gather | solution.py:1206
  242.7 229.6 %reduce-scatter.3.cloned.1.call-start = ((), (), s32[]{:S(2)}) async-start(), calls=%async_computation.10 | async-start | bytes 21233664 | tf_op jit(solution)/shard_map/reduce_scatter | solution.py:1252
  322.2 20.7 %all-to-all-start.3 = ((bf16[8,512,128]{2,1,0:T(8,128)(2,1)}), bf16[8,512,128]{2,1,0:T(8,128)(2,1)S(1)}, u32[]{:S(2)}, u32[]{:S(2)}) async-start(bf16[8,512,128]{2,1,0:T(8,128)(2,1)} %get-tuple-element.107), calls=%async_computation.3 | async-start | bytes 2097152 | tf_op jit(solution)/shard_map/all_to_all | solution.py:1234
  327.4 14.0 %collective-permute-start.2 = (bf16[4,4096]{1,0:T(4,128)(2,1)S(1)}, bf16[4,4096]{1,0:T(4,128)(2,1)S(1)}, u32[]{:S(2)}, u32[]{:S(2)}) collective-permute-start(bf16[4,4096]{1,0:T(4,128)(2,1)S(1)} %pad_maximum_fusion.5), channel_id=1, source_target_pairs={{0,8},{8,0},{16,24},{24,16},{1,9},{9,1},{17,25},{25,17},{2,10},{10... | collective-permute-start | bytes 98312 | tf_op jit(solution)/shard_map/ppermute | solution.py:956
  329.4 12.1 %collective-permute-start.3 = (bf16[4,4096]{1,0:T(4,128)(2,1)S(1)}, bf16[4,4096]{1,0:T(4,128)(2,1)S(1)}, u32[]{:S(2)}, u32[]{:S(2)}) collective-permute-start(bf16[4,4096]{1,0:T(4,128)(2,1)S(1)} %pad_maximum_fusion.5), channel_id=1, source_target_pairs={{0,16},{8,24},{16,0},{24,8},{1,17},{9,25},{17,1},{25,9},{2,18},{10... | collective-permute-start | bytes 98312 | tf_op jit(solution)/shard_map/ppermute | solution.py:956
  330.8 11.8 %collective-permute-start.4 = (bf16[4,4096]{1,0:T(4,128)(2,1)S(1)}, bf16[4,4096]{1,0:T(4,128)(2,1)S(1)}, u32[]{:S(2)}, u32[]{:S(2)}) collective-permute-start(bf16[4,4096]{1,0:T(4,128)(2,1)S(1)} %pad_maximum_fusion.5), channel_id=1, source_target_pairs={{0,24},{8,16},{16,8},{24,0},{1,25},{9,17},{17,9},{25,1},{2,26},{10... | collective-permute-start | bytes 98312 | tf_op jit(solution)/shard_map/ppermute | solution.py:956
  410.4 66.8 %all-to-all-start.4 = ((bf16[8,512,384]{2,1,0:T(8,128)(2,1)}), bf16[8,512,384]{2,1,0:T(8,128)(2,1)S(1)}, u32[]{:S(2)}, u32[]{:S(2)}) async-start(bf16[8,512,384]{2,1,0:T(8,128)(2,1)} %bitcast.156), calls=%async_computation.4 | async-start | bytes 6291456 | tf_op jit(solution)/shard_map/all_to_all | solution.py:1285
  414.2 120.4 %reduce-scatter.5.cloned.1.call-start = ((), (), s32[]{:S(2)}) async-start(), calls=%async_computation.11 | async-start | bytes 2949120 | tf_op jit(solution)/shard_map/reduce_scatter | solution.py:1257
  428.6 16.2 %collective-permute-start.10 = (bf16[16,4096]{1,0:T(8,128)(2,1)S(1)}, bf16[16,4096]{1,0:T(8,128)(2,1)S(1)}, u32[]{:S(2)}, u32[]{:S(2)}) collective-permute-start(bf16[16,4096]{1,0:T(8,128)(2,1)S(1)} %concatenate.54), channel_id=1, source_target_pairs={{0,6},{2,4},{4,2},{6,0},{1,7},{3,5},{5,3},{7,1},{8,14},{10,12},{12... | collective-permute-start | bytes 393224 | tf_op jit(solution)/shard_map/ppermute | solution.py:956
  431.4 15.3 %collective-permute-start.9 = (bf16[16,4096]{1,0:T(8,128)(2,1)S(1)}, bf16[16,4096]{1,0:T(8,128)(2,1)S(1)}, u32[]{:S(2)}, u32[]{:S(2)}) collective-permute-start(bf16[16,4096]{1,0:T(8,128)(2,1)S(1)} %concatenate.54), channel_id=1, source_target_pairs={{0,4},{2,6},{4,0},{6,2},{1,5},{3,7},{5,1},{7,3},{8,12},{10,14},{12... | collective-permute-start | bytes 393224 | tf_op jit(solution)/shard_map/ppermute | solution.py:956
  431.4 15.3 %collective-permute-start.8 = (bf16[16,4096]{1,0:T(8,128)(2,1)S(1)}, bf16[16,4096]{1,0:T(8,128)(2,1)S(1)}, u32[]{:S(2)}, u32[]{:S(2)}) collective-permute-start(bf16[16,4096]{1,0:T(8,128)(2,1)S(1)} %concatenate.54), channel_id=1, source_target_pairs={{0,2},{2,0},{4,6},{6,4},{1,3},{3,1},{5,7},{7,5},{8,10},{10,8},{12,... | collective-permute-start | bytes 393224 | tf_op jit(solution)/shard_map/ppermute | solution.py:956
  442.3 30.1 %collective-permute-start.7 = (bf16[8,32,384]{2,1,0:T(8,128)(2,1)}, bf16[8,32,384]{2,1,0:T(8,128)(2,1)}, u32[]{:S(2)}, u32[]{:S(2)}) collective-permute-start(bf16[8,32,384]{2,1,0:T(8,128)(2,1)} %get-tuple-element.273), channel_id=1, source_target_pairs={{0,6},{2,4},{4,2},{6,0},{1,7},{3,5},{5,3},{7,1},{8,14},{10,12},{12... | collective-permute-start | bytes 589832 | tf_op jit(solution)/shard_map/ppermute | solution.py:981
  444.7 27.6 %collective-permute-start.6 = (bf16[8,32,384]{2,1,0:T(8,128)(2,1)}, bf16[8,32,384]{2,1,0:T(8,128)(2,1)}, u32[]{:S(2)}, u32[]{:S(2)}) collective-permute-start(bf16[8,32,384]{2,1,0:T(8,128)(2,1)} %get-tuple-element.274), channel_id=1, source_target_pairs={{0,4},{2,6},{4,0},{6,2},{1,5},{3,7},{5,1},{7,3},{8,12},{10,14},{12... | collective-permute-start | bytes 589832 | tf_op jit(solution)/shard_map/ppermute | solution.py:981
  444.7 27.6 %collective-permute-start.5 = (bf16[8,32,384]{2,1,0:T(8,128)(2,1)}, bf16[8,32,384]{2,1,0:T(8,128)(2,1)}, u32[]{:S(2)}, u32[]{:S(2)}) collective-permute-start(bf16[8,32,384]{2,1,0:T(8,128)(2,1)} %get-tuple-element.272), channel_id=1, source_target_pairs={{0,2},{2,0},{4,6},{6,4},{1,3},{3,1},{5,7},{7,5},{8,10},{10,8},{12,... | collective-permute-start | bytes 589832 | tf_op jit(solution)/shard_map/ppermute | solution.py:981
  496.8 7.0 %collective-permute-start.18 = (bf16[2,2048]{1,0:T(2,128)(2,1)S(1)}, bf16[2,2048]{1,0:T(2,128)(2,1)S(1)}, u32[]{:S(2)}, u32[]{:S(2)}) collective-permute-start(bf16[2,2048]{1,0:T(2,128)(2,1)S(1)} %bitcast.162), channel_id=1, source_target_pairs={{0,1},{1,0},{2,3},{3,2},{4,5},{5,4},{6,7},{7,6},{8,9},{9,8},{10,11... | collective-permute-start | bytes 24584 | tf_op jit(solution)/shard_map/ppermute | solution.py:956
  498.1 8.2 %collective-permute-start.14 = (f32[4,8,128]{2,1,0:T(8,128)S(1)}, f32[4,8,128]{2,1,0:T(8,128)S(1)}, u32[]{:S(2)}, u32[]{:S(2)}) collective-permute-start(f32[4,8,128]{2,1,0:T(8,128)S(1)} %get-tuple-element.283), channel_id=1, source_target_pairs={{0,24},{8,16},{16,8},{24,0},{1,25},{9,17},{17,9},{25,1},{2,26},{10... | collective-permute-start | bytes 49160 | tf_op jit(solution)/shard_map/ppermute | solution.py:981
  502.1 5.4 collective-permute-start.13
  503.9 6.4 %collective-permute-start.19 = (bf16[4,2048]{1,0:T(4,128)(2,1)S(1)}, bf16[4,2048]{1,0:T(4,128)(2,1)S(1)}, u32[]{:S(2)}, u32[]{:S(2)}) collective-permute-start(bf16[4,2048]{1,0:T(4,128)(2,1)S(1)} %pad_maximum_fusion.7), channel_id=1, source_target_pairs={{0,8},{8,0},{16,24},{24,16},{1,9},{9,1},{17,25},{25,17},{2,10},{10... | collective-permute-start | bytes 49160 | tf_op jit(solution)/shard_map/ppermute | solution.py:956
  505.9 9.8 %collective-permute-start.20 = (bf16[4,2048]{1,0:T(4,128)(2,1)S(1)}, bf16[4,2048]{1,0:T(4,128)(2,1)S(1)}, u32[]{:S(2)}, u32[]{:S(2)}) collective-permute-start(bf16[4,2048]{1,0:T(4,128)(2,1)S(1)} %pad_maximum_fusion.7), channel_id=1, source_target_pairs={{0,16},{8,24},{16,0},{24,8},{1,17},{9,25},{17,1},{25,9},{2,18},{10... | collective-permute-start | bytes 49160 | tf_op jit(solution)/shard_map/ppermute | solution.py:956
  506.2 9.6 %collective-permute-start.21 = (bf16[4,2048]{1,0:T(4,128)(2,1)S(1)}, bf16[4,2048]{1,0:T(4,128)(2,1)S(1)}, u32[]{:S(2)}, u32[]{:S(2)}) collective-permute-start(bf16[4,2048]{1,0:T(4,128)(2,1)S(1)} %pad_maximum_fusion.7), channel_id=1, source_target_pairs={{0,24},{8,16},{16,8},{24,0},{1,25},{9,17},{17,9},{25,1},{2,26},{10... | collective-permute-start | bytes 49160 | tf_op jit(solution)/shard_map/ppermute | solution.py:956
  507.6 11.6 %collective-permute-start.17 = (f32[8,128]{1,0:T(8,128)S(1)}, f32[8,128]{1,0:T(8,128)S(1)}, u32[]{:S(2)}, u32[]{:S(2)}) collective-permute-start(f32[8,128]{1,0:T(8,128)S(1)} %get-tuple-element.288), channel_id=1, source_target_pairs={{0,6},{2,4},{4,2},{6,0},{1,7},{3,5},{5,3},{7,1},{8,14},{10,12},{12... | collective-permute-start | bytes 12296 | tf_op jit(solution)/shard_map/ppermute | solution.py:981
  510.3 10.1 %collective-permute-start.16 = (f32[8,128]{1,0:T(8,128)S(1)}, f32[8,128]{1,0:T(8,128)S(1)}, u32[]{:S(2)}, u32[]{:S(2)}) collective-permute-start(f32[8,128]{1,0:T(8,128)S(1)} %get-tuple-element.289), channel_id=1, source_target_pairs={{0,4},{2,6},{4,0},{6,2},{1,5},{3,7},{5,1},{7,3},{8,12},{10,14},{12... | collective-permute-start | bytes 12296 | tf_op jit(solution)/shard_map/ppermute | solution.py:981
  510.3 10.1 %collective-permute-start.15 = (f32[8,128]{1,0:T(8,128)S(1)}, f32[8,128]{1,0:T(8,128)S(1)}, u32[]{:S(2)}, u32[]{:S(2)}) collective-permute-start(f32[8,128]{1,0:T(8,128)S(1)} %get-tuple-element.287), channel_id=1, source_target_pairs={{0,2},{2,0},{4,6},{6,4},{1,3},{3,1},{5,7},{7,5},{8,10},{10,8},{12,... | collective-permute-start | bytes 12296 | tf_op jit(solution)/shard_map/ppermute | solution.py:981
  512.3 20.9 %all-to-all-start.5 = ((f32[8,32,384]{2,1,0:T(8,128)}), f32[8,32,384]{2,1,0:T(8,128)S(1)}, u32[]{:S(2)}, u32[]{:S(2)}) async-start(f32[8,32,384]{2,1,0:T(8,128)} %fusion.7), calls=%async_computation.5 | async-start | bytes 786432 | tf_op jit(solution)/shard_map/all_to_all | solution.py:1312
  515.9 9.5 %collective-permute-start.22 = (bf16[16,2048]{1,0:T(8,128)(2,1)S(1)}, bf16[16,2048]{1,0:T(8,128)(2,1)S(1)}, u32[]{:S(2)}, u32[]{:S(2)}) collective-permute-start(bf16[16,2048]{1,0:T(8,128)(2,1)S(1)} %concatenate.58), channel_id=1, source_target_pairs={{0,2},{2,0},{4,6},{6,4},{1,3},{3,1},{5,7},{7,5},{8,10},{10,8},{12,... | collective-permute-start | bytes 196616 | tf_op jit(solution)/shard_map/ppermute | solution.py:956
  516.2 11.1 %collective-permute-start.23 = (bf16[16,2048]{1,0:T(8,128)(2,1)S(1)}, bf16[16,2048]{1,0:T(8,128)(2,1)S(1)}, u32[]{:S(2)}, u32[]{:S(2)}) collective-permute-start(bf16[16,2048]{1,0:T(8,128)(2,1)S(1)} %concatenate.58), channel_id=1, source_target_pairs={{0,4},{2,6},{4,0},{6,2},{1,5},{3,7},{5,1},{7,3},{8,12},{10,14},{12... | collective-permute-start | bytes 196616 | tf_op jit(solution)/shard_map/ppermute | solution.py:956
  519.2 9.4 %collective-permute-start.24 = (bf16[16,2048]{1,0:T(8,128)(2,1)S(1)}, bf16[16,2048]{1,0:T(8,128)(2,1)S(1)}, u32[]{:S(2)}, u32[]{:S(2)}) collective-permute-start(bf16[16,2048]{1,0:T(8,128)(2,1)S(1)} %concatenate.58), channel_id=1, source_target_pairs={{0,6},{2,4},{4,2},{6,0},{1,7},{3,5},{5,3},{7,1},{8,14},{10,12},{12... | collective-permute-start | bytes 196616 | tf_op jit(solution)/shard_map/ppermute | solution.py:956
  554.5 6.1 %collective-permute-start.30 = (f32[8,128]{1,0:T(8,128)S(1)}, f32[8,128]{1,0:T(8,128)S(1)}, u32[]{:S(2)}, u32[]{:S(2)}) collective-permute-start(f32[8,128]{1,0:T(8,128)S(1)} %add_add_fusion.1), channel_id=1, source_target_pairs={{0,4},{2,6},{4,0},{6,2},{1,5},{3,7},{5,1},{7,3},{8,12},{10,14},{12... | collective-permute-start | bytes 12296 | tf_op jit(solution)/shard_map/ppermute | solution.py:956
  (88 other events, 1609.9 us)
Sparse Core Ops, SparseCore 0:
  11.5 95.0 all-gather.4
  110.2 141.4 all-gather.8
  253.7 53.3 all-gather.6
  320.7 151.5 reduce-scatter.2
  474.5 57.1 reduce-scatter.4

commit v4 on v3

--- a/solution.py
+++ b/solution.py
@@ -687,7 +687,7 @@
         ],
         out_specs=[by_frame] * 4,
         out_shape=[low, wide, wide, low],
-        compiler_params=pltpu.CompilerParams(vmem_limit_bytes=40 * 1024 * 1024),
+        compiler_params=pltpu.CompilerParams(vmem_limit_bytes=60 * 1024 * 1024),
         cost_estimate=about(4),
         name="project_norm",
     )(heads, weights, hidden, mods)
@@ -795,7 +795,7 @@
             jax.ShapeDtypeStruct((frames, 1, D), jnp.float32),
             jax.ShapeDtypeStruct((frames, 1, LANES), jnp.float32),
         ],
-        compiler_params=pltpu.CompilerParams(vmem_limit_bytes=56 * 1024 * 1024),
+        compiler_params=pltpu.CompilerParams(vmem_limit_bytes=60 * 1024 * 1024),
         cost_estimate=about(20),
         name="feed_forward",
     )(loss_scale, mixed, weights, weights, hidden, mods, first_weights, noise)
@@ -897,7 +897,7 @@
             jax.ShapeDtypeStruct((frames, 3, D), jnp.float32),
         ],
         scratch_shapes=[pltpu.VMEM((tokens, D), jnp.float32)],
-        compiler_params=pltpu.CompilerParams(vmem_limit_bytes=58 * 1024 * 1024),
+        compiler_params=pltpu.CompilerParams(vmem_limit_bytes=60 * 1024 * 1024),
         cost_estimate=about(22),
         name="feed_backward",
     )(grad_outer, weights, weights, inner, hidden, grad_hidden, branch, mods, weights)
@@ -950,6 +950,38 @@
         cost_estimate=about(28),
         name="weight_grads",
     )(active, grad_outer, attended, grad_branch, mixed, grad_inner)
+
+
+def update_kernel(rates, factor_ref, *refs):
+    for item, rate in enumerate(rates):
+        master, first, second, gradient = (refs[4 * item + part][...] for part in range(4))
+        new = adamw_update(master, first, second, gradient, factor_ref[0], rate)
+        for part in range(3):
+            refs[4 * len(rates) + 3 * item + part][...] = new[part]
+
+
+def update(factor, states, rates):
+    flat = [array for state in states for array in state]
+    steps = 4
+    specs = [
+        pl.BlockSpec((array.shape[0], array.shape[1] // steps), lambda i, *_: (0, i))
+        for array in flat
+    ]
+    outs = [4 * item + part for item in range(len(states)) for part in (1, 2, 0)]
+    new = pl.pallas_call(
+        functools.partial(update_kernel, rates),
+        grid_spec=pltpu.PrefetchScalarGridSpec(
+            num_scalar_prefetch=1,
+            grid=(steps,),
+            in_specs=specs,
+            out_specs=[specs[out] for out in outs],
+        ),
+        out_shape=[jax.ShapeDtypeStruct(flat[out].shape, jnp.float32) for out in outs],
+        compiler_params=pltpu.CompilerParams(vmem_limit_bytes=60 * 1024 * 1024),
+        cost_estimate=about(7),
+        name="update",
+    )(factor.reshape(1), *flat)
+    return [new[3 * item : 3 * item + 3] for item in range(len(states))]
 
 
 def swapped(value, axis, offset):
@@ -1254,7 +1286,6 @@
         ("batch", "core"),
         scatter_dimension=0,
     )
-    second_own = lax.psum_scatter(second_own, "row", scatter_dimension=0).astype(jnp.float32)
 
     grads = attend_back(
         query_order,
@@ -1302,6 +1333,8 @@
     grad_shift, grad_patch = triple_back(
         grad_heads, first_weights, hidden_zero, grad_hidden_one, mods, inputs, head_groups
     )
+    second_own, grad_shift = lax.optimization_barrier((second_own, grad_shift))
+    second_own = lax.psum_scatter(second_own, "row", scatter_dimension=0).astype(jnp.float32)
     late_adapt = gather_near(grad_shift.reshape(frame_local, 2 * D).astype(low_type))
     small = jnp.concatenate([grad_patch, grad_readout], axis=1)
     small = small.reshape(batch_count, row_count, core_count, -1, LANES)
@@ -1345,23 +1378,32 @@
         second_own[: FF // D * rows],
         small_own[:, PATCH_FEAT:],
     )
-    squares = sum((jnp.sum(gradient * gradient) for gradient in reduced))
-    level_hits = (my_levels[:, None] == jnp.arange(NB, dtype=jnp.int32)[None, :]).astype(
-        jnp.float32
-    )
-    bucket_local = jnp.sum(level_hits * frame_loss[:, None], axis=0)
-    sums = jnp.zeros((8, LANES), jnp.float32)
-    sums = sums.at[0, :NB].set(bucket_local)
-    sums = sums.at[1, 0].set(squares)
-    sums = sums.at[2, 0].set(jnp.sum(frame_loss))
+    squares = sum(
+        jnp.sum(gradient * gradient)
+        for gradient in (small_own, table_own, adapt_own, triple_own, second_own)
+    )
+    lane = jnp.arange(LANES, dtype=jnp.int32)
+    bucket_lanes = jnp.sum(
+        jnp.where(my_levels[:, None] == lane[None], frame_loss[:, None], 0.0), axis=0
+    )
+    sums = jnp.stack(
+        [bucket_lanes, jnp.full((LANES,), squares), jnp.full((LANES,), jnp.sum(frame_loss))]
+    )
     sums = total_sum(sums)
     clip_norm = jnp.sqrt(sums[1, 0])
     factor = jnp.minimum(1.0, clip_bound / clip_norm)
+    states = [
+        (masters[item], firsts[item], seconds[item], reduced[item]) for item in range(len(reduced))
+    ]
+    large = (2, 3, 4, 5, 6)
+    updated = update(
+        factor, [states[item] for item in large], tuple(learn_rates[item] for item in large)
+    )
     new = [
-        adamw_update(
-            masters[item], firsts[item], seconds[item], reduced[item], factor, learn_rates[item]
-        )
-        for item in range(8)
+        updated[large.index(item)]
+        if item in large
+        else adamw_update(*states[item], factor, learn_rates[item])
+        for item in range(len(states))
     ]
     return (sums[2, 0], frame_count, sums[0, :NB], clip_norm) + tuple(
         item for triple in new for item in triple

time: 595 us -> 581 us (0.976); the launches traced: 587 us -> 580 us
  other arithmetic: 32.9 us -> 21.6 us
  Pallas kernels: 199 us -> 210 us
  waiting for transfers between devices: 193 us -> 203 us
  local copies, waits for them, and re-layouts: 44.8 us -> 36 us
    reduce_scatter x1, waiting for transfers between devices: 24.8 us -> 0.02 us  [per_device(): lax.psum_scatter(second_grads.reshape((-1,) + second_grads.shape[2:]), ('...]
    all_to_all x1, waiting for transfers between devices: 2.74 us -> 19.7 us  [per_device(): grad_heads = lax.all_to_all(grad_heads, head_axes, 0, 0, tiled=True)]
    ppermute x10, waiting for transfers between devices: 0.52 us -> 16.4 us  [exchange_sum(): lax.ppermute(lax.dynamic_index_in_dim(value, mine ^ offset, at, keepdims=...]
    sub x8 -> x3, other arithmetic: 10.8 us -> 1.89 us  [adamw_update(): master - step_rate * (first_hat / (jnp.sqrt(second_hat) + adam_floor) + d...]
    pallas_call x0 -> x1, Pallas kernels: none -> 7.64 us  [update(): pl.pallas_call(functools.partial(update_kernel, rates), grid_spec=pltpu.P...]
    unnamed x170 -> x123, local copies, waits for them, and re-layouts: 17.6 us -> 15.6 us
  transfers between devices with their start and end apart: 42 -> 42, of which waited for: 20 -> 23; matrix products, arithmetic and copies ran while one was open for 8% -> 8% of each run, Pallas kernels for 34% -> 35%
where the time goes in v4:
time: 581 us; the launch traced here: 580 us
  Pallas kernels  210 us (36%)
  waiting for transfers between devices  203 us (35%)
  starting transfers between devices  60 us (10%)
  local copies, waits for them, and re-layouts  36 us (6%)
  other arithmetic  21.6 us (4%)
  between operations  20.6 us (4%)
  blocking collectives  18.5 us (3%)
  matrix products  10.3 us (2%)
    pallas_call x1, Pallas kernels, attend_back(): pl.pallas_call(attend_back_kernel, grid_spec=pltpu.PrefetchScalarGridSpec...  66.5 us
    all_to_all x1, waiting for transfers between devices, per_device(): heads = lax.all_to_all(heads, head_axes, 0, 0, tiled=True)  53.3 us
    all_to_all x1, waiting for transfers between devices, per_device(): mods = jnp.sum(lax.all_to_all(adapt, ALL, 0, 0, tiled=True), axis=0)  47.4 us
    pallas_call x1, Pallas kernels, attend(): pl.pallas_call(attend_kernel, grid_spec=pltpu.PrefetchScalarGridSpec(num_...  43.2 us
    all_gather x1, waiting for transfers between devices, per_device(): first_weights = lax.all_gather(first_weights, ALL, axis=0, tiled=True)  30.7 us
    ppermute x21, waiting for transfers between devices, swapped(): lax.ppermute(value, axis, [(i, i ^ offset) for i in range(lax.axis_size(a...  28.5 us
    ppermute x21, starting transfers between devices, swapped(): lax.ppermute(value, axis, [(i, i ^ offset) for i in range(lax.axis_size(a...  24.6 us
    pallas_call x1, Pallas kernels, feed_backward(): pl.pallas_call(backward_kernel, grid=(pieces,), in_specs=[whole((tokens,...  23.8 us
  transfers between devices with their start and end apart: 42, of which 23 were waited for; matrix products, arithmetic and copies ran while one was open for 8% of the time, Pallas kernels for 35%

profile of v4, /device:TPU:0, one launch (start us, length us, event | category | flops | bytes accessed | tf_op | source)
XLA Modules:
  0.0 579.5 jit_solution(4985880398485520987)
XLA Ops:
  17.0 7.3 %all-to-all-start = ((f32[32,2,6144]{2,1,0:T(2,128)}), f32[32,2,6144]{2,1,0:T(2,128)S(1)}, u32[]{:S(2)}, u32[]{:S(2)}) async-start(f32[32,2,6144]{2,1,0:T(2,128)} %reshape.595), calls=%async_computation | async-start | bytes 3145728 | tf_op jit(solution)/shard_map/all_to_all | solution.py:1179
  28.1 47.4 %all-to-all-done = f32[32,2,6144]{2,1,0:T(2,128)S(1)} async-done(((f32[32,2,6144]{2,1,0:T(2,128)}), f32[32,2,6144]{2,1,0:T(2,128)S(1)}, u32[]{:S(2)}, u32[]{:S(2)}) %all-to-all-start) | async-done | bytes 1572896 | tf_op jit(solution)/shard_map/all_to_all | solution.py:1179
  76.0 30.7 %all-gather.5.cloned.1.call-done.extra_ref.weight_ref.readout_ref = bf16[1024,3200]{1,0:T(8,128)(2,1)} async-done(((bf16[32,3200]{1,0:T(8,128)(2,1)}), bf16[1024,3200]{1,0:T(8,128)(2,1)}) %all-gather.5.cloned.1.call-update) | async-done | bytes 6553616 | tf_op jit(solution)/shard_map/all_gather | solution.py:1137
  106.7 2.9 copy-done.10
  109.6 11.7 %triple_heads.1 = (f32[512,1024]{1,0:T(8,128)S(1)}, bf16[512,1024]{1,0:T(8,128)(2,1)}, bf16[8,512,384]{2,1,0:T(8,128)(2,1)}) custom-call(bf16[512,16]{1,0:T(8,128)(2,1)S(1)} %get-tuple-element.240.inputs_ref, bf16[1024,3200]{1,0:T(8,128)(2,1)S(1)} %copy-done.10, f32[2,6,1024]{2,1,0:T(8,128)S(1)} %reshape.596.mods_ref, bf16[1024,3200]{1,0:T(8,128)(2,1)S(1)} %copy-done.10, ...), custom_call_target="tpu_custom_call" | custom-call | flops 13200000000 | bytes 1048576 | tf_op jit(solution)/shard_map/triple_heads/pallas_call | solution.py:225
  122.6 3.6 all-to-all-start.1
  127.6 53.3 %all-to-all-done.1 = bf16[8,512,384]{2,1,0:T(8,128)(2,1)S(1)} async-done(((bf16[8,512,384]{2,1,0:T(8,128)(2,1)}), bf16[8,512,384]{2,1,0:T(8,128)(2,1)S(1)}, u32[]{:S(2)}, u32[]{:S(2)}) %all-to-all-start.1) | async-done | bytes 3145760 | tf_op jit(solution)/shard_map/all_to_all | solution.py:1225
  182.6 43.2 %attend.1 = (bf16[8,2,256,128]{3,2,1,0:T(8,128)(2,1)S(1)}, f32[16,128,256]{2,1,0:T(8,128)S(1)}, f32[16,1,512]{2,1,0:T(1,128)S(1)}) custom-call(s32[16]{0:T(128)S(1)} %get-tuple-element.266.order_ref, s32[16]{0:T(128)S(1)} %get-tuple-element.210.count_ref, bf16[8,2,256,384]{3,2,1,0:T(8,128)(2,1)} %bitcast.146, bf16[8,2,256,384]{3,2,1,0:T(8,128)(2,1)} %bitcast.147, ...), custom_call_target="tpu_custom_call" | custom-call | flops 49500000256 | bytes 1048576 | tf_op jit(solution)/shard_map/attend/pallas_call | solution.py:445
  226.4 18.5 %all_to_all.30.heads_ref = bf16[8,512,128]{2,1,0:T(8,128)(2,1)} all-to-all(bf16[8,512,128]{2,1,0:T(8,128)(2,1)S(1)} %bitcast.133), channel_id=1, replica_groups=mesh['batch'=4,'row'=4,'core'=2] {'batch','core'}, dimensions={0} | all-to-all | bytes 2097152 | tf_op jit(solution)/shard_map/all_to_all | solution.py:1236
  246.9 4.6 all-gather.9.cloned.1.call-done
  251.5 5.5 project_norm.1
  257.0 21.0 %feed_forward.1 = (f32[512,4096]{1,0:T(8,128)}, bf16[512,4096]{1,0:T(8,128)(2,1)}, f32[512,1024]{1,0:T(8,128)}, bf16[512,1024]{1,0:T(8,128)(2,1)}, f32[1024,16]{...) custom-call(f32[2]{0:T(128)} %fusion.48.scale_ref, bf16[512,1024]{1,0:T(8,128)(2,1)} %get-tuple-element.81.mixed_ref, ...), custom_call_target="tpu_custom_call" | custom-call | flops 22000001024 | bytes 1048576 | tf_op jit(solution)/shard_map/feed_forward/pallas_call | solution.py:764
  278.1 23.8 %feed_backward.1 = (bf16[512,4096]{1,0:T(8,128)(2,1)}, f32[512,1024]{1,0:T(8,128)}, bf16[512,1024]{1,0:T(8,128)(2,1)}, bf16[8,512,128]{2,1,0:T(8,128)(2,1)}, f32[2,3,1024]{2,1,0:T(4,128)}) custom-call(bf16[512,1024]{1,0:T(8,128)(2,1)} %get-tuple-element.84.grad_outer_ref, bf16[32,288,1024]{2,1,0:T(8,128)(2,1)} %bitcast.138, ...), custom_call_target="tpu_custom_call" | custom-call | flops 24199999488 | bytes 1048576 | tf_op jit(solution)/shard_map/feed_backward/pallas_call | solution.py:871
  301.9 16.6 %weight_grads.1 = bf16[4,2,4,288,1024]{4,3,2,1,0:T(8,128)(2,1)} custom-call(bf16[512,4096]{1,0:T(8,128)(2,1)} %get-tuple-element.100.active_ref, bf16[512,1024]{1,0:T(8,128)(2,1)} %get-tuple-element.84.grad_outer_ref, bf16[512,1024]{1,0:T(8,128)(2,1)} %get-tuple-element.101.attended_ref, bf16[512,1024]{1,0:T(8,128)(2,1)} %get-tuple-element.102.grad_branch_ref, ...), custom_call_target="tpu_custom_call" | custom-call | flops 30799998976 | bytes 1048576 | tf_op jit(solution)/shard_map/weight_grads/pallas_call | solution.py:936
  318.6 3.7 all-to-all-start.3
  328.3 9.5 %collective-permute-done.2 = bf16[4,4096]{1,0:T(4,128)(2,1)S(1)} collective-permute-done((bf16[4,4096]{1,0:T(4,128)(2,1)S(1)}, bf16[4,4096]{1,0:T(4,128)(2,1)S(1)}, u32[]{:S(2)}, u32[]{:S(2)}) %collective-permute-start.2) | collective-permute-done | bytes 32800 | tf_op jit(solution)/shard_map/ppermute | solution.py:988
  340.2 66.5 %attend_back.1 = bf16[8,2,256,384]{3,2,1,0:T(8,128)(2,1)} custom-call(s32[16]{0:T(128)} %get-tuple-element.265.order_ref, s32[16]{0:T(128)} %get-tuple-element.208.count_ref, bf16[8,2,256,384]{3,2,1,0:T(8,128)(2,1)} %bitcast.149, bf16[8,2,256,384]{3,2,1,0:T(8,128)(2,1)} %bitcast.150, bf16[8,2,256,384]{3,2,1,0:T(8,128)(2,1)} %bitcast.151, ...), custom_call_target="tpu_custom_call" | custom-call | flops 71499997184 | bytes 1048576 | tf_op jit(solution)/shard_map/attend_back/pallas_call | solution.py:621
  406.7 3.6 all-to-all-start.4
  410.5 11.2 %copy.160 = bf16[1024,4096]{1,0:T(8,128)(2,1)} copy(bf16[1024,4096]{0,1:T(8,128)(2,1)} %bitcast.141) | data formatting | bytes 16777216 | tf_op jit(solution)/shard_map/dot_general | solution.py:39
  423.4 2.7 collective-permute-start.8
  426.1 7.8 %convolution_bitcast_fusion = f32[4,4,2,32,384]{4,3,2,0,1:T(8,128)S(1)} fusion(bf16[4,4,2,32,4096]{4,3,2,1,0:T(8,128)(2,1)} %bitcast.142, bf16[4096,384,1,1,1]{1,0,4,3,2:T(8,128)(2,1)} %bitcast.153), kind=kOutput, calls=%fused_computation | convolution fusion | flops 3221225472 | bytes 13107200 | tf_op jit(solution)/shard_map/dot_general | solution.py:39
  435.8 2.9 collective-permute-start.5
  439.5 4.5 collective-permute-done.7
  444.0 8.9 %collective-permute-done.6 = bf16[8,32,384]{2,1,0:T(8,128)(2,1)S(1)} collective-permute-done((bf16[8,32,384]{2,1,0:T(8,128)(2,1)S(1)}, bf16[8,32,384]{2,1,0:T(8,128)(2,1)S(1)}, u32[]{:S(2)}, u32[]{:S(2)}) %collective-permute-start.6) | collective-permute-done | bytes 196640 | tf_op jit(solution)/shard_map/ppermute | solution.py:1013
  453.8 19.7 %all-to-all-done.4.grads_ref = bf16[8,512,384]{2,1,0:T(8,128)(2,1)S(1)} async-done(((bf16[8,512,384]{2,1,0:T(8,128)(2,1)}), bf16[8,512,384]{2,1,0:T(8,128)(2,1)S(1)}, u32[]{:S(2)}, u32[]{:S(2)}) %all-to-all-start.4) | async-done | bytes 3145760 | tf_op jit(solution)/shard_map/all_to_all | solution.py:1316
  476.6 13.6 %triple_back.1 = (f32[2,2,1024]{2,1,0:T(2,128)S(1)}, f32[1024,16]{1,0:T(8,128)S(1)}) custom-call(bf16[8,512,384]{2,1,0:T(8,128)(2,1)S(1)} %all-to-all-done.4.grads_ref, bf16[1024,3200]{1,0:T(8,128)(2,1)} %all-gather.5.cloned.1.call-done.extra_ref.weight_ref.readout_ref, f32[512,1024]{1,0:T(8,128)S(1)} %copy-done.1, f32[512,1024]{1,0:T(8,128)S(1)} %copy-done.11, ...), custom_call_target="tpu_custom_call" | custom-call | flops 13200000000 | bytes 1048576 | tf_op jit(solution)/shard_map/triple_back/pallas_call | solution.py:297
  497.4 2.5 collective-permute-start.12
  500.1 3.5 all-to-all-start.5
  505.2 2.9 collective-permute-start.15
  516.3 2.4 collective-permute-done.21
  527.5 6.0 %collective-permute-done.23 = bf16[16,2048]{1,0:T(8,128)(2,1)S(1)} collective-permute-done((bf16[16,2048]{1,0:T(8,128)(2,1)S(1)}, bf16[16,2048]{1,0:T(8,128)(2,1)S(1)}, u32[]{:S(2)}, u32[]{:S(2)}) %collective-permute-start.23) | collective-permute-done | bytes 65568 | tf_op jit(solution)/shard_map/ppermute | solution.py:988
  564.2 7.6 %update.1 = (f32[32,6144]{1,0:T(8,128)}, f32[32,6144]{1,0:T(8,128)}, f32[32,6144]{1,0:T(8,128)}, f32[32,3072]{1,0:T(8,128)}, f32[32,3072]{1,0:T(8,128)}, /*index...) custom-call(f32[1]{0:T(128)} %bitcast.42.factor_ref, ...), custom_call_target="tpu_custom_call" | custom-call | flops 7699999744 | bytes 1048576 | tf_op jit(solution)/shard_map/update/pallas_call | solution.py:971
  (295 shorter events, 89.0 us)
Async XLA Ops:
  7.3 99.4 %all-gather.5.cloned.1.call-start = ((), (), s32[]{:S(2)}) async-start(), calls=%async_computation.8 | async-start | bytes 6758400 | tf_op jit(solution)/shard_map/all_gather | solution.py:1137
  10.8 240.7 %all-gather.9.cloned.1.call-start = ((), (), s32[]{:S(2)}) async-start(), calls=%async_computation.12 | async-start | bytes 19464192 | tf_op jit(solution)/shard_map/all_gather | solution.py:1143
  17.0 58.5 %all-to-all-start = ((f32[32,2,6144]{2,1,0:T(2,128)}), f32[32,2,6144]{2,1,0:T(2,128)S(1)}, u32[]{:S(2)}, u32[]{:S(2)}) async-start(f32[32,2,6144]{2,1,0:T(2,128)} %reshape.595), calls=%async_computation | async-start | bytes 3145728 | tf_op jit(solution)/shard_map/all_to_all | solution.py:1179
  122.6 58.3 %all-to-all-start.1 = ((bf16[8,512,384]{2,1,0:T(8,128)(2,1)}), bf16[8,512,384]{2,1,0:T(8,128)(2,1)S(1)}, u32[]{:S(2)}, u32[]{:S(2)}) async-start(bf16[8,512,384]{2,1,0:T(8,128)(2,1)} %get-tuple-element.76), calls=%async_computation.1 | async-start | bytes 6291456 | tf_op jit(solution)/shard_map/all_to_all | solution.py:1225
  126.3 284.2 %all-gather.7.cloned.1.call-start = ((), (), s32[]{:S(2)}) async-start(), calls=%async_computation.9 | async-start | bytes 9437184 | tf_op jit(solution)/shard_map/all_gather | solution.py:1238
  244.9 246.2 %reduce-scatter.3.cloned.1.call-start = ((), (), s32[]{:S(2)}) async-start(), calls=%async_computation.10 | async-start | bytes 21233664 | tf_op jit(solution)/shard_map/reduce_scatter | solution.py:1284
  318.6 20.6 %all-to-all-start.3 = ((bf16[8,512,128]{2,1,0:T(8,128)(2,1)}), bf16[8,512,128]{2,1,0:T(8,128)(2,1)S(1)}, u32[]{:S(2)}, u32[]{:S(2)}) async-start(bf16[8,512,128]{2,1,0:T(8,128)(2,1)} %get-tuple-element.88), calls=%async_computation.3 | async-start | bytes 2097152 | tf_op jit(solution)/shard_map/all_to_all | solution.py:1266
  323.8 14.0 %collective-permute-start.2 = (bf16[4,4096]{1,0:T(4,128)(2,1)S(1)}, bf16[4,4096]{1,0:T(4,128)(2,1)S(1)}, u32[]{:S(2)}, u32[]{:S(2)}) collective-permute-start(bf16[4,4096]{1,0:T(4,128)(2,1)S(1)} %pad_maximum_fusion.5), channel_id=1, source_target_pairs={{0,8},{8,0},{16,24},{24,16},{1,9},{9,1},{17,25},{25,17},{2,10},{10... | collective-permute-start | bytes 98312 | tf_op jit(solution)/shard_map/ppermute | solution.py:988
  325.7 12.1 %collective-permute-start.3 = (bf16[4,4096]{1,0:T(4,128)(2,1)S(1)}, bf16[4,4096]{1,0:T(4,128)(2,1)S(1)}, u32[]{:S(2)}, u32[]{:S(2)}) collective-permute-start(bf16[4,4096]{1,0:T(4,128)(2,1)S(1)} %pad_maximum_fusion.5), channel_id=1, source_target_pairs={{0,16},{8,24},{16,0},{24,8},{1,17},{9,25},{17,1},{25,9},{2,18},{10... | collective-permute-start | bytes 98312 | tf_op jit(solution)/shard_map/ppermute | solution.py:988
  327.2 11.8 %collective-permute-start.4 = (bf16[4,4096]{1,0:T(4,128)(2,1)S(1)}, bf16[4,4096]{1,0:T(4,128)(2,1)S(1)}, u32[]{:S(2)}, u32[]{:S(2)}) collective-permute-start(bf16[4,4096]{1,0:T(4,128)(2,1)S(1)} %pad_maximum_fusion.5), channel_id=1, source_target_pairs={{0,24},{8,16},{16,8},{24,0},{1,25},{9,17},{17,9},{25,1},{2,26},{10... | collective-permute-start | bytes 98312 | tf_op jit(solution)/shard_map/ppermute | solution.py:988
  406.7 66.7 %all-to-all-start.4 = ((bf16[8,512,384]{2,1,0:T(8,128)(2,1)}), bf16[8,512,384]{2,1,0:T(8,128)(2,1)S(1)}, u32[]{:S(2)}, u32[]{:S(2)}) async-start(bf16[8,512,384]{2,1,0:T(8,128)(2,1)} %bitcast.152), calls=%async_computation.4 | async-start | bytes 6291456 | tf_op jit(solution)/shard_map/all_to_all | solution.py:1316
  410.4 130.6 %reduce-scatter.5.cloned.1.call-start = ((), (), s32[]{:S(2)}) async-start(), calls=%async_computation.11 | async-start | bytes 2949120 | tf_op jit(solution)/shard_map/reduce_scatter | solution.py:1337
  421.7 14.0 %collective-permute-start.10 = (bf16[16,4096]{1,0:T(8,128)(2,1)S(1)}, bf16[16,4096]{1,0:T(8,128)(2,1)S(1)}, u32[]{:S(2)}, u32[]{:S(2)}) collective-permute-start(bf16[16,4096]{1,0:T(8,128)(2,1)S(1)} %concatenate.48), channel_id=1, source_target_pairs={{0,6},{2,4},{4,2},{6,0},{1,7},{3,5},{5,3},{7,1},{8,14},{10,12},{12... | collective-permute-start | bytes 393224 | tf_op jit(solution)/shard_map/ppermute | solution.py:988
  422.7 15.9 %collective-permute-start.9 = (bf16[16,4096]{1,0:T(8,128)(2,1)S(1)}, bf16[16,4096]{1,0:T(8,128)(2,1)S(1)}, u32[]{:S(2)}, u32[]{:S(2)}) collective-permute-start(bf16[16,4096]{1,0:T(8,128)(2,1)S(1)} %concatenate.48), channel_id=1, source_target_pairs={{0,4},{2,6},{4,0},{6,2},{1,5},{3,7},{5,1},{7,3},{8,12},{10,14},{12... | collective-permute-start | bytes 393224 | tf_op jit(solution)/shard_map/ppermute | solution.py:988
  423.4 15.3 %collective-permute-start.8 = (bf16[16,4096]{1,0:T(8,128)(2,1)S(1)}, bf16[16,4096]{1,0:T(8,128)(2,1)S(1)}, u32[]{:S(2)}, u32[]{:S(2)}) collective-permute-start(bf16[16,4096]{1,0:T(8,128)(2,1)S(1)} %concatenate.48), channel_id=1, source_target_pairs={{0,2},{2,0},{4,6},{6,4},{1,3},{3,1},{5,7},{7,5},{8,10},{10,8},{12,... | collective-permute-start | bytes 393224 | tf_op jit(solution)/shard_map/ppermute | solution.py:988
  434.2 9.8 %collective-permute-start.7 = (bf16[8,32,384]{2,1,0:T(8,128)(2,1)S(1)}, bf16[8,32,384]{2,1,0:T(8,128)(2,1)S(1)}, u32[]{:S(2)}, u32[]{:S(2)}) collective-permute-start(bf16[8,32,384]{2,1,0:T(8,128)(2,1)S(1)} %get-tuple-element.230), channel_id=1, source_target_pairs={{0,6},{2,4},{4,2},{6,0},{1,7},{3,5},{5,3},{7,1},{8,14},{10,12},{12... | collective-permute-start | bytes 589832 | tf_op jit(solution)/shard_map/ppermute | solution.py:1013
  435.4 17.6 %collective-permute-start.6 = (bf16[8,32,384]{2,1,0:T(8,128)(2,1)S(1)}, bf16[8,32,384]{2,1,0:T(8,128)(2,1)S(1)}, u32[]{:S(2)}, u32[]{:S(2)}) collective-permute-start(bf16[8,32,384]{2,1,0:T(8,128)(2,1)S(1)} %get-tuple-element.231), channel_id=1, source_target_pairs={{0,4},{2,6},{4,0},{6,2},{1,5},{3,7},{5,1},{7,3},{8,12},{10,14},{12... | collective-permute-start | bytes 589832 | tf_op jit(solution)/shard_map/ppermute | solution.py:1013
  435.8 17.2 %collective-permute-start.5 = (bf16[8,32,384]{2,1,0:T(8,128)(2,1)S(1)}, bf16[8,32,384]{2,1,0:T(8,128)(2,1)S(1)}, u32[]{:S(2)}, u32[]{:S(2)}) collective-permute-start(bf16[8,32,384]{2,1,0:T(8,128)(2,1)S(1)} %get-tuple-element.229), channel_id=1, source_target_pairs={{0,2},{2,0},{4,6},{6,4},{1,3},{3,1},{5,7},{7,5},{8,10},{10,8},{12,... | collective-permute-start | bytes 589832 | tf_op jit(solution)/shard_map/ppermute | solution.py:1013
  496.3 7.3 %collective-permute-start.14 = (f32[4,8,128]{2,1,0:T(8,128)S(1)}, f32[4,8,128]{2,1,0:T(8,128)S(1)}, u32[]{:S(2)}, u32[]{:S(2)}) collective-permute-start(f32[4,8,128]{2,1,0:T(8,128)S(1)} %get-tuple-element.242), channel_id=1, source_target_pairs={{0,24},{8,16},{16,8},{24,0},{1,25},{9,17},{17,9},{25,1},{2,26},{10... | collective-permute-start | bytes 49160 | tf_op jit(solution)/shard_map/ppermute | solution.py:1013
  497.0 6.6 %collective-permute-start.13 = (f32[4,8,128]{2,1,0:T(8,128)S(1)}, f32[4,8,128]{2,1,0:T(8,128)S(1)}, u32[]{:S(2)}, u32[]{:S(2)}) collective-permute-start(f32[4,8,128]{2,1,0:T(8,128)S(1)} %get-tuple-element.243), channel_id=1, source_target_pairs={{0,16},{8,24},{16,0},{24,8},{1,17},{9,25},{17,1},{25,9},{2,18},{10... | collective-permute-start | bytes 49160 | tf_op jit(solution)/shard_map/ppermute | solution.py:1013
  497.4 6.2 %collective-permute-start.12 = (f32[4,8,128]{2,1,0:T(8,128)S(1)}, f32[4,8,128]{2,1,0:T(8,128)S(1)}, u32[]{:S(2)}, u32[]{:S(2)}) collective-permute-start(f32[4,8,128]{2,1,0:T(8,128)S(1)} %get-tuple-element.241), channel_id=1, source_target_pairs={{0,8},{8,0},{16,24},{24,16},{1,9},{9,1},{17,25},{25,17},{2,10},{10... | collective-permute-start | bytes 49160 | tf_op jit(solution)/shard_map/ppermute | solution.py:1013
  500.1 14.6 %all-to-all-start.5 = ((f32[8,32,384]{2,1,0:T(8,128)}), f32[8,32,384]{2,1,0:T(8,128)S(1)}, u32[]{:S(2)}, u32[]{:S(2)}) async-start(f32[8,32,384]{2,1,0:T(8,128)} %fusion.1), calls=%async_computation.6 | async-start | bytes 786432 | tf_op jit(solution)/shard_map/all_to_all | solution.py:1345
  503.7 5.7 collective-permute-start.17
  504.3 5.6 collective-permute-start.16
  505.2 5.0 collective-permute-start.15
  514.0 4.6 collective-permute-start.21
  518.7 8.7 %collective-permute-start.22 = (bf16[16,2048]{1,0:T(8,128)(2,1)S(1)}, bf16[16,2048]{1,0:T(8,128)(2,1)S(1)}, u32[]{:S(2)}, u32[]{:S(2)}) collective-permute-start(bf16[16,2048]{1,0:T(8,128)(2,1)S(1)} %concatenate.52), channel_id=1, source_target_pairs={{0,2},{2,0},{4,6},{6,4},{1,3},{3,1},{5,7},{7,5},{8,10},{10,8},{12,... | collective-permute-start | bytes 196616 | tf_op jit(solution)/shard_map/ppermute | solution.py:988
  521.0 12.5 %collective-permute-start.23 = (bf16[16,2048]{1,0:T(8,128)(2,1)S(1)}, bf16[16,2048]{1,0:T(8,128)(2,1)S(1)}, u32[]{:S(2)}, u32[]{:S(2)}) collective-permute-start(bf16[16,2048]{1,0:T(8,128)(2,1)S(1)} %concatenate.52), channel_id=1, source_target_pairs={{0,4},{2,6},{4,0},{6,2},{1,5},{3,7},{5,1},{7,3},{8,12},{10,14},{12... | collective-permute-start | bytes 196616 | tf_op jit(solution)/shard_map/ppermute | solution.py:988
  521.9 11.6 %collective-permute-start.24 = (bf16[16,2048]{1,0:T(8,128)(2,1)S(1)}, bf16[16,2048]{1,0:T(8,128)(2,1)S(1)}, u32[]{:S(2)}, u32[]{:S(2)}) collective-permute-start(bf16[16,2048]{1,0:T(8,128)(2,1)S(1)} %concatenate.52), channel_id=1, source_target_pairs={{0,6},{2,4},{4,2},{6,0},{1,7},{3,5},{5,3},{7,1},{8,14},{10,12},{12... | collective-permute-start | bytes 196616 | tf_op jit(solution)/shard_map/ppermute | solution.py:988
  547.4 4.5 collective-permute-start.28
  552.5 5.3 collective-permute-start.30
  554.5 5.4 collective-permute-start.31
  (64 other events, 945.5 us)
Sparse Core Ops, SparseCore 0:
  11.5 95.1 all-gather.4
  110.3 141.1 all-gather.8
  253.4 52.5 all-gather.6
  318.7 149.3 reduce-scatter.2
  491.3 49.6 reduce-scatter.4

commit v5 on v4

--- a/solution.py
+++ b/solution.py
@@ -952,35 +952,33 @@
     )(active, grad_outer, attended, grad_branch, mixed, grad_inner)
 
 
-def update_kernel(rates, factor_ref, *refs):
+def update_kernel(rates, squares_ref, *refs):
+    factor = jnp.minimum(1.0, clip_bound / jnp.sqrt(squares_ref[...]))
     for item, rate in enumerate(rates):
         master, first, second, gradient = (refs[4 * item + part][...] for part in range(4))
-        new = adamw_update(master, first, second, gradient, factor_ref[0], rate)
+        new = adamw_update(master, first, second, gradient, factor, rate)
         for part in range(3):
             refs[4 * len(rates) + 3 * item + part][...] = new[part]
 
 
-def update(factor, states, rates):
+def update(squares, states, rates):
     flat = [array for state in states for array in state]
     steps = 4
     specs = [
-        pl.BlockSpec((array.shape[0], array.shape[1] // steps), lambda i, *_: (0, i))
+        pl.BlockSpec((array.shape[0], array.shape[1] // steps), lambda i: (0, i))
         for array in flat
     ]
     outs = [4 * item + part for item in range(len(states)) for part in (1, 2, 0)]
     new = pl.pallas_call(
         functools.partial(update_kernel, rates),
-        grid_spec=pltpu.PrefetchScalarGridSpec(
-            num_scalar_prefetch=1,
-            grid=(steps,),
-            in_specs=specs,
-            out_specs=[specs[out] for out in outs],
-        ),
+        grid=(steps,),
+        in_specs=[whole((1, 1))] + specs,
+        out_specs=[specs[out] for out in outs],
         out_shape=[jax.ShapeDtypeStruct(flat[out].shape, jnp.float32) for out in outs],
         compiler_params=pltpu.CompilerParams(vmem_limit_bytes=60 * 1024 * 1024),
         cost_estimate=about(7),
         name="update",
-    )(factor.reshape(1), *flat)
+    )(squares, *flat)
     return [new[3 * item : 3 * item + 3] for item in range(len(states))]
 
 
@@ -1334,7 +1332,7 @@
         grad_heads, first_weights, hidden_zero, grad_hidden_one, mods, inputs, head_groups
     )
     second_own, grad_shift = lax.optimization_barrier((second_own, grad_shift))
-    second_own = lax.psum_scatter(second_own, "row", scatter_dimension=0).astype(jnp.float32)
+    second_own = lax.psum_scatter(second_own, "row", scatter_dimension=0)
     late_adapt = gather_near(grad_shift.reshape(frame_local, 2 * D).astype(low_type))
     small = jnp.concatenate([grad_patch, grad_readout], axis=1)
     small = small.reshape(batch_count, row_count, core_count, -1, LANES)
@@ -1361,6 +1359,11 @@
         precision=lax.Precision.HIGHEST,
         preferred_element_type=jnp.float32,
     )
+    squares = sum(
+        jnp.sum(gradient * gradient) for gradient in (small_own, table_own, adapt_own, triple_own)
+    )
+    second_own, squares = lax.optimization_barrier((second_own, squares))
+    second_own = second_own.astype(jnp.float32)
     expand_own = jnp.concatenate(
         [
             second_own[(FF // D + 1 + k) * rows : (FF // D + 2 + k) * rows]
@@ -1378,10 +1381,7 @@
         second_own[: FF // D * rows],
         small_own[:, PATCH_FEAT:],
     )
-    squares = sum(
-        jnp.sum(gradient * gradient)
-        for gradient in (small_own, table_own, adapt_own, triple_own, second_own)
-    )
+    squares = squares + jnp.sum(second_own * second_own)
     lane = jnp.arange(LANES, dtype=jnp.int32)
     bucket_lanes = jnp.sum(
         jnp.where(my_levels[:, None] == lane[None], frame_loss[:, None], 0.0), axis=0
@@ -1397,7 +1397,7 @@
     ]
     large = (2, 3, 4, 5, 6)
     updated = update(
-        factor, [states[item] for item in large], tuple(learn_rates[item] for item in large)
+        sums[1:2, :1], [states[item] for item in large], tuple(learn_rates[item] for item in large)
     )
     new = [
         updated[large.index(item)]

time: 581 us -> 585 us (level)
    unnamed x123 -> x119, local copies, waits for them, and re-layouts: 15.6 us -> 15.3 us
  transfers between devices with their start and end apart: 42 -> 42, of which waited for: 23 -> 20; matrix products, arithmetic and copies ran while one was open for 8% -> 9% of each run, Pallas kernels for 35% -> 35%
where the time goes in v5:
time: 585 us; the launch traced here: 583 us
  Pallas kernels  210 us (36%)
  waiting for transfers between devices  200 us (34%)
  starting transfers between devices  60.3 us (10%)
  local copies, waits for them, and re-layouts  39.9 us (7%)
  other arithmetic  22.5 us (4%)
  between operations  20.7 us (4%)
  blocking collectives  18.5 us (3%)
  matrix products  11.1 us (2%)
    pallas_call x1, Pallas kernels, attend_back(): pl.pallas_call(attend_back_kernel, grid_spec=pltpu.PrefetchScalarGridSpec...  66.4 us
    all_to_all x1, waiting for transfers between devices, per_device(): heads = lax.all_to_all(heads, head_axes, 0, 0, tiled=True)  53.3 us
    all_to_all x1, waiting for transfers between devices, per_device(): mods = jnp.sum(lax.all_to_all(adapt, ALL, 0, 0, tiled=True), axis=0)  46.6 us
    pallas_call x1, Pallas kernels, attend(): pl.pallas_call(attend_kernel, grid_spec=pltpu.PrefetchScalarGridSpec(num_...  43.2 us
    all_gather x1, waiting for transfers between devices, per_device(): first_weights = lax.all_gather(first_weights, ALL, axis=0, tiled=True)  30.8 us
    ppermute x21, waiting for transfers between devices, swapped(): lax.ppermute(value, axis, [(i, i ^ offset) for i in range(lax.axis_size(a...  25.6 us
    ppermute x21, starting transfers between devices, swapped(): lax.ppermute(value, axis, [(i, i ^ offset) for i in range(lax.axis_size(a...  25 us
    pallas_call x1, Pallas kernels, feed_backward(): pl.pallas_call(backward_kernel, grid=(pieces,), in_specs=[whole((tokens,...  23.9 us
  transfers between devices with their start and end apart: 42, of which 20 were waited for; matrix products, arithmetic and copies ran while one was open for 9% of the time, Pallas kernels for 35%

profile of v5, /device:TPU:0, one launch (start us, length us, event | category | flops | bytes accessed | tf_op | source)
XLA Modules:
  0.0 583.0 jit_solution(6048467655392456499)
XLA Ops:
  18.8 7.3 %all-to-all-start = ((f32[32,2,6144]{2,1,0:T(2,128)}), f32[32,2,6144]{2,1,0:T(2,128)S(1)}, u32[]{:S(2)}, u32[]{:S(2)}) async-start(f32[32,2,6144]{2,1,0:T(2,128)} %reshape.584), calls=%async_computation | async-start | bytes 3145728 | tf_op jit(solution)/shard_map/all_to_all | solution.py:1177
  30.1 46.6 %all-to-all-done = f32[32,2,6144]{2,1,0:T(2,128)S(1)} async-done(((f32[32,2,6144]{2,1,0:T(2,128)}), f32[32,2,6144]{2,1,0:T(2,128)S(1)}, u32[]{:S(2)}, u32[]{:S(2)}) %all-to-all-start) | async-done | bytes 1572896 | tf_op jit(solution)/shard_map/all_to_all | solution.py:1177
  77.3 30.8 %all-gather.5.cloned.1.call-done.extra_ref.weight_ref.readout_ref = bf16[1024,3200]{1,0:T(8,128)(2,1)} async-done(((bf16[32,3200]{1,0:T(8,128)(2,1)}), bf16[1024,3200]{1,0:T(8,128)(2,1)}) %all-gather.5.cloned.1.call-update) | async-done | bytes 6553616 | tf_op jit(solution)/shard_map/all_gather | solution.py:1135
  108.0 2.9 copy-done.10
  110.9 11.8 %triple_heads.1 = (f32[512,1024]{1,0:T(8,128)S(1)}, bf16[512,1024]{1,0:T(8,128)(2,1)}, bf16[8,512,384]{2,1,0:T(8,128)(2,1)}) custom-call(bf16[512,16]{1,0:T(8,128)(2,1)S(1)} %get-tuple-element.244.inputs_ref, bf16[1024,3200]{1,0:T(8,128)(2,1)S(1)} %copy-done.10, f32[2,6,1024]{2,1,0:T(8,128)S(1)} %reshape.585.mods_ref, bf16[1024,3200]{1,0:T(8,128)(2,1)S(1)} %copy-done.10, ...), custom_call_target="tpu_custom_call" | custom-call | flops 13200000000 | bytes 1048576 | tf_op jit(solution)/shard_map/triple_heads/pallas_call | solution.py:225
  124.0 3.7 all-to-all-start.1
  129.0 53.3 %all-to-all-done.1 = bf16[8,512,384]{2,1,0:T(8,128)(2,1)S(1)} async-done(((bf16[8,512,384]{2,1,0:T(8,128)(2,1)}), bf16[8,512,384]{2,1,0:T(8,128)(2,1)S(1)}, u32[]{:S(2)}, u32[]{:S(2)}) %all-to-all-start.1) | async-done | bytes 3145760 | tf_op jit(solution)/shard_map/all_to_all | solution.py:1223
  184.0 43.2 %attend.1 = (bf16[8,2,256,128]{3,2,1,0:T(8,128)(2,1)S(1)}, f32[16,128,256]{2,1,0:T(8,128)S(1)}, f32[16,1,512]{2,1,0:T(1,128)S(1)}) custom-call(s32[16]{0:T(128)S(1)} %get-tuple-element.270.order_ref, s32[16]{0:T(128)S(1)} %get-tuple-element.214.count_ref, bf16[8,2,256,384]{3,2,1,0:T(8,128)(2,1)} %bitcast.137, bf16[8,2,256,384]{3,2,1,0:T(8,128)(2,1)} %bitcast.138, ...), custom_call_target="tpu_custom_call" | custom-call | flops 49500000256 | bytes 1048576 | tf_op jit(solution)/shard_map/attend/pallas_call | solution.py:445
  227.9 18.5 %all_to_all.30.heads_ref = bf16[8,512,128]{2,1,0:T(8,128)(2,1)} all-to-all(bf16[8,512,128]{2,1,0:T(8,128)(2,1)S(1)} %bitcast.121), channel_id=1, replica_groups=mesh['batch'=4,'row'=4,'core'=2] {'batch','core'}, dimensions={0} | all-to-all | bytes 2097152 | tf_op jit(solution)/shard_map/all_to_all | solution.py:1234
  248.4 5.1 all-gather.9.cloned.1.call-done
  253.5 5.5 project_norm.1
  259.0 21.0 %feed_forward.1 = (f32[512,4096]{1,0:T(8,128)}, bf16[512,4096]{1,0:T(8,128)(2,1)}, f32[512,1024]{1,0:T(8,128)}, bf16[512,1024]{1,0:T(8,128)(2,1)}, f32[1024,16]{...) custom-call(f32[2]{0:T(128)} %fusion.48.scale_ref, bf16[512,1024]{1,0:T(8,128)(2,1)} %get-tuple-element.83.mixed_ref, ...), custom_call_target="tpu_custom_call" | custom-call | flops 22000001024 | bytes 1048576 | tf_op jit(solution)/shard_map/feed_forward/pallas_call | solution.py:764
  280.0 23.9 %feed_backward.1 = (bf16[512,4096]{1,0:T(8,128)(2,1)}, f32[512,1024]{1,0:T(8,128)}, bf16[512,1024]{1,0:T(8,128)(2,1)}, bf16[8,512,128]{2,1,0:T(8,128)(2,1)}, f32[2,3,1024]{2,1,0:T(4,128)}) custom-call(bf16[512,1024]{1,0:T(8,128)(2,1)} %get-tuple-element.87.grad_outer_ref, bf16[32,288,1024]{2,1,0:T(8,128)(2,1)} %bitcast.126, ...), custom_call_target="tpu_custom_call" | custom-call | flops 24199999488 | bytes 1048576 | tf_op jit(solution)/shard_map/feed_backward/pallas_call | solution.py:871
  303.9 16.6 %weight_grads.1 = bf16[4,2,4,288,1024]{4,3,2,1,0:T(8,128)(2,1)} custom-call(bf16[512,4096]{1,0:T(8,128)(2,1)} %get-tuple-element.86.active_ref, bf16[512,1024]{1,0:T(8,128)(2,1)} %get-tuple-element.87.grad_outer_ref, bf16[512,1024]{1,0:T(8,128)(2,1)} %get-tuple-element.88.attended_ref, bf16[512,1024]{1,0:T(8,128)(2,1)} %get-tuple-element.92.grad_branch_ref, ...), custom_call_target="tpu_custom_call" | custom-call | flops 30799998976 | bytes 1048576 | tf_op jit(solution)/shard_map/weight_grads/pallas_call | solution.py:936
  320.6 3.7 all-to-all-start.3
  330.2 9.5 %collective-permute-done.2 = bf16[4,4096]{1,0:T(4,128)(2,1)S(1)} collective-permute-done((bf16[4,4096]{1,0:T(4,128)(2,1)S(1)}, bf16[4,4096]{1,0:T(4,128)(2,1)S(1)}, u32[]{:S(2)}, u32[]{:S(2)}) %collective-permute-start.2) | collective-permute-done | bytes 32800 | tf_op jit(solution)/shard_map/ppermute | solution.py:986
  343.4 66.4 %attend_back.1 = bf16[8,2,256,384]{3,2,1,0:T(8,128)(2,1)} custom-call(s32[16]{0:T(128)} %get-tuple-element.269.order_ref, s32[16]{0:T(128)} %get-tuple-element.212.count_ref, bf16[8,2,256,384]{3,2,1,0:T(8,128)(2,1)} %bitcast.140, bf16[8,2,256,384]{3,2,1,0:T(8,128)(2,1)} %bitcast.141, bf16[8,2,256,384]{3,2,1,0:T(8,128)(2,1)} %bitcast.142, ...), custom_call_target="tpu_custom_call" | custom-call | flops 71499997184 | bytes 1048576 | tf_op jit(solution)/shard_map/attend_back/pallas_call | solution.py:621
  409.8 3.6 all-to-all-start.4
  413.6 11.3 %copy.160 = bf16[1024,4096]{1,0:T(8,128)(2,1)} copy(bf16[1024,4096]{0,1:T(8,128)(2,1)} %bitcast.129) | data formatting | bytes 16777216 | tf_op jit(solution)/shard_map/dot_general | solution.py:39
  429.3 8.0 %convolution_bitcast_fusion = f32[4,4,2,32,384]{4,3,2,0,1:T(8,128)S(1)} fusion(bf16[4,4,2,32,4096]{4,3,2,1,0:T(8,128)(2,1)} %bitcast.130, bf16[4096,384,1,1,1]{1,0,4,3,2:T(8,128)(2,1)} %bitcast.144), kind=kOutput, calls=%fused_computation | convolution fusion | flops 3221225472 | bytes 13107200 | tf_op jit(solution)/shard_map/dot_general | solution.py:39
  439.0 3.0 collective-permute-start.5
  442.8 4.5 collective-permute-done.7
  447.3 8.8 %collective-permute-done.6 = bf16[8,32,384]{2,1,0:T(8,128)(2,1)S(1)} collective-permute-done((bf16[8,32,384]{2,1,0:T(8,128)(2,1)S(1)}, bf16[8,32,384]{2,1,0:T(8,128)(2,1)S(1)}, u32[]{:S(2)}, u32[]{:S(2)}) %collective-permute-start.6) | collective-permute-done | bytes 196640 | tf_op jit(solution)/shard_map/ppermute | solution.py:1011
  457.0 19.6 %all-to-all-done.4.grads_ref = bf16[8,512,384]{2,1,0:T(8,128)(2,1)S(1)} async-done(((bf16[8,512,384]{2,1,0:T(8,128)(2,1)}), bf16[8,512,384]{2,1,0:T(8,128)(2,1)S(1)}, u32[]{:S(2)}, u32[]{:S(2)}) %all-to-all-start.4) | async-done | bytes 3145760 | tf_op jit(solution)/shard_map/all_to_all | solution.py:1314
  479.7 13.6 %triple_back.1 = (f32[2,2,1024]{2,1,0:T(2,128)S(1)}, f32[1024,16]{1,0:T(8,128)S(1)}) custom-call(bf16[8,512,384]{2,1,0:T(8,128)(2,1)S(1)} %all-to-all-done.4.grads_ref, bf16[1024,3200]{1,0:T(8,128)(2,1)} %all-gather.5.cloned.1.call-done.extra_ref.weight_ref.readout_ref, f32[512,1024]{1,0:T(8,128)S(1)} %copy-done.1, f32[512,1024]{1,0:T(8,128)S(1)} %copy-done.11, ...), custom_call_target="tpu_custom_call" | custom-call | flops 13200000000 | bytes 1048576 | tf_op jit(solution)/shard_map/triple_back/pallas_call | solution.py:297
  505.2 3.5 all-to-all-start.5
  510.8 2.8 collective-permute-start.15
  522.5 3.6 collective-permute-start.24
  526.9 3.5 collective-permute-done.22
  530.4 3.9 collective-permute-done.23
  539.9 4.4 reduce-scatter.5.cloned.1.call-done
  567.0 8.3 %update.1 = (f32[32,6144]{1,0:T(8,128)}, f32[32,6144]{1,0:T(8,128)}, f32[32,6144]{1,0:T(8,128)}, f32[32,3072]{1,0:T(8,128)}, f32[32,3072]{1,0:T(8,128)}, /*index...) custom-call(f32[1,1]{1,0:T(1,128)} %get-tuple-element.255.squares_re, ...), custom_call_target="tpu_custom_call" | custom-call | flops 7699999744 | bytes 1048576 | tf_op jit(solution)/shard_map/update/pallas_call | solution.py:972
  (290 shorter events, 90.3 us)
Async XLA Ops:
  7.2 100.8 %all-gather.5.cloned.1.call-start = ((), (), s32[]{:S(2)}) async-start(), calls=%async_computation.8 | async-start | bytes 6758400 | tf_op jit(solution)/shard_map/all_gather | solution.py:1135
  10.8 242.7 %all-gather.9.cloned.1.call-start = ((), (), s32[]{:S(2)}) async-start(), calls=%async_computation.12 | async-start | bytes 19464192 | tf_op jit(solution)/shard_map/all_gather | solution.py:1141
  18.8 57.8 %all-to-all-start = ((f32[32,2,6144]{2,1,0:T(2,128)}), f32[32,2,6144]{2,1,0:T(2,128)S(1)}, u32[]{:S(2)}, u32[]{:S(2)}) async-start(f32[32,2,6144]{2,1,0:T(2,128)} %reshape.584), calls=%async_computation | async-start | bytes 3145728 | tf_op jit(solution)/shard_map/all_to_all | solution.py:1177
  124.0 58.3 %all-to-all-start.1 = ((bf16[8,512,384]{2,1,0:T(8,128)(2,1)}), bf16[8,512,384]{2,1,0:T(8,128)(2,1)S(1)}, u32[]{:S(2)}, u32[]{:S(2)}) async-start(bf16[8,512,384]{2,1,0:T(8,128)(2,1)} %get-tuple-element.78), calls=%async_computation.1 | async-start | bytes 6291456 | tf_op jit(solution)/shard_map/all_to_all | solution.py:1223
  127.7 285.9 %all-gather.7.cloned.1.call-start = ((), (), s32[]{:S(2)}) async-start(), calls=%async_computation.10 | async-start | bytes 9437184 | tf_op jit(solution)/shard_map/all_gather | solution.py:1236
  246.3 247.9 %reduce-scatter.3.cloned.1.call-start = ((), (), s32[]{:S(2)}) async-start(), calls=%async_computation.9 | async-start | bytes 21233664 | tf_op jit(solution)/shard_map/reduce_scatter | solution.py:1282
  320.6 21.8 %all-to-all-start.3 = ((bf16[8,512,128]{2,1,0:T(8,128)(2,1)}), bf16[8,512,128]{2,1,0:T(8,128)(2,1)S(1)}, u32[]{:S(2)}, u32[]{:S(2)}) async-start(bf16[8,512,128]{2,1,0:T(8,128)(2,1)} %get-tuple-element.94), calls=%async_computation.4 | async-start | bytes 2097152 | tf_op jit(solution)/shard_map/all_to_all | solution.py:1264
  325.7 14.0 %collective-permute-start.2 = (bf16[4,4096]{1,0:T(4,128)(2,1)S(1)}, bf16[4,4096]{1,0:T(4,128)(2,1)S(1)}, u32[]{:S(2)}, u32[]{:S(2)}) collective-permute-start(bf16[4,4096]{1,0:T(4,128)(2,1)S(1)} %pad_maximum_fusion.5), channel_id=1, source_target_pairs={{0,8},{8,0},{16,24},{24,16},{1,9},{9,1},{17,25},{25,17},{2,10},{10... | collective-permute-start | bytes 98312 | tf_op jit(solution)/shard_map/ppermute | solution.py:986
  327.7 12.1 %collective-permute-start.3 = (bf16[4,4096]{1,0:T(4,128)(2,1)S(1)}, bf16[4,4096]{1,0:T(4,128)(2,1)S(1)}, u32[]{:S(2)}, u32[]{:S(2)}) collective-permute-start(bf16[4,4096]{1,0:T(4,128)(2,1)S(1)} %pad_maximum_fusion.5), channel_id=1, source_target_pairs={{0,16},{8,24},{16,0},{24,8},{1,17},{9,25},{17,1},{25,9},{2,18},{10... | collective-permute-start | bytes 98312 | tf_op jit(solution)/shard_map/ppermute | solution.py:986
  329.2 11.8 %collective-permute-start.4 = (bf16[4,4096]{1,0:T(4,128)(2,1)S(1)}, bf16[4,4096]{1,0:T(4,128)(2,1)S(1)}, u32[]{:S(2)}, u32[]{:S(2)}) collective-permute-start(bf16[4,4096]{1,0:T(4,128)(2,1)S(1)} %pad_maximum_fusion.5), channel_id=1, source_target_pairs={{0,24},{8,16},{16,8},{24,0},{1,25},{9,17},{17,9},{25,1},{2,26},{10... | collective-permute-start | bytes 98312 | tf_op jit(solution)/shard_map/ppermute | solution.py:986
  409.8 66.7 %all-to-all-start.4 = ((bf16[8,512,384]{2,1,0:T(8,128)(2,1)}), bf16[8,512,384]{2,1,0:T(8,128)(2,1)S(1)}, u32[]{:S(2)}, u32[]{:S(2)}) async-start(bf16[8,512,384]{2,1,0:T(8,128)(2,1)} %bitcast.143), calls=%async_computation.5 | async-start | bytes 6291456 | tf_op jit(solution)/shard_map/all_to_all | solution.py:1314
  413.5 130.8 %reduce-scatter.5.cloned.1.call-start = ((), (), s32[]{:S(2)}) async-start(), calls=%async_computation.11 | async-start | bytes 2949120 | tf_op jit(solution)/shard_map/reduce_scatter | solution.py:1335
  424.9 14.0 %collective-permute-start.10 = (bf16[16,4096]{1,0:T(8,128)(2,1)S(1)}, bf16[16,4096]{1,0:T(8,128)(2,1)S(1)}, u32[]{:S(2)}, u32[]{:S(2)}) collective-permute-start(bf16[16,4096]{1,0:T(8,128)(2,1)S(1)} %copy-done.22), channel_id=1, source_target_pairs={{0,6},{2,4},{4,2},{6,0},{1,7},{3,5},{5,3},{7,1},{8,14},{10,12},{12... | collective-permute-start | bytes 393224 | tf_op jit(solution)/shard_map/ppermute | solution.py:986
  425.9 16.1 %collective-permute-start.9 = (bf16[16,4096]{1,0:T(8,128)(2,1)S(1)}, bf16[16,4096]{1,0:T(8,128)(2,1)S(1)}, u32[]{:S(2)}, u32[]{:S(2)}) collective-permute-start(bf16[16,4096]{1,0:T(8,128)(2,1)S(1)} %copy-done.22), channel_id=1, source_target_pairs={{0,4},{2,6},{4,0},{6,2},{1,5},{3,7},{5,1},{7,3},{8,12},{10,14},{12... | collective-permute-start | bytes 393224 | tf_op jit(solution)/shard_map/ppermute | solution.py:986
  426.8 15.2 %collective-permute-start.8 = (bf16[16,4096]{1,0:T(8,128)(2,1)S(1)}, bf16[16,4096]{1,0:T(8,128)(2,1)S(1)}, u32[]{:S(2)}, u32[]{:S(2)}) collective-permute-start(bf16[16,4096]{1,0:T(8,128)(2,1)S(1)} %copy-done.22), channel_id=1, source_target_pairs={{0,2},{2,0},{4,6},{6,4},{1,3},{3,1},{5,7},{7,5},{8,10},{10,8},{12,... | collective-permute-start | bytes 393224 | tf_op jit(solution)/shard_map/ppermute | solution.py:986
  437.5 9.8 %collective-permute-start.7 = (bf16[8,32,384]{2,1,0:T(8,128)(2,1)S(1)}, bf16[8,32,384]{2,1,0:T(8,128)(2,1)S(1)}, u32[]{:S(2)}, u32[]{:S(2)}) collective-permute-start(bf16[8,32,384]{2,1,0:T(8,128)(2,1)S(1)} %get-tuple-element.234), channel_id=1, source_target_pairs={{0,6},{2,4},{4,2},{6,0},{1,7},{3,5},{5,3},{7,1},{8,14},{10,12},{12... | collective-permute-start | bytes 589832 | tf_op jit(solution)/shard_map/ppermute | solution.py:1011
  438.5 17.7 %collective-permute-start.6 = (bf16[8,32,384]{2,1,0:T(8,128)(2,1)S(1)}, bf16[8,32,384]{2,1,0:T(8,128)(2,1)S(1)}, u32[]{:S(2)}, u32[]{:S(2)}) collective-permute-start(bf16[8,32,384]{2,1,0:T(8,128)(2,1)S(1)} %get-tuple-element.235), channel_id=1, source_target_pairs={{0,4},{2,6},{4,0},{6,2},{1,5},{3,7},{5,1},{7,3},{8,12},{10,14},{12... | collective-permute-start | bytes 589832 | tf_op jit(solution)/shard_map/ppermute | solution.py:1011
  439.0 17.2 %collective-permute-start.5 = (bf16[8,32,384]{2,1,0:T(8,128)(2,1)S(1)}, bf16[8,32,384]{2,1,0:T(8,128)(2,1)S(1)}, u32[]{:S(2)}, u32[]{:S(2)}) collective-permute-start(bf16[8,32,384]{2,1,0:T(8,128)(2,1)S(1)} %get-tuple-element.233), channel_id=1, source_target_pairs={{0,2},{2,0},{4,6},{6,4},{1,3},{3,1},{5,7},{7,5},{8,10},{10,8},{12,... | collective-permute-start | bytes 589832 | tf_op jit(solution)/shard_map/ppermute | solution.py:1011
  501.4 7.3 %collective-permute-start.14 = (f32[4,8,128]{2,1,0:T(8,128)S(1)}, f32[4,8,128]{2,1,0:T(8,128)S(1)}, u32[]{:S(2)}, u32[]{:S(2)}) collective-permute-start(f32[4,8,128]{2,1,0:T(8,128)S(1)} %get-tuple-element.246), channel_id=1, source_target_pairs={{0,24},{8,16},{16,8},{24,0},{1,25},{9,17},{17,9},{25,1},{2,26},{10... | collective-permute-start | bytes 49160 | tf_op jit(solution)/shard_map/ppermute | solution.py:1011
  502.0 6.6 %collective-permute-start.13 = (f32[4,8,128]{2,1,0:T(8,128)S(1)}, f32[4,8,128]{2,1,0:T(8,128)S(1)}, u32[]{:S(2)}, u32[]{:S(2)}) collective-permute-start(f32[4,8,128]{2,1,0:T(8,128)S(1)} %get-tuple-element.247), channel_id=1, source_target_pairs={{0,16},{8,24},{16,0},{24,8},{1,17},{9,25},{17,1},{25,9},{2,18},{10... | collective-permute-start | bytes 49160 | tf_op jit(solution)/shard_map/ppermute | solution.py:1011
  502.4 6.3 %collective-permute-start.12 = (f32[4,8,128]{2,1,0:T(8,128)S(1)}, f32[4,8,128]{2,1,0:T(8,128)S(1)}, u32[]{:S(2)}, u32[]{:S(2)}) collective-permute-start(f32[4,8,128]{2,1,0:T(8,128)S(1)} %get-tuple-element.245), channel_id=1, source_target_pairs={{0,8},{8,0},{16,24},{24,16},{1,9},{9,1},{17,25},{25,17},{2,10},{10... | collective-permute-start | bytes 49160 | tf_op jit(solution)/shard_map/ppermute | solution.py:1011
  505.2 12.8 %all-to-all-start.5 = ((f32[8,32,384]{2,1,0:T(8,128)}), f32[8,32,384]{2,1,0:T(8,128)S(1)}, u32[]{:S(2)}, u32[]{:S(2)}) async-start(f32[8,32,384]{2,1,0:T(8,128)} %fusion.1), calls=%async_computation.7 | async-start | bytes 786432 | tf_op jit(solution)/shard_map/all_to_all | solution.py:1343
  508.7 4.9 collective-permute-start.18
  509.2 7.7 %collective-permute-start.17 = (f32[8,128]{1,0:T(8,128)S(1)}, f32[8,128]{1,0:T(8,128)S(1)}, u32[]{:S(2)}, u32[]{:S(2)}) collective-permute-start(f32[8,128]{1,0:T(8,128)S(1)} %get-tuple-element.251), channel_id=1, source_target_pairs={{0,6},{2,4},{4,2},{6,0},{1,7},{3,5},{5,3},{7,1},{8,14},{10,12},{12... | collective-permute-start | bytes 12296 | tf_op jit(solution)/shard_map/ppermute | solution.py:1011
  509.4 7.8 %collective-permute-start.16 = (f32[8,128]{1,0:T(8,128)S(1)}, f32[8,128]{1,0:T(8,128)S(1)}, u32[]{:S(2)}, u32[]{:S(2)}) collective-permute-start(f32[8,128]{1,0:T(8,128)S(1)} %get-tuple-element.252), channel_id=1, source_target_pairs={{0,4},{2,6},{4,0},{6,2},{1,5},{3,7},{5,1},{7,3},{8,12},{10,14},{12... | collective-permute-start | bytes 12296 | tf_op jit(solution)/shard_map/ppermute | solution.py:1011
  510.8 6.5 %collective-permute-start.15 = (f32[8,128]{1,0:T(8,128)S(1)}, f32[8,128]{1,0:T(8,128)S(1)}, u32[]{:S(2)}, u32[]{:S(2)}) collective-permute-start(f32[8,128]{1,0:T(8,128)S(1)} %get-tuple-element.250), channel_id=1, source_target_pairs={{0,2},{2,0},{4,6},{6,4},{1,3},{3,1},{5,7},{7,5},{8,10},{10,8},{12,... | collective-permute-start | bytes 12296 | tf_op jit(solution)/shard_map/ppermute | solution.py:1011
  521.6 8.8 %collective-permute-start.22 = (bf16[16,2048]{1,0:T(8,128)(2,1)S(1)}, bf16[16,2048]{1,0:T(8,128)(2,1)S(1)}, u32[]{:S(2)}, u32[]{:S(2)}) collective-permute-start(bf16[16,2048]{1,0:T(8,128)(2,1)S(1)} %concatenate.52), channel_id=1, source_target_pairs={{0,2},{2,0},{4,6},{6,4},{1,3},{3,1},{5,7},{7,5},{8,10},{10,8},{12,... | collective-permute-start | bytes 196616 | tf_op jit(solution)/shard_map/ppermute | solution.py:986
  521.7 12.6 %collective-permute-start.23 = (bf16[16,2048]{1,0:T(8,128)(2,1)S(1)}, bf16[16,2048]{1,0:T(8,128)(2,1)S(1)}, u32[]{:S(2)}, u32[]{:S(2)}) collective-permute-start(bf16[16,2048]{1,0:T(8,128)(2,1)S(1)} %concatenate.52), channel_id=1, source_target_pairs={{0,4},{2,6},{4,0},{6,2},{1,5},{3,7},{5,1},{7,3},{8,12},{10,14},{12... | collective-permute-start | bytes 196616 | tf_op jit(solution)/shard_map/ppermute | solution.py:986
  522.5 11.8 %collective-permute-start.24 = (bf16[16,2048]{1,0:T(8,128)(2,1)S(1)}, bf16[16,2048]{1,0:T(8,128)(2,1)S(1)}, u32[]{:S(2)}, u32[]{:S(2)}) collective-permute-start(bf16[16,2048]{1,0:T(8,128)(2,1)S(1)} %concatenate.52), channel_id=1, source_target_pairs={{0,6},{2,4},{4,2},{6,0},{1,7},{3,5},{5,3},{7,1},{8,14},{10,12},{12... | collective-permute-start | bytes 196616 | tf_op jit(solution)/shard_map/ppermute | solution.py:986
  548.5 5.2 collective-permute-start.27
  555.1 6.2 %collective-permute-start.30 = (f32[3,128]{1,0:T(4,128)S(1)}, f32[3,128]{1,0:T(4,128)S(1)}, u32[]{:S(2)}, u32[]{:S(2)}) collective-permute-start(f32[3,128]{1,0:T(4,128)S(1)} %add_add_fusion.1), channel_id=1, source_target_pairs={{0,4},{2,6},{4,0},{6,2},{1,5},{3,7},{5,1},{7,3},{8,12},{10,14},{12... | collective-permute-start | bytes 4616 | tf_op jit(solution)/shard_map/ppermute | solution.py:986
  557.2 5.4 collective-permute-start.31
  (62 other events, 1279.2 us)
Sparse Core Ops, SparseCore 0:
  11.5 96.4 all-gather.4
  111.6 141.8 all-gather.8
  255.4 52.5 all-gather.6
  320.7 149.2 reduce-scatter.2
  494.4 49.8 reduce-scatter.4
